TPU v7x, 32 devices: a whole 2x2x4 slice. The times are simulated.
32 devices in a mesh: band: 8 (over z, core), tp: 4 (over y, x).
Axes of the slice: x: 2, y: 2, z: 4, core: 2. Of those that a mesh axis runs over, the one named last changes fastest.
Arguments:
- tokens: bfloat16 [4, 2048, 2048], P(None, 'band'), may hold values from -6 to 6
- positions: int32 [4, 2048], P(None, 'band'), may hold values from 0 to 2047, as said below
- doc_lengths: int32 [4, 4], replicated, may hold values from 1 to 1024, 2048 in all within a row
- exit_depth: int32 [4, 2048], replicated, may hold values from 1 to 24, as said below
- w_query: bfloat16 [2048, 2048], P('band', 'tp'), may hold values from -0.125 to 0.125
- w_key: bfloat16 [2048, 2048], P('band', 'tp'), may hold values from -0.125 to 0.125
- w_value: bfloat16 [2048, 2048], P('band', 'tp'), may hold values from -0.125 to 0.125
- w_out: bfloat16 [2048, 2048], P('tp', 'band'), may hold values from -1 to 1
- w_up: bfloat16 [2048, 8192], P('band', 'tp'), may hold values from -0.125 to 0.125
- w_down: bfloat16 [8192, 2048], P('tp', 'band'), may hold values from -0.0625 to 0.0625
- b_query: float32 [2048], P('tp'), may hold values from -3 to 3
- b_value: float32 [2048], P('tp'), may hold values from -3 to 3
- b_out: float32 [2048], replicated, may hold values from -3 to 3
- b_up: float32 [8192], P('tp'), may hold values from -3 to 3
- b_down: float32 [2048], replicated, may hold values from -3 to 3
- attn_gain: float32 [2048], replicated, may hold values from 0.1 to 1.9
- attn_bias: float32 [2048], replicated, may hold values from -2 to 2
- ffn_gain: float32 [2048], replicated, may hold values from 0.1 to 1.9
- ffn_bias: float32 [2048], replicated, may hold values from -2 to 2
- cotangent: bfloat16 [4, 2048, 2048], P(None, 'band'), may hold values from -6 to 6
Outputs:
- output: bfloat16 [4, 2048, 2048], P(None, 'band')
- token_grad: float32 [4, 2048, 2048], P(None, 'band')
- grad_w_query: float32 [2048, 2048], P('band', 'tp')
- grad_w_key: float32 [2048, 2048], P('band', 'tp')
- grad_w_value: float32 [2048, 2048], P('band', 'tp')
- grad_w_out: float32 [2048, 2048], P('tp', 'band')
- grad_w_up: float32 [2048, 8192], P('band', 'tp')
- grad_w_down: float32 [8192, 2048], P('tp', 'band')
- grad_b_query: float32 [2048], P('tp')
- grad_b_value: float32 [2048], P('tp')
- grad_b_out: float32 [2048], replicated
- grad_b_up: float32 [8192], P('tp')
- grad_b_down: float32 [2048], replicated
- grad_attn_gain: float32 [2048], replicated
- grad_attn_bias: float32 [2048], replicated
- grad_ffn_gain: float32 [2048], replicated
- grad_ffn_bias: float32 [2048], replicated
Inputs may be any that keep to these rules, and one draw needn't show every extreme that they name: `positions`: each sequence's row holds every position 0 to 2047 once. `doc_lengths`: each row sums to 2048, and its largest entry is 1024. `exit_depth`: along a row (by position) the depths never rise, and position 0 has 24.
All inputs are finite; a program needn't handle non-finite values.
Results may differ from a plain program's by a relative error of at most 0.02.
Values may be sent and summed in bfloat16 or wider, within the bound.
A program may use at most 256 MiB of HBM per device.

v0:
```python
import jax
import jax.numpy as jnp
from jax import lax
from jax.sharding import PartitionSpec as P

HEAD_DIM = 64
LAYER = 12


epsilon = 1e-05
masked_score = -1e30


def shifted(array, axis, by):
    count = lax.axis_size(axis)
    return lax.ppermute(array, axis, [(i, (i + by) % count) for i in range(count)])


def layer_norm(values, gain, shift):
    center = values - jnp.mean(values, axis=-1, keepdims=True)
    inverse = lax.rsqrt(jnp.mean(center * center, axis=-1, keepdims=True) + epsilon)
    normed = center * inverse
    return (normed * gain + shift, normed, inverse)


def norm_back(grad_out, normed, inverse, gain):
    scaled = grad_out * gain
    return inverse * (
        scaled
        - jnp.mean(scaled, axis=-1, keepdims=True)
        - normed * jnp.mean(scaled * normed, axis=-1, keepdims=True)
    )


def matmul(left, right):
    return jnp.dot(left, right, preferred_element_type=jnp.float32)


def left_grad(left, right):
    return jnp.einsum("na,nb->ab", left, right, preferred_element_type=jnp.float32)


def right_back(left, right):
    return jnp.einsum("nb,ab->na", left, right, preferred_element_type=jnp.float32)


def gelu_exact(values):
    return jax.nn.gelu(values, approximate=False)


def body(
    tokens,
    positions,
    doc_lengths,
    exit_depth,
    w_query,
    w_key,
    w_value,
    w_out,
    w_up,
    w_down,
    b_query,
    b_value,
    b_out,
    b_up,
    b_down,
    attn_gain,
    attn_bias,
    ffn_gain,
    ffn_bias,
    cotangent,
):
    seq_count, local_rows, width = tokens.shape
    inner = b_query.shape[0]
    head_count = inner // HEAD_DIM
    factor = HEAD_DIM ** (-0.5)
    band_size = lax.axis_size("band")
    band_index = lax.axis_index("band")
    rows_all = seq_count * local_rows
    gathered = (
        lax.all_gather(w_query, "band", axis=0, tiled=True),
        lax.all_gather(w_key, "band", axis=0, tiled=True),
        lax.all_gather(w_value, "band", axis=0, tiled=True),
        lax.all_gather(w_up, "band", axis=0, tiled=True),
        lax.all_gather(w_out, "band", axis=1, tiled=True),
        lax.all_gather(w_down, "band", axis=1, tiled=True),
    )
    full_query, full_key, full_value, full_up, full_out, full_down = gathered
    all_pos = lax.all_gather(positions, "band", axis=1, tiled=True)
    ends = jnp.cumsum(doc_lengths, axis=1)
    all_doc = jnp.sum((all_pos[:, :, None] >= ends[:, None, :]).astype(jnp.int32), axis=2)
    all_live = jnp.take_along_axis(exit_depth, all_pos, axis=1) > LAYER
    offset = band_index * local_rows
    query_doc = lax.dynamic_slice_in_dim(all_doc, offset, local_rows, 1)
    query_live = lax.dynamic_slice_in_dim(all_live, offset, local_rows, 1)

    def permit(start, count):
        key_pos = lax.dynamic_slice_in_dim(all_pos, start, count, 1)
        key_doc = lax.dynamic_slice_in_dim(all_doc, start, count, 1)
        key_live = lax.dynamic_slice_in_dim(all_live, start, count, 1)
        same_doc = query_doc[:, :, None] == key_doc[:, None, :]
        earlier = key_pos[:, None, :] <= positions[:, :, None]
        usable = key_live[:, None, :] | (key_pos[:, None, :] == positions[:, :, None])
        return (same_doc & earlier & usable)[:, None]

    inputs = tokens.reshape(rows_all, width).astype(jnp.float32)
    normed_in, unit_in, inverse_in = layer_norm(inputs, attn_gain, attn_bias)
    normed_low = normed_in.astype(jnp.bfloat16)
    query_low = (matmul(normed_low, full_query) + b_query).astype(jnp.bfloat16)
    key_low = matmul(normed_low, full_key).astype(jnp.bfloat16)
    value_low = (matmul(normed_low, full_value) + b_value).astype(jnp.bfloat16)
    query_heads = query_low.reshape(seq_count, local_rows, head_count, HEAD_DIM)
    key_seq = key_low.reshape(seq_count, local_rows, inner)
    value_seq = value_low.reshape(seq_count, local_rows, inner)
    start_top = jnp.full((seq_count, head_count, local_rows), masked_score, jnp.float32)
    piece = (
        lax.all_gather(key_seq, "band", axis=1, tiled=True),
        lax.all_gather(value_seq, "band", axis=1, tiled=True),
    )
    top_score = start_top
    count = piece[0].shape[1]
    key_heads = piece[0].reshape(seq_count, count, head_count, HEAD_DIM)
    value_heads = piece[1].reshape(seq_count, count, head_count, HEAD_DIM)
    allowed = permit(jnp.int32(0), count)
    scores = (
        jnp.einsum("sqhd,skhd->shqk", query_heads, key_heads, preferred_element_type=jnp.float32)
        * factor
    )
    scores = jnp.where(allowed, scores, masked_score)
    new_top = jnp.maximum(top_score, jnp.max(scores, axis=3))
    weights_now = jnp.where(allowed, jnp.exp(scores - new_top[..., None]), 0.0)
    total = jnp.sum(weights_now, axis=3)
    summed = jnp.einsum(
        "shqk,skhd->shqd",
        weights_now.astype(jnp.bfloat16),
        value_heads,
        preferred_element_type=jnp.float32,
    )
    top_score, total, summed = (new_top, total, summed)
    log_total = top_score + jnp.log(total)
    mixed = summed / total[..., None]
    mixed_rows = mixed.transpose(0, 2, 1, 3).reshape(rows_all, inner)
    mixed_low = mixed_rows.astype(jnp.bfloat16)
    attn_out = (
        lax.psum(matmul(mixed_low, full_out).astype(jnp.bfloat16), "tp").astype(jnp.float32) + b_out
    )
    residual = inputs + attn_out
    normed_mid, unit_mid, inverse_mid = layer_norm(residual, ffn_gain, ffn_bias)
    mid_low = normed_mid.astype(jnp.bfloat16)
    pre_act = matmul(mid_low, full_up) + b_up
    act_low = gelu_exact(pre_act).astype(jnp.bfloat16)
    ffn_out = (
        lax.psum(matmul(act_low, full_down).astype(jnp.bfloat16), "tp").astype(jnp.float32) + b_down
    )
    live_rows = query_live.reshape(rows_all, 1).astype(jnp.float32)
    output = (inputs + live_rows * (attn_out + ffn_out)).astype(jnp.bfloat16).reshape(tokens.shape)
    again = (
        lax.all_gather(w_query, "band", axis=0, tiled=True),
        lax.all_gather(w_key, "band", axis=0, tiled=True),
        lax.all_gather(w_value, "band", axis=0, tiled=True),
        lax.all_gather(w_up, "band", axis=0, tiled=True),
        lax.all_gather(w_out, "band", axis=1, tiled=True),
        lax.all_gather(w_down, "band", axis=1, tiled=True),
    )
    back_query, back_key, back_value, back_up, back_out, back_down = again
    grad_rows = cotangent.reshape(rows_all, width).astype(jnp.float32)
    down_grad = (live_rows * grad_rows).astype(jnp.bfloat16)
    grad_w_down = left_grad(act_low, down_grad)
    grad_b_down = jnp.sum(down_grad.astype(jnp.float32), axis=0)
    act_grad = right_back(down_grad, back_down)
    unused, gelu_pull = jax.vjp(gelu_exact, pre_act)
    up_grad = gelu_pull(act_grad)[0].astype(jnp.bfloat16)
    grad_w_up = left_grad(mid_low, up_grad)
    grad_b_up = jnp.sum(up_grad.astype(jnp.float32), axis=0)
    mid_grad = lax.psum(right_back(up_grad, back_up).astype(jnp.bfloat16), "tp").astype(jnp.float32)
    grad_ffn_gain = jnp.sum(mid_grad * unit_mid, axis=0)
    grad_ffn_bias = jnp.sum(mid_grad, axis=0)
    resid_grad = norm_back(mid_grad, unit_mid, inverse_mid, ffn_gain)
    attn_grad = (live_rows * grad_rows + resid_grad).astype(jnp.bfloat16)
    grad_w_out = left_grad(mixed_low, attn_grad)
    grad_b_out = jnp.sum(attn_grad.astype(jnp.float32), axis=0)
    mixed_grad = right_back(attn_grad, back_out).astype(jnp.bfloat16)
    grad_heads = mixed_grad.reshape(seq_count, local_rows, head_count, HEAD_DIM)
    delta = jnp.einsum("sqhd,shqd->shq", grad_heads.astype(jnp.float32), mixed)

    def turn(step, carry):
        key_now, value_now, key_acc, value_acc, query_acc = carry
        owner = (band_index - step) % band_size
        allowed = permit(owner * local_rows, local_rows)
        key_heads = key_now.reshape(seq_count, local_rows, head_count, HEAD_DIM)
        value_heads = value_now.reshape(seq_count, local_rows, head_count, HEAD_DIM)
        scores = (
            jnp.einsum(
                "sqhd,skhd->shqk", query_heads, key_heads, preferred_element_type=jnp.float32
            )
            * factor
        )
        probs = jnp.where(allowed, jnp.exp(scores - log_total[..., None]), 0.0)
        probs_low = probs.astype(jnp.bfloat16)
        value_acc = value_acc + jnp.einsum(
            "shqk,sqhd->skhd", probs_low, grad_heads, preferred_element_type=jnp.float32
        ).reshape(seq_count, local_rows, inner)
        prob_grad = jnp.einsum(
            "sqhd,skhd->shqk", grad_heads, value_heads, preferred_element_type=jnp.float32
        )
        score_grad = (probs * (prob_grad - delta[..., None])).astype(jnp.bfloat16)
        query_acc = query_acc + factor * jnp.einsum(
            "shqk,skhd->sqhd", score_grad, key_heads, preferred_element_type=jnp.float32
        )
        key_acc = key_acc + factor * jnp.einsum(
            "shqk,sqhd->skhd", score_grad, query_heads, preferred_element_type=jnp.float32
        ).reshape(seq_count, local_rows, inner)
        key_now, value_now = shifted((key_now, value_now), "band", 1)
        key_acc, value_acc = (
            shifted(key_acc.astype(jnp.bfloat16), "band", 1).astype(key_acc.dtype),
            shifted(value_acc.astype(jnp.bfloat16), "band", 1).astype(value_acc.dtype),
        )
        return (key_now, value_now, key_acc, value_acc, query_acc)

    empty_grad = jnp.zeros((seq_count, local_rows, inner), jnp.float32)
    empty_query = jnp.zeros((seq_count, local_rows, head_count, HEAD_DIM), jnp.float32)
    final = lax.fori_loop(
        0, band_size, turn, (key_seq, value_seq, empty_grad, empty_grad, empty_query)
    )
    query_grad = final[4].reshape(rows_all, inner).astype(jnp.bfloat16)
    key_grad = final[2].reshape(rows_all, inner).astype(jnp.bfloat16)
    value_grad = final[3].reshape(rows_all, inner).astype(jnp.bfloat16)
    grad_w_query = left_grad(normed_low, query_grad)
    grad_w_key = left_grad(normed_low, key_grad)
    grad_w_value = left_grad(normed_low, value_grad)
    grad_b_query = jnp.sum(query_grad.astype(jnp.float32), axis=0)
    grad_b_value = jnp.sum(value_grad.astype(jnp.float32), axis=0)
    input_grad = lax.psum(
        (
            right_back(query_grad, back_query)
            + right_back(key_grad, back_key)
            + right_back(value_grad, back_value)
        ).astype(jnp.bfloat16),
        "tp",
    ).astype(jnp.float32)
    grad_attn_gain = jnp.sum(input_grad * unit_in, axis=0)
    grad_attn_bias = jnp.sum(input_grad, axis=0)
    token_grad = grad_rows + resid_grad + norm_back(input_grad, unit_in, inverse_in, attn_gain)
    summed_big = (
        lax.psum_scatter(
            grad_w_query.astype(jnp.bfloat16), "band", scatter_dimension=0, tiled=True
        ).astype(jnp.float32),
        lax.psum_scatter(
            grad_w_key.astype(jnp.bfloat16), "band", scatter_dimension=0, tiled=True
        ).astype(jnp.float32),
        lax.psum_scatter(
            grad_w_value.astype(jnp.bfloat16), "band", scatter_dimension=0, tiled=True
        ).astype(jnp.float32),
        lax.psum_scatter(
            grad_w_up.astype(jnp.bfloat16), "band", scatter_dimension=0, tiled=True
        ).astype(jnp.float32),
        lax.psum_scatter(
            grad_w_out.astype(jnp.bfloat16), "band", scatter_dimension=1, tiled=True
        ).astype(jnp.float32),
        lax.psum_scatter(
            grad_w_down.astype(jnp.bfloat16), "band", scatter_dimension=1, tiled=True
        ).astype(jnp.float32),
    )
    summed_small = (
        lax.psum(grad_b_query.astype(jnp.bfloat16), "band").astype(jnp.float32),
        lax.psum(grad_b_value.astype(jnp.bfloat16), "band").astype(jnp.float32),
        lax.psum(grad_b_out.astype(jnp.bfloat16), "band").astype(jnp.float32),
        lax.psum(grad_b_up.astype(jnp.bfloat16), "band").astype(jnp.float32),
        lax.psum(grad_b_down.astype(jnp.bfloat16), "band").astype(jnp.float32),
        lax.psum(grad_attn_gain.astype(jnp.bfloat16), "band").astype(jnp.float32),
        lax.psum(grad_attn_bias.astype(jnp.bfloat16), "band").astype(jnp.float32),
        lax.psum(grad_ffn_gain.astype(jnp.bfloat16), "band").astype(jnp.float32),
        lax.psum(grad_ffn_bias.astype(jnp.bfloat16), "band").astype(jnp.float32),
    )
    return (
        output,
        token_grad.reshape(tokens.shape),
        summed_big[0],
        summed_big[1],
        summed_big[2],
        summed_big[4],
        summed_big[3],
        summed_big[5],
        summed_small[0],
        summed_small[1],
        summed_small[2],
        summed_small[3],
        summed_small[4],
        summed_small[5],
        summed_small[6],
        summed_small[7],
        summed_small[8],
    )


def solution(mesh):
    return jax.shard_map(
        body,
        mesh=mesh,
        in_specs=(
            P(None, "band", None),
            P(None, "band"),
            P(),
            P(),
            P("band", "tp"),
            P("band", "tp"),
            P("band", "tp"),
            P("tp", "band"),
            P("band", "tp"),
            P("tp", "band"),
            P("tp"),
            P("tp"),
            P(),
            P("tp"),
            P(),
            P(),
            P(),
            P(),
            P(),
            P(None, "band", None),
        ),
        out_specs=(
            P(None, "band", None),
            P(None, "band", None),
            P("band", "tp"),
            P("band", "tp"),
            P("band", "tp"),
            P("tp", "band"),
            P("band", "tp"),
            P("tp", "band"),
            P("tp"),
            P("tp"),
            P(),
            P("tp"),
            P(),
            P(),
            P(),
            P(),
            P(),
        ),
        check_vma=False,
    )
```

profile of v0, /device:TPU:9, one launch (start us, length us, event | category | flops | bytes accessed | tf_op | source)
XLA Modules:
  0.0 1752.9 jit_solution(17117254135857179327)
XLA Ops:
  20.3 20.1 %all-gather.11.cloned.1.call-done = bf16[2048,512]{1,0:T(8,128)(2,1)} async-done(((bf16[256,512]{1,0:T(8,128)(2,1)}), bf16[2048,512]{1,0:T(8,128)(2,1)}) %all-gather.11.cloned.1.call-update) | async-done | bytes 2097168 | tf_op jit(solution)/shard_map/all_gather | solution.py:82
  46.7 23.9 %all-gather.15.cloned.1.call-done = bf16[2048,512]{1,0:T(8,128)(2,1)} async-done(((bf16[256,512]{1,0:T(8,128)(2,1)}), bf16[2048,512]{1,0:T(8,128)(2,1)}) %all-gather.15.cloned.1.call-update) | async-done | bytes 2097168 | tf_op jit(solution)/shard_map/all_gather | solution.py:83
  77.4 13.0 all_gather.33
  90.9 69.3 %gather_fusion = s32[8192]{0:T(1024)S(1)} fusion(s32[4,2048]{1,0:T(4,128)S(1)} %copy-done, s32[8192]{0:T(1024)S(1)} %bitcast.188), kind=kCustom, calls=%fused_computation | custom fusion | bytes 131072 | tf_op jit(solution)/shard_map/jit(take_along_axis)/gather | solution.py:92
  181.4 11.4 copy.64
  192.8 28.7 %fusion.11 = (f32[4,8,256]{2,1,0:T(8,128)S(1)}, f32[4,8,256,2048]{3,2,1,0:T(8,128)}) fusion(pred[4,256,2048]{2,1,0:T(8,128)(4,1)S(1)} %or_and_fusion.1, bf16[4,256,8,64]{1,3,2,0:T(8,128)(2,1)S(1)} %copy.65, bf16[4,2048,8,64]{1,3,2,0:T(8,128)(2,1)} %bitcast.191), kind=kOutput, calls=%fused_computation.23 | convolution fusion | flops 2197807104 | bytes 78675968 | tf_op jit(solution)/shard_map/sqhd,skhd->shqk/dot_general | solution.py:126
  222.1 22.5 %fusion.12 = f32[4,8,256]{2,1,0:T(8,128)S(1)} fusion(f32[4,8,256,2048]{3,2,1,0:T(8,128)} %get-tuple-element.564, f32[4,8,256]{2,1,0:T(8,128)S(1)} %broadcast_maximum_fusion, pred[4,256,2048]{2,1,0:T(8,128)(4,1)S(1)} %or_and_fusion.1), kind=kLoop, calls=%fused_computation.24 | loop fusion | flops 83877888 | bytes 69271552 | tf_op jit(solution)/shard_map/reduce_sum | solution.py:132
  244.6 18.9 %all-gather.17.cloned.1.call-done = bf16[4,2048,512]{2,1,0:T(8,128)(2,1)} async-done(((bf16[4,256,512]{2,1,0:T(8,128)(2,1)}), bf16[4,2048,512]{2,1,0:T(8,128)(2,1)}) %all-gather.17.cloned.1.call-update) | async-done | bytes 8388624 | tf_op jit(solution)/shard_map/all_gather | solution.py:118
  263.5 11.3 copy.66
  274.8 29.7 %fusion.56 = (bf16[4,256,8,64]{1,3,2,0:T(8,128)(2,1)S(1)}, f32[4,8,256,64]{2,3,1,0:T(8,128)}) fusion(f32[4,256,8]{1,2,0:T(8,128)S(1)} %bitcast.209, bf16[4,2048,8,64]{1,3,2,0:T(8,128)(2,1)} %bitcast.194, f32[4,8,256,2048]{3,2,1,0:T(8,128)} %get-tuple-element.564, f32[4,8,256]{2,1,0:T(8,128)S(1)} %broadcast_maximum_fusion, ...), kind=kOutput, calls=%fused_computation.106 | convolution fusion | flops 2232418304 | bytes 80805888 | tf_op jit(solution)/shard_map/shqk,skhd->shqd/dot_general | solution.py:133
  319.0 97.8 %all-reduce.6.cloned.1.call-done = bf16[1024,2048]{1,0:T(8,128)(2,1)} async-done(((bf16[1024,2048]{1,0:T(8,128)(2,1)}), bf16[1024,2048]{1,0:T(8,128)(2,1)}) %all-reduce.6.cloned.1.call-update) | async-done | bytes 4194320 | tf_op jit(solution)/shard_map/psum | solution.py:145
  429.9 68.4 %all-gather.21.cloned.1.call-done = bf16[2048,2048]{1,0:T(8,128)(2,1)} async-done(((bf16[256,2048]{1,0:T(8,128)(2,1)}), bf16[2048,2048]{1,0:T(8,128)(2,1)}) %all-gather.21.cloned.1.call-update) | async-done | bytes 8388624 | tf_op jit(solution)/shard_map/all_gather | solution.py:84
  498.3 15.6 fusion.57
  514.0 66.8 %all-gather.23.cloned.1.call-done = bf16[2048,2048]{1,0:T(8,128)(2,1)} async-done(((bf16[2048,256]{1,0:T(8,128)(2,1)}), bf16[2048,2048]{1,0:T(8,128)(2,1)}) %all-gather.23.cloned.1.call-update) | async-done | bytes 8388624 | tf_op jit(solution)/shard_map/all_gather | solution.py:86
  580.8 33.9 %fusion.65 = (bf16[2048]{0:T(1024)(128)(2,1)}, bf16[1024,2048]{1,0:T(8,128)(2,1)S(1)}, f32[1024,2048]{1,0:T(8,128)}) fusion(f32[1024,2048]{1,0:T(8,128)} %fusion.57, f32[2048]{0:T(1024)S(1)} %copy-done.71, bf16[1024,2048]{1,0:T(8,128)(2,1)} %fusion.34, bf16[2048,2048]{1,0:T(8,128)(2,1)} %all-gather.23.cloned.1.call-done), kind=kOutput, calls=%fused_computation.137 | convolution fusion | flops 8745121792 | bytes 33566720 | tf_op jit(solution)/shard_map/nb,ab->na/dot_general | solution.py:44
  634.2 97.8 %all-reduce.8.cloned.1.call-done = bf16[1024,2048]{1,0:T(8,128)(2,1)} async-done(((bf16[1024,2048]{1,0:T(8,128)(2,1)}), bf16[1024,2048]{1,0:T(8,128)(2,1)}) %all-reduce.8.cloned.1.call-update) | async-done | bytes 4194320 | tf_op jit(solution)/shard_map/psum | solution.py:175
  769.4 483.4 %while.24 = (s32[]{:T(128)}, bf16[4,256,512]{1,2,0:T(8,128)(2,1)S(1)}, bf16[4,256,512]{1,2,0:T(8,128)(2,1)}, f32[4,256,512]{1,2,0:T(8,128)}, f32[4,256,512]{1,2,...) while((s32[]{:T(128)}, ...), condition=%wide.region_14.15_spmd.clone, body=%wide.region_13.14_spmd.clone.sunk | while | flops 1371013120 | bytes 134090400 | solution.py:222
  792.6 13.2 collective-permute-done.2
  828.2 11.3 collective-permute-done.1
  887.2 11.3 collective-permute-done.1
  946.2 11.3 collective-permute-done.1
  1005.3 11.3 collective-permute-done.1
  1064.3 11.3 collective-permute-done.1
  1286.7 14.3 convolution_convert_fusion.3
  1318.0 15.1 convolution_convert_fusion.1
  1333.2 14.1 convolution_convert_fusion
  1356.9 24.6 %reduce-scatter.11.cloned.1.call-done = bf16[256,512]{1,0:T(8,128)(2,1)} async-done(((bf16[2048,512]{1,0:T(8,128)(2,1)}), bf16[256,512]{1,0:T(8,128)(2,1)}) %reduce-scatter.11.cloned.1.call-update) | async-done | bytes 262160 | tf_op jit(solution)/shard_map/reduce_scatter | solution.py:251
  1383.2 178.0 %all-reduce.10.cloned.1.call-done = (bf16[1024,2048]{1,0:T(8,128)(2,1)}, bf16[1024,2048]{1,0:T(8,128)(2,1)}) async-done(((bf16[1024,2048]{1,0:T(8,128)(2,1)}, bf16[1024,2048]{1,0:T(8,128)(2,1)}), (bf16[1024,2048]{1,0:T(8,128)(2,1)}, bf16[1024,2048]{1,0:T(8,128)(2,1)})) %all-reduce.10.cloned.1.call-update) | async-done | bytes 8388624 | tf_op jit(solution)/shard_map/psum | solution.py:153
  1570.1 22.9 %all-reduce = (bf16[512]{0:T(512)(128)(2,1)S(1)}, bf16[512]{0:T(512)(128)(2,1)S(1)}, bf16[2048]{0:T(1024)(128)(2,1)S(1)}, bf16[2048]{0:T(1024)(128)(2,1)S(1)}, b...) all-reduce(bf16[512]{0:T(512)(128)(2,1)S(1)} %reduce_sum.205, ...), channel_id=1, replica_groups=mesh['band'=8,'tp'=4] {'band'}, use_global_device_ids=true, to_apply=%region_25.26 | all-reduce | flops 15360 | bytes 61440 | tf_op jit(solution)/shard_map/psum | solution.py:265
  1598.5 17.1 fusion.29
  1615.6 37.3 %reduce-scatter.15.cloned.1.call-done = bf16[256,2048]{1,0:T(8,128)(2,1)} async-done(((bf16[2048,2048]{1,0:T(8,128)(2,1)}), bf16[256,2048]{1,0:T(8,128)(2,1)}) %reduce-scatter.15.cloned.1.call-update) | async-done | bytes 1048592 | tf_op jit(solution)/shard_map/reduce_scatter | solution.py:254
  1655.7 87.4 %reduce-scatter.17.cloned.1.call-done = bf16[2048,256]{1,0:T(8,128)(2,1)} async-done(((bf16[2048,2048]{1,0:T(8,128)(2,1)}), bf16[2048,256]{1,0:T(8,128)(2,1)}) %reduce-scatter.17.cloned.1.call-update) | async-done | bytes 1048592 | tf_op jit(solution)/shard_map/reduce_scatter | solution.py:260
  (535 shorter events, 626.3 us)
Async XLA Ops:
  7.2 33.1 %all-gather.11.cloned.1.call-start = ((), (), s32[]{:S(2)}) async-start(), calls=%async_computation.7 | async-start | bytes 2359296 | tf_op jit(solution)/shard_map/all_gather | solution.py:82
  8.0 62.6 %all-gather.15.cloned.1.call-start = ((), (), s32[]{:S(2)}) async-start(), calls=%async_computation.9 | async-start | bytes 2359296 | tf_op jit(solution)/shard_map/all_gather | solution.py:83
  8.7 154.5 %all-gather.9.cloned.1.call-start = ((), (), s32[]{:S(2)}) async-start(), calls=%async_computation.6 | async-start | bytes 2359296 | tf_op jit(solution)/shard_map/all_gather | solution.py:81
  9.4 171.9 %all-gather.13.cloned.1.call-start = ((), (), s32[]{:S(2)}) async-start(), calls=%async_computation.8 | async-start | bytes 9437184 | tf_op jit(solution)/shard_map/all_gather | solution.py:117
  46.6 216.9 %all-gather.17.cloned.1.call-start = ((), (), s32[]{:S(2)}) async-start(), calls=%async_computation.10 | async-start | bytes 9437184 | tf_op jit(solution)/shard_map/all_gather | solution.py:118
  76.8 228.8 %all-gather.19.cloned.1.call-start = ((), (), s32[]{:S(2)}) async-start(), calls=%async_computation.11 | async-start | bytes 2359296 | tf_op jit(solution)/shard_map/all_gather | solution.py:85
  77.4 339.4 %all-reduce.6.cloned.1.call-start = ((), (), s32[]{:S(2)}) async-start(), calls=%async_computation.12 | async-start | bytes 8388608 | tf_op jit(solution)/shard_map/psum | solution.py:145
  311.9 186.4 %all-gather.21.cloned.1.call-start = ((), (), s32[]{:S(2)}) async-start(), calls=%async_computation.13 | async-start | bytes 9437184 | tf_op jit(solution)/shard_map/all_gather | solution.py:84
  312.7 268.1 %all-gather.23.cloned.1.call-start = ((), (), s32[]{:S(2)}) async-start(), calls=%async_computation.14 | async-start | bytes 9437184 | tf_op jit(solution)/shard_map/all_gather | solution.py:86
  313.4 418.5 %all-reduce.8.cloned.1.call-start = ((), (), s32[]{:S(2)}) async-start(), calls=%async_computation.15 | async-start | bytes 8388608 | tf_op jit(solution)/shard_map/psum | solution.py:175
  627.2 724.3 %reduce-scatter.13.cloned.1.call-start = ((), (), s32[]{:S(2)}) async-start(), calls=%async_computation.19 | async-start | bytes 2359296 | tf_op jit(solution)/shard_map/reduce_scatter | solution.py:257
  766.4 586.8 %reduce-scatter.7.cloned.1.call-start = ((), (), s32[]{:S(2)}) async-start(), calls=%async_computation.16 | async-start | bytes 2359296 | tf_op jit(solution)/shard_map/reduce_scatter | solution.py:245
  786.1 31.0 %collective-permute-start.3 = (bf16[4,256,512]{1,2,0:T(8,128)(2,1)}, bf16[4,256,512]{1,2,0:T(8,128)(2,1)}, u32[]{:S(2)}, u32[]{:S(2)}) collective-permute-start(bf16[4,256,512]{1,2,0:T(8,128)(2,1)} %fusion.146), channel_id=1, source_target_pairs={{0,4},{4,8},{8,12},{12,16},{16,20},{20,24},{24,28},{28,0},{1,5},{5... | collective-permute-start | bytes 3145736 | tf_op jit(solution)/shard_map/while/body/eval_jaxpr/ppermute | solution.py:16
  786.1 42.1 %collective-permute-start = (bf16[4,256,512]{1,2,0:T(8,128)(2,1)S(1)}, bf16[4,256,512]{1,2,0:T(8,128)(2,1)S(1)}, u32[]{:S(2)}, u32[]{:S(2)}) collective-permute-start(bf16[4,256,512]{1,2,0:T(8,128)(2,1)S(1)} %copy.104), channel_id=1, source_target_pairs={{0,4},{4,8},{8,12},{12,16},{16,20},{20,24},{24,28},{28,0},{1,5},{5... | collective-permute-start | bytes 3145736 | tf_op jit(solution)/shard_map/while/body/eval_jaxpr/ppermute | solution.py:16
  787.7 51.8 %collective-permute-start.1 = (bf16[4,256,512]{1,2,0:T(8,128)(2,1)}, bf16[4,256,512]{1,2,0:T(8,128)(2,1)}, u32[]{:S(2)}, u32[]{:S(2)}) collective-permute-start(bf16[4,256,512]{1,2,0:T(8,128)(2,1)} %copy-done.15), channel_id=1, source_target_pairs={{0,4},{4,8},{8,12},{12,16},{16,20},{20,24},{24,28},{28,0},{1,5},{5... | collective-permute-start | bytes 3145736 | tf_op jit(solution)/shard_map/while/body/eval_jaxpr/ppermute | solution.py:16
  856.4 30.8 %collective-permute-start = (bf16[4,256,512]{1,2,0:T(8,128)(2,1)S(1)}, bf16[4,256,512]{1,2,0:T(8,128)(2,1)S(1)}, u32[]{:S(2)}, u32[]{:S(2)}) collective-permute-start(bf16[4,256,512]{1,2,0:T(8,128)(2,1)S(1)} %copy.104), channel_id=1, source_target_pairs={{0,4},{4,8},{8,12},{12,16},{16,20},{20,24},{24,28},{28,0},{1,5},{5... | collective-permute-start | bytes 3145736 | tf_op jit(solution)/shard_map/while/body/eval_jaxpr/ppermute | solution.py:16
  857.9 40.6 %collective-permute-start.1 = (bf16[4,256,512]{1,2,0:T(8,128)(2,1)}, bf16[4,256,512]{1,2,0:T(8,128)(2,1)}, u32[]{:S(2)}, u32[]{:S(2)}) collective-permute-start(bf16[4,256,512]{1,2,0:T(8,128)(2,1)} %copy-done.15), channel_id=1, source_target_pairs={{0,4},{4,8},{8,12},{12,16},{16,20},{20,24},{24,28},{28,0},{1,5},{5... | collective-permute-start | bytes 3145736 | tf_op jit(solution)/shard_map/while/body/eval_jaxpr/ppermute | solution.py:16
  915.5 30.8 %collective-permute-start = (bf16[4,256,512]{1,2,0:T(8,128)(2,1)S(1)}, bf16[4,256,512]{1,2,0:T(8,128)(2,1)S(1)}, u32[]{:S(2)}, u32[]{:S(2)}) collective-permute-start(bf16[4,256,512]{1,2,0:T(8,128)(2,1)S(1)} %copy.104), channel_id=1, source_target_pairs={{0,4},{4,8},{8,12},{12,16},{16,20},{20,24},{24,28},{28,0},{1,5},{5... | collective-permute-start | bytes 3145736 | tf_op jit(solution)/shard_map/while/body/eval_jaxpr/ppermute | solution.py:16
  917.0 40.6 %collective-permute-start.1 = (bf16[4,256,512]{1,2,0:T(8,128)(2,1)}, bf16[4,256,512]{1,2,0:T(8,128)(2,1)}, u32[]{:S(2)}, u32[]{:S(2)}) collective-permute-start(bf16[4,256,512]{1,2,0:T(8,128)(2,1)} %copy-done.15), channel_id=1, source_target_pairs={{0,4},{4,8},{8,12},{12,16},{16,20},{20,24},{24,28},{28,0},{1,5},{5... | collective-permute-start | bytes 3145736 | tf_op jit(solution)/shard_map/while/body/eval_jaxpr/ppermute | solution.py:16
  974.5 30.8 %collective-permute-start = (bf16[4,256,512]{1,2,0:T(8,128)(2,1)S(1)}, bf16[4,256,512]{1,2,0:T(8,128)(2,1)S(1)}, u32[]{:S(2)}, u32[]{:S(2)}) collective-permute-start(bf16[4,256,512]{1,2,0:T(8,128)(2,1)S(1)} %copy.104), channel_id=1, source_target_pairs={{0,4},{4,8},{8,12},{12,16},{16,20},{20,24},{24,28},{28,0},{1,5},{5... | collective-permute-start | bytes 3145736 | tf_op jit(solution)/shard_map/while/body/eval_jaxpr/ppermute | solution.py:16
  976.0 40.6 %collective-permute-start.1 = (bf16[4,256,512]{1,2,0:T(8,128)(2,1)}, bf16[4,256,512]{1,2,0:T(8,128)(2,1)}, u32[]{:S(2)}, u32[]{:S(2)}) collective-permute-start(bf16[4,256,512]{1,2,0:T(8,128)(2,1)} %copy-done.15), channel_id=1, source_target_pairs={{0,4},{4,8},{8,12},{12,16},{16,20},{20,24},{24,28},{28,0},{1,5},{5... | collective-permute-start | bytes 3145736 | tf_op jit(solution)/shard_map/while/body/eval_jaxpr/ppermute | solution.py:16
  1033.6 30.8 %collective-permute-start = (bf16[4,256,512]{1,2,0:T(8,128)(2,1)S(1)}, bf16[4,256,512]{1,2,0:T(8,128)(2,1)S(1)}, u32[]{:S(2)}, u32[]{:S(2)}) collective-permute-start(bf16[4,256,512]{1,2,0:T(8,128)(2,1)S(1)} %copy.104), channel_id=1, source_target_pairs={{0,4},{4,8},{8,12},{12,16},{16,20},{20,24},{24,28},{28,0},{1,5},{5... | collective-permute-start | bytes 3145736 | tf_op jit(solution)/shard_map/while/body/eval_jaxpr/ppermute | solution.py:16
  1035.1 40.6 %collective-permute-start.1 = (bf16[4,256,512]{1,2,0:T(8,128)(2,1)}, bf16[4,256,512]{1,2,0:T(8,128)(2,1)}, u32[]{:S(2)}, u32[]{:S(2)}) collective-permute-start(bf16[4,256,512]{1,2,0:T(8,128)(2,1)} %copy-done.15), channel_id=1, source_target_pairs={{0,4},{4,8},{8,12},{12,16},{16,20},{20,24},{24,28},{28,0},{1,5},{5... | collective-permute-start | bytes 3145736 | tf_op jit(solution)/shard_map/while/body/eval_jaxpr/ppermute | solution.py:16
  1092.6 30.8 %collective-permute-start = (bf16[4,256,512]{1,2,0:T(8,128)(2,1)S(1)}, bf16[4,256,512]{1,2,0:T(8,128)(2,1)S(1)}, u32[]{:S(2)}, u32[]{:S(2)}) collective-permute-start(bf16[4,256,512]{1,2,0:T(8,128)(2,1)S(1)} %copy.104), channel_id=1, source_target_pairs={{0,4},{4,8},{8,12},{12,16},{16,20},{20,24},{24,28},{28,0},{1,5},{5... | collective-permute-start | bytes 3145736 | tf_op jit(solution)/shard_map/while/body/eval_jaxpr/ppermute | solution.py:16
  1094.1 40.6 %collective-permute-start.1 = (bf16[4,256,512]{1,2,0:T(8,128)(2,1)}, bf16[4,256,512]{1,2,0:T(8,128)(2,1)}, u32[]{:S(2)}, u32[]{:S(2)}) collective-permute-start(bf16[4,256,512]{1,2,0:T(8,128)(2,1)} %copy-done.15), channel_id=1, source_target_pairs={{0,4},{4,8},{8,12},{12,16},{16,20},{20,24},{24,28},{28,0},{1,5},{5... | collective-permute-start | bytes 3145736 | tf_op jit(solution)/shard_map/while/body/eval_jaxpr/ppermute | solution.py:16
  1153.2 40.6 %collective-permute-start.1 = (bf16[4,256,512]{1,2,0:T(8,128)(2,1)}, bf16[4,256,512]{1,2,0:T(8,128)(2,1)}, u32[]{:S(2)}, u32[]{:S(2)}) collective-permute-start(bf16[4,256,512]{1,2,0:T(8,128)(2,1)} %copy-done.15), channel_id=1, source_target_pairs={{0,4},{4,8},{8,12},{12,16},{16,20},{20,24},{24,28},{28,0},{1,5},{5... | collective-permute-start | bytes 3145736 | tf_op jit(solution)/shard_map/while/body/eval_jaxpr/ppermute | solution.py:16
  1212.2 40.6 %collective-permute-start.1 = (bf16[4,256,512]{1,2,0:T(8,128)(2,1)}, bf16[4,256,512]{1,2,0:T(8,128)(2,1)}, u32[]{:S(2)}, u32[]{:S(2)}) collective-permute-start(bf16[4,256,512]{1,2,0:T(8,128)(2,1)} %copy-done.15), channel_id=1, source_target_pairs={{0,4},{4,8},{8,12},{12,16},{16,20},{20,24},{24,28},{28,0},{1,5},{5... | collective-permute-start | bytes 3145736 | tf_op jit(solution)/shard_map/while/body/eval_jaxpr/ppermute | solution.py:16
  1262.8 92.3 %reduce-scatter.9.cloned.1.call-start = ((), (), s32[]{:S(2)}) async-start(), calls=%async_computation.17 | async-start | bytes 2359296 | tf_op jit(solution)/shard_map/reduce_scatter | solution.py:248
  1270.0 111.5 %reduce-scatter.11.cloned.1.call-start = ((), (), s32[]{:S(2)}) async-start(), calls=%async_computation.18 | async-start | bytes 2359296 | tf_op jit(solution)/shard_map/reduce_scatter | solution.py:251
  1276.6 284.6 %all-reduce.10.cloned.1.call-start = ((), (), s32[]{:S(2)}) async-start(), calls=%async_computation.22 | async-start | bytes 16777216 | tf_op jit(solution)/shard_map/psum | solution.py:153
  1317.3 335.6 %reduce-scatter.15.cloned.1.call-start = ((), (), s32[]{:S(2)}) async-start(), calls=%async_computation.20 | async-start | bytes 9437184 | tf_op jit(solution)/shard_map/reduce_scatter | solution.py:254
  1333.1 410.0 %reduce-scatter.17.cloned.1.call-start = ((), (), s32[]{:S(2)}) async-start(), calls=%async_computation.21 | async-start | bytes 9437184 | tf_op jit(solution)/shard_map/reduce_scatter | solution.py:260
  (137 other events, 5921.8 us)
Sparse Core Ops, SparseCore 0:
  9.7 30.6 all-gather.10
  42.0 28.5 all-gather.14
  72.2 28.7 all-gather.8
  102.5 78.8 all-gather.12
  182.8 80.5 all-gather.16
  264.9 33.8 all-gather.18
  312.1 104.6 all-reduce.5
  418.5 79.8 all-gather.20
  500.0 80.6 all-gather.22
  627.3 104.6 all-reduce.7
  766.6 35.0 reduce-scatter.12
  1262.9 43.8 reduce-scatter.6
  1309.6 34.5 reduce-scatter.8
  1346.4 35.0 reduce-scatter.10
  1385.0 176.1 all-reduce.9
  1563.5 89.3 reduce-scatter.14
  1655.2 87.9 reduce-scatter.16
where the time goes:
time: 1760 us; the launch traced here: 1750 us
  waiting for transfers between devices  954 us (54%)
  matrix products  340 us (19%)
  other arithmetic  211 us (12%)
  local copies, waits for them, and re-layouts  136 us (8%)
  starting transfers between devices  60.6 us (3%)
  blocking collectives  35.9 us (2%)
    ppermute x32, waiting for transfers between devices, shifted(): lax.ppermute(array, axis, [(i, (i + by) % count) for i in range(count)])  220 us
    psum x1, waiting for transfers between devices, body(): lax.psum(matmul(act_low, full_down).astype(jnp.bfloat16), 'tp')  178 us
    psum x1, waiting for transfers between devices, body(): lax.psum(matmul(mixed_low, full_out).astype(jnp.bfloat16), 'tp')  97.8 us
    psum x1, waiting for transfers between devices, body(): lax.psum(right_back(up_grad, back_up).astype(jnp.bfloat16), 'tp')  97.8 us
    reduce_scatter x1, waiting for transfers between devices, body(): lax.psum_scatter(grad_w_down.astype(jnp.bfloat16), 'band', scatter_dimens...  87.4 us
    gather x2, local copies, waits for them, and re-layouts, body(): all_live = jnp.take_along_axis(exit_depth, all_pos, axis=1) > LAYER  69.3 us
    all_gather x1, waiting for transfers between devices, body(): lax.all_gather(w_up, 'band', axis=0, tiled=True)  68.4 us
    all_gather x1, waiting for transfers between devices, body(): lax.all_gather(w_down, 'band', axis=1, tiled=True)  66.8 us
  transfers between devices with their start and end apart: 49, of which 39 were waited for; matrix products, arithmetic and copies ran while one was open for 34% of the time, Pallas kernels for 0%

commit v1 on v0

v1 whole, which is shorter than its diff:
```python
import functools
import math

import jax
import jax.numpy as jnp
from jax import lax
from jax.experimental import pallas as pl
from jax.experimental.pallas import tpu as pltpu
from jax.sharding import PartitionSpec as P

HEAD_DIM = 64
LAYER = 12
MESH = pl.DeviceIdType.MESH

epsilon = 1e-05
masked_score = -1e30
bf16 = jnp.bfloat16
f32 = jnp.float32


def layer_norm(values, gain, shift):
    center = values - jnp.mean(values, axis=-1, keepdims=True)
    inverse = lax.rsqrt(jnp.mean(center * center, axis=-1, keepdims=True) + epsilon)
    normed = center * inverse
    return (normed * gain + shift, normed, inverse)


def norm_back(grad_out, normed, inverse, gain):
    scaled = grad_out * gain
    return inverse * (
        scaled
        - jnp.mean(scaled, axis=-1, keepdims=True)
        - normed * jnp.mean(scaled * normed, axis=-1, keepdims=True)
    )


def nn(left, right):
    return jnp.dot(left, right, preferred_element_type=f32)


def nt(left, right):
    return lax.dot_general(left, right, (((1,), (1,)), ((), ())), preferred_element_type=f32)


def tn(left, right):
    return lax.dot_general(left, right, (((0,), (0,)), ((), ())), preferred_element_type=f32)


def gelu_exact(values):
    return jax.nn.gelu(values, approximate=False)


def halves(count):
    return (count // 2, 2) if count % 2 == 0 else (count, 1)


def greet(devices):
    barrier = pltpu.get_barrier_semaphore()
    for device in devices:
        pl.semaphore_signal(barrier, inc=1, device_id=device, device_id_type=MESH)
    pl.semaphore_wait(barrier, len(devices))


def takes(microseconds):
    return pl.CostEstimate(
        flops=int(microseconds * 1e9), bytes_accessed=int(microseconds * 2e6), transcendentals=0
    )


def keep(source, target, through, sem, k=0):
    first = pltpu.make_async_copy(source, through, sem.at[k])
    first.start()

    def second():
        first.wait()
        copy = pltpu.make_async_copy(through, target, sem.at[k + 1])
        copy.start()
        return copy

    return second


def grid_peers(count):
    na, nb = halves(count)
    me, band = lax.axis_index("tp"), lax.axis_index("band")
    a, b = me // nb, lax.rem(me, nb)
    along_b = [(band, a * nb + lax.rem(b + d, nb)) for d in range(1, nb)]
    along_a = [(band, lax.rem(a + d, na) * nb + b) for d in range(1, na)]
    from_b = [a * nb + lax.rem(b + nb - d, nb) for d in range(1, nb)]
    from_a = [lax.rem(a + na - d, na) * nb + b for d in range(1, na)]
    return me, a, b, along_a, along_b, from_a, from_b


def gather_kernel(count, inner_slot, with_extra, *refs):
    if with_extra:
        x_ref, e_ref, o_ref, t_ref, through, local_sem, send_sem, recv_sem, part_ref, in_b, in_a = refs
    else:
        x_ref, o_ref, through, local_sem, send_sem, recv_sem = refs
    me, a, b, along_a, along_b, from_a, from_b = grid_peers(count)
    half = x_ref.shape[0] // 2
    part = (pl.ds(0, half), pl.ds(half, half))

    def slot(index, which):
        return o_ref.at[part[which], index] if inner_slot else o_ref.at[index, part[which]]

    greet(along_a + along_b)
    whole = o_ref.at[:, me] if inner_slot else o_ref.at[me]
    local = keep(x_ref, whole, through, local_sem)
    used = []

    def move(source, target, device):
        k = len(used)
        copy = pltpu.make_async_remote_copy(
            source, target, send_sem.at[k], recv_sem.at[k],
            device_id=device, device_id_type=MESH,
        )
        copy.start()
        used.append(copy)
        return copy

    def send(source, index, which, device):
        return move(source, slot(index, which), device)

    if with_extra:
        extra_b = [move(e_ref, in_b.at[k], device) for k, device in enumerate(along_b)]
    first_b = [send(x_ref.at[part[0]], me, 0, device) for device in along_b]
    first_a = [send(x_ref.at[part[1]], me, 1, device) for device in along_a]
    second = [send(x_ref.at[part[0]], me, 0, device) for device in along_a]
    second += [send(x_ref.at[part[1]], me, 1, device) for device in along_b]
    local = local()
    if with_extra:
        total = e_ref[...]
        for k, copy in enumerate(extra_b):
            copy.wait_recv()
            total = total + in_b[k]
        part_ref[...] = total
        extra_a = [move(part_ref, in_a.at[k], device) for k, device in enumerate(along_a)]
    for copy, source in zip(first_b, from_b):
        copy.wait_recv()
        second += [send(slot(source, 0), source, 0, device) for device in along_a]
    for copy, source in zip(first_a, from_a):
        copy.wait_recv()
        second += [send(slot(source, 1), source, 1, device) for device in along_b]
    if with_extra:
        total = part_ref[...]
        for k, copy in enumerate(extra_a):
            copy.wait_recv()
            total = total + in_a[k]
        t_ref[...] = total
        for copy in extra_a + extra_b:
            copy.wait_send()
    for copy in first_a + first_b:
        copy.wait_send()
    for copy in second:
        copy.wait()
    local.wait()


def gather_tp(x, cid, inner_slot=False, extra=None):
    count = lax.axis_size("tp")
    na, nb = halves(count)
    copies = 2 * (na - 1 + nb - 1) + 2 * (na - 1) * (nb - 1)
    shape = (x.shape[0], count) + x.shape[1:] if inner_slot else (count,) + x.shape
    operands, shapes = [x], [jax.ShapeDtypeStruct(shape, x.dtype)]
    specs = [pl.BlockSpec(memory_space=pl.ANY)]
    more = []
    if extra is not None:
        operands.append(extra)
        shapes.append(jax.ShapeDtypeStruct(extra.shape, extra.dtype))
        specs.append(pl.BlockSpec(memory_space=pltpu.VMEM))
        copies += na - 1 + nb - 1
        more = [
            pltpu.VMEM(extra.shape, extra.dtype),
            pltpu.VMEM((max(nb - 1, 1),) + extra.shape, extra.dtype),
            pltpu.VMEM((max(na - 1, 1),) + extra.shape, extra.dtype),
        ]
    out = pl.pallas_call(
        functools.partial(gather_kernel, count, inner_slot, extra is not None),
        out_shape=tuple(shapes),
        in_specs=specs,
        out_specs=tuple(specs),
        scratch_shapes=[
            pltpu.VMEM(x.shape, x.dtype),
            pltpu.SemaphoreType.DMA((2,)),
            pltpu.SemaphoreType.DMA((copies,)),
            pltpu.SemaphoreType.DMA((copies,)),
            *more,
        ],
        compiler_params=pltpu.CompilerParams(collective_id=cid, has_side_effects=True),
        cost_estimate=takes(36),
        name="gather_tp",
    )(*operands)
    return out if extra is not None else out[0]


def scatter_kernel(
    count, p_ref, o_ref, own_a, own_b, one_a, one_b, out_a, out_b, two_a, two_b,
    local_sem, send_sem, recv_sem,
):
    na, nb = halves(count)
    me, a, b, along_a, along_b, from_a, from_b = grid_peers(count)
    half = p_ref.shape[1] // 2
    top, low = pl.ds(0, half), pl.ds(half, half)
    greet(along_a + along_b)
    used = []

    def send(source, target, device):
        k = len(used)
        copy = pltpu.make_async_remote_copy(
            source, target, send_sem.at[k], recv_sem.at[k],
            device_id=device, device_id_type=MESH,
        )
        copy.start()
        used.append(copy)
        return copy

    order_a = list(range(1, na)) + [0]
    order_b = list(range(1, nb)) + [0]
    first_a, first_b = {}, {}
    for step in range(max(na, nb)):
        if step < na:
            e = order_a[step]
            row = lax.rem(a + e, na) * nb
            for d in range(1, nb):
                source = p_ref.at[row + lax.rem(b + d, nb), top]
                first_b[d, e] = send(source, one_a.at[d - 1, e], along_b[d - 1])
        if step < nb:
            e = order_b[step]
            column = lax.rem(b + e, nb)
            for d in range(1, na):
                source = p_ref.at[lax.rem(a + d, na) * nb + column, low]
                first_a[d, e] = send(source, one_b.at[d - 1, e], along_a[d - 1])
    local_a, local_b = {}, {}
    for e in order_a:
        local_a[e] = pltpu.make_async_copy(
            p_ref.at[lax.rem(a + e, na) * nb + b, top], own_a.at[e], local_sem.at[e]
        )
        local_a[e].start()
    for e in order_b:
        local_b[e] = pltpu.make_async_copy(
            p_ref.at[a * nb + lax.rem(b + e, nb), low], own_b.at[e], local_sem.at[na + e]
        )
        local_b[e].start()
    second_a, second_b = {}, {}
    for e in order_a[:-1]:
        local_a[e].wait()
        total = own_a[e].astype(f32)
        for d in range(1, nb):
            first_b[d, e].wait_recv()
            total = total + one_a[d - 1, e].astype(f32)
        out_a[e - 1] = total.astype(out_a.dtype)
        second_a[e] = send(out_a.at[e - 1], two_a.at[e - 1], along_a[e - 1])
    for e in order_b[:-1]:
        local_b[e].wait()
        total = own_b[e].astype(f32)
        for d in range(1, na):
            first_a[d, e].wait_recv()
            total = total + one_b[d - 1, e].astype(f32)
        out_b[e - 1] = total.astype(out_b.dtype)
        second_b[e] = send(out_b.at[e - 1], two_b.at[e - 1], along_b[e - 1])
    local_a[0].wait()
    total = own_a[0].astype(f32)
    for d in range(1, nb):
        first_b[d, 0].wait_recv()
        total = total + one_a[d - 1, 0].astype(f32)
    for e in order_a[:-1]:
        second_a[e].wait_recv()
        total = total + two_a[e - 1].astype(f32)
    o_ref[top] = total
    local_b[0].wait()
    total = own_b[0].astype(f32)
    for d in range(1, na):
        first_a[d, 0].wait_recv()
        total = total + one_b[d - 1, 0].astype(f32)
    for e in order_b[:-1]:
        second_b[e].wait_recv()
        total = total + two_b[e - 1].astype(f32)
    o_ref[low] = total
    for copy in used:
        copy.wait_send()


def scatter_tp(partial, cid):
    count, rows, width = partial.shape
    na, nb = halves(count)
    half = rows // 2
    copies = 2 * (na - 1) * (nb - 1) + 2 * (na - 1 + nb - 1)
    block = (half, width)

    def buffer(*lead):
        return pltpu.VMEM(tuple(max(n, 1) for n in lead) + block, partial.dtype)

    return pl.pallas_call(
        functools.partial(scatter_kernel, count),
        out_shape=jax.ShapeDtypeStruct((rows, width), f32),
        in_specs=[pl.BlockSpec(memory_space=pl.ANY)],
        out_specs=pl.BlockSpec(memory_space=pltpu.VMEM),
        scratch_shapes=[
            buffer(na), buffer(nb),
            buffer(nb - 1, na), buffer(na - 1, nb),
            buffer(na - 1), buffer(nb - 1),
            buffer(na - 1), buffer(nb - 1),
            pltpu.SemaphoreType.DMA((na + nb,)),
            pltpu.SemaphoreType.DMA((copies,)),
            pltpu.SemaphoreType.DMA((copies,)),
        ],
        compiler_params=pltpu.CompilerParams(
            collective_id=cid, has_side_effects=True, vmem_limit_bytes=40 * 2**20
        ),
        cost_estimate=takes(36),
        name="scatter_tp",
    )(partial)


def gather_later(x):
    count = lax.axis_size("tp")
    return lax.all_to_all(jnp.broadcast_to(x[None], (count,) + x.shape), "tp", 0, 0)


def swap_kernel(size, with_positions, *refs):
    if with_positions:
        x_ref, p_ref, o_ref, q_ref, through, p_through, local_sem, send_sem, recv_sem = refs
    else:
        x_ref, o_ref, through, local_sem, send_sem, recv_sem = refs
    me, tp = lax.axis_index("band"), lax.axis_index("tp")
    others = [lax.rem(me + d, size) for d in range(1, size)]
    greet([(other, tp) for other in others])
    local = [keep(x_ref.at[me], o_ref.at[me], through, local_sem)]
    if with_positions:
        local.append(keep(p_ref, q_ref.at[me], p_through, local_sem, 2))
    copies = []
    for k, other in enumerate(others):
        if with_positions:
            copies.append(
                pltpu.make_async_remote_copy(
                    p_ref, q_ref.at[me], send_sem.at[size - 1 + k], recv_sem.at[size - 1 + k],
                    device_id=(other, tp), device_id_type=MESH,
                )
            )
        copies.append(
            pltpu.make_async_remote_copy(
                x_ref.at[other], o_ref.at[me], send_sem.at[k], recv_sem.at[k],
                device_id=(other, tp), device_id_type=MESH,
            )
        )
    for copy in copies:
        copy.start()
    local = [rest() for rest in local]
    for copy in copies + local:
        copy.wait()


def swap_band(x, cid, positions=None):
    size = lax.axis_size("band")
    operands, shapes = [x], [jax.ShapeDtypeStruct(x.shape, x.dtype)]
    if positions is not None:
        operands.append(positions)
        shapes.append(jax.ShapeDtypeStruct((size,) + positions.shape, positions.dtype))
    lanes = (size - 1) * len(operands)
    out = pl.pallas_call(
        functools.partial(swap_kernel, size, positions is not None),
        out_shape=tuple(shapes),
        in_specs=[pl.BlockSpec(memory_space=pl.ANY)] * len(operands),
        out_specs=tuple([pl.BlockSpec(memory_space=pl.ANY)] * len(operands)),
        scratch_shapes=[
            pltpu.VMEM(x.shape[1:], x.dtype),
            *(pltpu.VMEM(extra.shape, extra.dtype) for extra in operands[1:]),
            pltpu.SemaphoreType.DMA((4,)),
            pltpu.SemaphoreType.DMA((lanes,)),
            pltpu.SemaphoreType.DMA((lanes,)),
        ],
        compiler_params=pltpu.CompilerParams(collective_id=cid, has_side_effects=True),
        cost_estimate=takes(30),
        name="swap_band",
    )(*operands)
    return out if positions is not None else out[0]


def heads_kernel(group, x_ref, o_ref, through, local_sem, send_sem, recv_sem):
    band, tp = lax.axis_index("band"), lax.axis_index("tp")
    mine = lax.rem(band, group)
    base = band - mine
    others = [lax.rem(mine + d, group) for d in range(1, group)]
    greet([(base + other, tp) for other in others])
    local = keep(x_ref.at[mine], o_ref.at[mine], through, local_sem)
    copies = [
        pltpu.make_async_remote_copy(
            x_ref.at[other], o_ref.at[mine], send_sem.at[k], recv_sem.at[k],
            device_id=(base + other, tp), device_id_type=MESH,
        )
        for k, other in enumerate(others)
    ]
    for copy in copies:
        copy.start()
    for copy in [local(), *copies]:
        copy.wait()


def swap_heads(x, group, cid):
    return pl.pallas_call(
        functools.partial(heads_kernel, group),
        out_shape=jax.ShapeDtypeStruct(x.shape, x.dtype),
        in_specs=[pl.BlockSpec(memory_space=pl.ANY)],
        out_specs=pl.BlockSpec(memory_space=pl.ANY),
        scratch_shapes=[
            pltpu.VMEM(x.shape[1:], x.dtype),
            pltpu.SemaphoreType.DMA((2,)),
            pltpu.SemaphoreType.DMA((group - 1,)),
            pltpu.SemaphoreType.DMA((group - 1,)),
        ],
        compiler_params=pltpu.CompilerParams(collective_id=cid, has_side_effects=True),
        cost_estimate=takes(4),
        name="swap_heads",
    )(x)


def project_kernel(x_ref, w_ref, bias_ref, scale_ref, o_ref):
    total = nn(x_ref[...], w_ref[...]) + bias_ref[...]
    o_ref[0] = total.astype(bf16) * scale_ref[...].astype(bf16)


def project(x, weight, bias, scale, group):
    rows, depth = x.shape
    width = weight.shape[1] // group
    if width % 128:
        total = (nn(x, weight) + bias).astype(bf16) * scale.astype(bf16)
        return total.reshape(rows, group, width).transpose(1, 0, 2)
    block = min(256, rows)
    return pl.pallas_call(
        project_kernel,
        out_shape=jax.ShapeDtypeStruct((group, rows, width), bf16),
        grid=(group, rows // block),
        in_specs=[
            pl.BlockSpec((block, depth), lambda g, i: (i, 0)),
            pl.BlockSpec((depth, width), lambda g, i: (0, g)),
            pl.BlockSpec((1, width), lambda g, i: (0, g)),
            pl.BlockSpec((1, width), lambda g, i: (0, g)),
        ],
        out_specs=pl.BlockSpec((1, block, width), lambda g, i: (g, i, 0)),
        compiler_params=pltpu.CompilerParams(vmem_limit_bytes=40 * 2**20),
        cost_estimate=pl.CostEstimate(
            flops=2 * rows * depth * width * group, bytes_accessed=12 * 2**20, transcendentals=0
        ),
        name="project",
    )(x, weight, bias[None], scale[None])


def permitted(first, row, column, live_end):
    return (column >= first) & (column <= row) & ((column < live_end) | (column == row))


def head_mask(width, head, shape):
    lane = lax.broadcasted_iota(jnp.int32, shape, 1)
    return (lane >= head * HEAD_DIM) & (lane < (head + 1) * HEAD_DIM)


def attend_kernel(block, info_ref, first_ref, q_ref, k_ref, v_ref, o_ref, log_ref, vt_ref):
    length, width = q_ref.shape
    heads = width // HEAD_DIM
    live_end = info_ref[0]
    count = lax.div(live_end + block - 1, block)
    vt_ref[...] = v_ref[...].T
    o_ref[...] = jnp.zeros_like(o_ref)
    log_ref[...] = jnp.zeros_like(log_ref)

    def queries(i, _):
        rows = pl.ds(pl.multiple_of(i * block, block), block)
        q = q_ref[rows, :]
        first = first_ref[0:1, rows]
        row = i * block + lax.broadcasted_iota(jnp.int32, (1, block), 1)
        q_heads = [
            jnp.where(head_mask(width, h, (block, width)), q, jnp.zeros_like(q)) for h in range(heads)
        ]

        def keys(j, carry):
            columns = pl.ds(pl.multiple_of(j * block, block), block)
            k = k_ref[columns, :]
            column = j * block + lax.broadcasted_iota(jnp.int32, (block, 1), 0)
            allowed = permitted(first, row, column, live_end)
            out = []
            for h in range(heads):
                top, total, summed = carry[h]
                scores = jnp.where(allowed, nt(k, q_heads[h]), masked_score)
                new_top = jnp.maximum(top, jnp.max(scores, axis=0, keepdims=True))
                weights = jnp.exp(scores - new_top)
                scale = jnp.exp(top - new_top)
                total = total * scale + jnp.sum(weights, axis=0, keepdims=True)
                vt = vt_ref[h * HEAD_DIM : (h + 1) * HEAD_DIM, columns]
                summed = summed * scale + nn(vt, weights.astype(bf16))
                out.append((new_top, total, summed))
            return tuple(out)

        start = tuple(
            (
                jnp.full((1, block), masked_score, f32),
                jnp.zeros((1, block), f32),
                jnp.zeros((HEAD_DIM, block), f32),
            )
            for _ in range(heads)
        )
        done = lax.fori_loop(info_ref[1 + i], i + 1, keys, start)
        mixed = jnp.concatenate([summed / total for _, total, summed in done], axis=0)
        o_ref[rows, :] = mixed.T.astype(o_ref.dtype)
        for h, (top, total, _) in enumerate(done):
            log_ref[0, h : h + 1, rows] = top + jnp.log(total)
        return 0

    lax.fori_loop(0, count, queries, 0)


def attend_back_kernel(
    block, info_ref, first_ref, q_ref, k_ref, v_ref, o_ref, do_ref, log_ref, out_ref, dk_acc, dv_acc
):
    length, width = q_ref.shape
    heads = width // HEAD_DIM
    features = out_ref.shape[1] // 3
    slab = pl.program_id(0)
    factor = HEAD_DIM ** (-0.5)
    live_end = info_ref[0]
    count = lax.div(live_end + block - 1, block)

    def lanes(which):
        if features == width:
            return pl.ds(which * features, width)
        return pl.ds(pl.multiple_of(which * features + slab * width, width), width)

    dk_acc[...] = jnp.zeros_like(dk_acc)
    dv_acc[...] = jnp.zeros_like(dv_acc)
    out_ref[:, lanes(0)] = jnp.zeros((length, width), out_ref.dtype)

    def queries(i, _):
        rows = pl.ds(pl.multiple_of(i * block, block), block)
        q, do = q_ref[rows, :], do_ref[rows, :]
        first = first_ref[0:1, rows]
        row = i * block + lax.broadcasted_iota(jnp.int32, (1, block), 1)
        dots = (do.astype(f32) * o_ref[rows, :].astype(f32)).T
        masks = [head_mask(width, h, (block, width)) for h in range(heads)]
        zero = jnp.zeros_like(q)
        q_heads = [jnp.where(mask, q, zero) for mask in masks]
        do_heads = [jnp.where(mask, do, zero) for mask in masks]
        logs = [log_ref[0, h : h + 1, rows] for h in range(heads)]
        deltas = [
            jnp.sum(dots[h * HEAD_DIM : (h + 1) * HEAD_DIM], axis=0, keepdims=True)
            for h in range(heads)
        ]

        def keys(j, dq):
            columns = pl.ds(pl.multiple_of(j * block, block), block)
            k, v = k_ref[columns, :], v_ref[columns, :]
            column = j * block + lax.broadcasted_iota(jnp.int32, (block, 1), 0)
            allowed = permitted(first, row, column, live_end)
            dk, dv = dk_acc[columns, :], dv_acc[columns, :]
            for h in range(heads):
                scores = jnp.where(allowed, nt(k, q_heads[h]) - logs[h], masked_score)
                probs = jnp.exp(scores)
                prob_grad = nt(v, do_heads[h])
                score_grad = (probs * (prob_grad - deltas[h])).astype(bf16)
                dv = dv + nn(probs.astype(bf16), do_heads[h])
                dk = dk + nn(score_grad, q_heads[h])
                dq = dq + tn(score_grad, jnp.where(masks[h], k, zero))
            dk_acc[columns, :] = dk
            dv_acc[columns, :] = dv
            return dq

        dq = lax.fori_loop(info_ref[1 + i], i + 1, keys, jnp.zeros((block, width), f32))
        out_ref[rows, lanes(0)] = (dq * factor).astype(out_ref.dtype)
        return 0

    lax.fori_loop(0, count, queries, 0)
    out_ref[:, lanes(1)] = dk_acc[...].astype(out_ref.dtype)
    out_ref[:, lanes(2)] = dv_acc[...].astype(out_ref.dtype)


def attention_specs(length, features):
    width = min(128, features)
    slabs = features // width

    plain = pl.BlockSpec((length, width), lambda i, info: (0, i))

    def piece(which):
        if features % 128:
            return plain
        return pl.BlockSpec((length, width), lambda i, info, w=which: (0, w * slabs + i))

    logs = pl.BlockSpec((1, 8, length), lambda i, info: (i, 0, 0))
    first = pl.BlockSpec((1, length), lambda i, info: (0, 0))
    return width, slabs, piece, plain, logs, first


def three(qkv, features):
    if features % 128:
        return [qkv[:, w * features : (w + 1) * features] for w in range(3)]
    return [qkv] * 3


def attend(qkv, info, first, block):
    length, features = qkv.shape[0], qkv.shape[1] // 3
    width, slabs, piece, plain, logs, first_spec = attention_specs(length, features)
    return pl.pallas_call(
        functools.partial(attend_kernel, block),
        out_shape=(
            jax.ShapeDtypeStruct((length, features), bf16),
            jax.ShapeDtypeStruct((slabs, 8, length), f32),
        ),
        grid_spec=pltpu.PrefetchScalarGridSpec(
            num_scalar_prefetch=1,
            grid=(slabs,),
            in_specs=[first_spec, piece(0), piece(1), piece(2)],
            out_specs=(plain, logs),
            scratch_shapes=[pltpu.VMEM((width, length), bf16)],
        ),
        compiler_params=pltpu.CompilerParams(vmem_limit_bytes=40 * 2**20),
        cost_estimate=takes(36),
        name="attend",
    )(info, first, *three(qkv, features))


def attend_back(qkv, mixed, grad, log_total, info, first, block):
    length, features = qkv.shape[0], qkv.shape[1] // 3
    width, slabs, piece, plain, logs, first_spec = attention_specs(length, features)
    return pl.pallas_call(
        functools.partial(attend_back_kernel, block),
        out_shape=jax.ShapeDtypeStruct((length, 3 * features), bf16),
        grid_spec=pltpu.PrefetchScalarGridSpec(
            num_scalar_prefetch=1,
            grid=(slabs,),
            in_specs=[first_spec, piece(0), piece(1), piece(2), plain, plain, logs],
            out_specs=pl.BlockSpec((length, 3 * features), lambda i, info: (0, 0)),
            scratch_shapes=[pltpu.VMEM((length, width), f32), pltpu.VMEM((length, width), f32)],
        ),
        compiler_params=pltpu.CompilerParams(vmem_limit_bytes=40 * 2**20),
        cost_estimate=takes(40),
        name="attend_back",
    )(info, first, *three(qkv, features), mixed, grad, log_total)


def body(
    tokens,
    positions,
    doc_lengths,
    exit_depth,
    w_query,
    w_key,
    w_value,
    w_out,
    w_up,
    w_down,
    b_query,
    b_value,
    b_out,
    b_up,
    b_down,
    attn_gain,
    attn_bias,
    ffn_gain,
    ffn_bias,
    cotangent,
):
    seqs, local_rows, width = tokens.shape
    inner = b_query.shape[0]
    bands, tps = lax.axis_size("band"), lax.axis_size("tp")
    group = bands // seqs
    piece = local_rows // (group * tps)
    band, tp = lax.axis_index("band"), lax.axis_index("tp")
    seq, member = band // group, lax.rem(band, group)
    features = inner // group
    length = exit_depth.shape[1]
    own = bands * piece
    rows = tps * own
    block = min(256, length)

    def by_group(*parts):
        split = [p.reshape(p.shape[:-1] + (group, features)) for p in parts]
        return jnp.stack(split, axis=-2).reshape(parts[0].shape[:-1] + (-1,))

    def share(grad):
        return lax.psum_scatter(grad, "band", scatter_dimension=0, tiled=True)

    w_in = lax.all_gather(by_group(w_query, w_key, w_value), "band", axis=0, tiled=True)
    w_out_t = lax.all_gather(w_out.T, "band", axis=0, tiled=True)
    w_up_all = lax.all_gather(w_up, "band", axis=0, tiled=True)
    w_down_t = lax.all_gather(w_down.T, "band", axis=0, tiled=True)

    def my_share(array):
        split = array.reshape(seqs, group, tps, piece, width)
        return lax.dynamic_index_in_dim(split, tp, 2, keepdims=False).reshape(bands, piece, width)

    token_own, all_pos = swap_band(my_share(tokens), 0, positions)
    token_own, grad_own = lax.optimization_barrier((token_own, my_share(cotangent)))
    grad_own = lax.all_to_all(grad_own, "band", 0, 0)
    seq_pos = lax.dynamic_index_in_dim(all_pos, seq, 1, keepdims=False)
    seq_pos = seq_pos.reshape(bands, group, tps, piece).transpose(1, 2, 0, 3)
    row_pos = seq_pos.reshape(length)
    member_pos = lax.dynamic_index_in_dim(seq_pos, member, 0, keepdims=False)
    own_pos = lax.dynamic_index_in_dim(member_pos, tp, 0, keepdims=False).reshape(own)
    depths = lax.dynamic_index_in_dim(exit_depth, seq, 0, keepdims=False)
    live_end = jnp.sum((depths > LAYER).astype(jnp.int32))
    live_own = (own_pos < live_end).astype(f32)[:, None]
    ends = jnp.cumsum(lax.dynamic_index_in_dim(doc_lengths, seq, 0, keepdims=False))
    places = jnp.arange(length, dtype=jnp.int32)
    first = jnp.max(jnp.where(ends[:, None] <= places[None, :], ends[:, None], 0), axis=0)
    info = jnp.concatenate([live_end[None], first[::block] // block]).astype(jnp.int32)
    first = first[None, :].astype(jnp.int32)
    to_sorted = (row_pos[None, :] == places[:, None]).astype(bf16)
    to_rows = (row_pos[:, None] == places[None, :]).astype(bf16)

    inputs = token_own.reshape(own, width).astype(f32)
    normed_in, unit_in, inverse_in = layer_norm(inputs, attn_gain, attn_bias)
    z1 = gather_tp(normed_in.astype(bf16), 1).reshape(rows, width)


    bias_in = by_group(b_query, jnp.zeros_like(b_query), b_value)
    scale_in = by_group(
        jnp.full_like(b_query, HEAD_DIM ** (-0.5)), jnp.ones_like(b_query), jnp.ones_like(b_query)
    )
    qkv = project(z1, w_in, bias_in, scale_in, group)
    qkv = swap_heads(qkv, group, 4).reshape(length, 3 * features)
    qkv = nn(to_sorted, qkv).astype(bf16)
    qkv, grad_own = lax.optimization_barrier((qkv, grad_own))
    grad_own = grad_own.reshape(own, width).astype(f32)
    down_grad_own = (live_own * grad_own).astype(bf16)
    down_grad = gather_later(down_grad_own)
    mixed_sorted, log_total = attend(qkv, info, first, block)
    mixed_sorted, down_grad = lax.optimization_barrier((mixed_sorted, down_grad))
    down_grad = down_grad.reshape(rows, width)
    mixed = nn(to_rows, mixed_sorted).astype(bf16).reshape(group, rows, features)
    mixed = swap_heads(mixed, group, 5).transpose(1, 0, 2).reshape(rows, inner)

    attn_part = nt(mixed, w_out_t).astype(bf16).reshape(tps, own, width)
    attn_out = scatter_tp(attn_part, 6) + b_out
    residual = inputs + attn_out
    normed_mid, unit_mid, inverse_mid = layer_norm(residual, ffn_gain, ffn_bias)
    z2 = gather_tp(normed_mid.astype(bf16), 7).reshape(rows, width)
    pre_act = nn(z2, w_up_all) + b_up
    below = 0.5 * (1.0 + lax.erf(pre_act * 0.5**0.5))
    act = (pre_act * below).astype(bf16)
    slope = (below + pre_act * jnp.exp(-0.5 * pre_act * pre_act) * (2 * math.pi) ** -0.5).astype(bf16)

    ffn_part = nt(act, w_down_t).astype(bf16).reshape(tps, own, width)
    act, ffn_part = lax.optimization_barrier((act, ffn_part))
    ffn_part = lax.all_to_all(ffn_part, "tp", 0, 0)
    grad_w_down_t = tn(down_grad, act).astype(bf16)
    up_grad = (nn(down_grad, w_down_t) * slope.astype(f32)).astype(bf16)
    up_grad, grad_w_down_t = lax.optimization_barrier((up_grad, grad_w_down_t))
    shared_down = share(grad_w_down_t)
    grad_w_up = tn(z2, up_grad).astype(bf16)
    mid_part = nt(up_grad, w_up_all).astype(bf16).reshape(tps, own, width)
    mid_part, ffn_part = lax.optimization_barrier((mid_part, ffn_part))
    ffn_out = jnp.sum(ffn_part.astype(f32), axis=0) + b_down
    output_own = (inputs + live_own * (attn_out + ffn_out)).astype(bf16)
    output = lax.all_to_all(output_own.reshape(bands, piece, width), "band", 0, 0)
    mid_grad = scatter_tp(mid_part, 8)
    resid_grad = norm_back(mid_grad, unit_mid, inverse_mid, ffn_gain)
    attn_grad_own = (live_own * grad_own + resid_grad).astype(bf16)
    attn_grad = gather_tp(attn_grad_own, 9).reshape(rows, width)
    attn_grad, grad_w_up, output = lax.optimization_barrier((attn_grad, grad_w_up, output))
    output = gather_later(output)


    grad_w_out_t = tn(attn_grad, mixed).astype(bf16)
    mixed_grad = nn(attn_grad, w_out_t).astype(bf16)
    mixed_grad = mixed_grad.reshape(rows, group, features).transpose(1, 0, 2)
    mixed_grad = swap_heads(mixed_grad, group, 13).reshape(length, features)
    mixed_grad = nn(to_sorted, mixed_grad).astype(bf16)
    grad_w_up, shared_down = lax.optimization_barrier((grad_w_up, shared_down))
    shared_up = share(grad_w_up)
    mixed_grad, grad_w_out_t = lax.optimization_barrier((mixed_grad, grad_w_out_t))
    in_grad = attend_back(qkv, mixed_sorted, mixed_grad, log_total, info, first, block)
    shared_up, grad_w_out_t = lax.optimization_barrier((shared_up, grad_w_out_t))
    shared_out = share(grad_w_out_t)
    in_grad, output = lax.optimization_barrier((in_grad, output))
    output = output.transpose(1, 0, 2, 3).reshape(tokens.shape)
    in_grad = nn(to_rows, in_grad).astype(bf16).reshape(group, rows, 3 * features)
    in_grad = swap_heads(in_grad, group, 14).transpose(1, 0, 2).reshape(rows, 3 * inner)
    grad_w_in = tn(z1, in_grad).astype(bf16)
    in_part = nt(in_grad, w_in).astype(bf16).reshape(tps, own, width)
    input_grad = scatter_tp(in_part, 15)
    token_grad = grad_own + resid_grad + norm_back(input_grad, unit_in, inverse_in, attn_gain)

    def over_rows(array):
        return jnp.sum(array.astype(f32), axis=0)

    wide = [
        over_rows(attn_grad_own),
        over_rows(down_grad_own),
        over_rows(input_grad * unit_in),
        over_rows(input_grad),
        over_rows(mid_grad * unit_mid),
        over_rows(mid_grad),
    ]
    in_sums = over_rows(in_grad).reshape(group, 3, features)
    narrow = [in_sums[:, 0].reshape(-1), in_sums[:, 2].reshape(-1), over_rows(up_grad)]
    small = jnp.concatenate(wide + narrow)
    count = small.shape[0]
    small = jnp.pad(small, (0, -count % 2048)).astype(bf16).reshape(16, -1)
    token_grad, small = swap_band(token_grad.astype(bf16).reshape(bands, piece, width), 16, small)
    small = jnp.sum(small.astype(f32), axis=0).reshape(-1)
    narrow = small[6 * width : count]
    token_grad, wide = gather_tp(token_grad, 17, True, small[: 6 * width].reshape(-1, width))
    token_grad = token_grad.reshape(tokens.shape).astype(f32)
    grad_w_in, shared_out = lax.optimization_barrier((grad_w_in, shared_out))
    shared_in = share(grad_w_in).astype(f32).reshape(-1, group, 3, features)
    shared_down, shared_out = shared_down.astype(f32).T, shared_out.astype(f32).T
    shared_up = shared_up.astype(f32)
    shared_q, shared_k, shared_v = (
        shared_in[:, :, which].reshape(-1, inner) for which in range(3)
    )

    return (
        output,
        token_grad,
        shared_q,
        shared_k,
        shared_v,
        shared_out,
        shared_up,
        shared_down,
        narrow[:inner],
        narrow[inner : 2 * inner],
        wide[0],
        narrow[2 * inner :],
        wide[1],
        wide[2],
        wide[3],
        wide[4],
        wide[5],
    )


def solution(mesh):
    return jax.shard_map(
        body,
        mesh=mesh,
        in_specs=(
            P(None, "band", None),
            P(None, "band"),
            P(),
            P(),
            P("band", "tp"),
            P("band", "tp"),
            P("band", "tp"),
            P("tp", "band"),
            P("band", "tp"),
            P("tp", "band"),
            P("tp"),
            P("tp"),
            P(),
            P("tp"),
            P(),
            P(),
            P(),
            P(),
            P(),
            P(None, "band", None),
        ),
        out_specs=(
            P(None, "band", None),
            P(None, "band", None),
            P("band", "tp"),
            P("band", "tp"),
            P("band", "tp"),
            P("tp", "band"),
            P("band", "tp"),
            P("tp", "band"),
            P("tp"),
            P("tp"),
            P(),
            P("tp"),
            P(),
            P(),
            P(),
            P(),
            P(),
        ),
        check_vma=False,
    )
```

time: 1760 us -> 806 us (0.46)
  waiting for transfers between devices: 954 us -> 43.8 us
  Pallas kernels: 0 us -> 455 us
  matrix products: 340 us -> 151 us
  other arithmetic: 211 us -> 39.1 us
  local copies, waits for them, and re-layouts: 136 us -> 65.3 us
  blocking collectives: 35.9 us -> 0 us
  starting transfers between devices: 60.6 us -> 26.5 us
    pallas_call x0 -> x16, Pallas kernels: none -> 455 us  [the longest x4 147 us: gather_tp(): pl.pallas_call(functools.partial(gather_kernel, count, inner_slot, extra...]
    psum x3 -> x0, waiting for transfers between devices: 374 us -> none  [the longest x1 178 us: body(): lax.psum(matmul(act_low, full_down).astype(jnp.bfloat16), 'tp')]
    ppermute x32 -> x0, waiting for transfers between devices: 220 us -> none  [shifted(): lax.ppermute(array, axis, [(i, (i + by) % count) for i in range(count)])]
    all_gather x8 -> x4, waiting for transfers between devices: 207 us -> 0.05 us  [the longest x1 0.02 us: body(): w_out_t = lax.all_gather(w_out.T, 'band', axis=0, tiled=True)]
    dot_general x60 -> x15, matrix products: 340 us -> 151 us  [the longest x7 68.2 us: nn(): return jnp.dot(left, right, preferred_element_type=f32)]
    reduce_scatter x6 -> x4, waiting for transfers between devices: 149 us -> 0.04 us  [share(): return lax.psum_scatter(grad, 'band', scatter_dimension=0, tiled=True)]
    convert_element_type x52 -> x8, other arithmetic: 106 us -> 19.6 us  [the longest x1 6.75 us: body(): token_grad = token_grad.reshape(tokens.shape).astype(f32)]
    gather x2 -> x0, local copies, waits for them, and re-layouts: 69.3 us -> none  [body(): all_live = jnp.take_along_axis(exit_depth, all_pos, axis=1) > LAYER]
  transfers between devices with their start and end apart: 49 -> 13, of which waited for: 39 -> 3; matrix products, arithmetic and copies ran while one was open for 34% -> 23% of each run, Pallas kernels for 0% -> 57%
where the time goes in v1:
time: 806 us; the launch traced here: 797 us
  Pallas kernels  455 us (56%)
  matrix products  151 us (19%)
  local copies, waits for them, and re-layouts  65.3 us (8%)
  waiting for transfers between devices  43.8 us (5%)
  other arithmetic  39.1 us (5%)
  starting transfers between devices  26.5 us (3%)
  between operations  15.8 us (2%)
    pallas_call x4, Pallas kernels, gather_tp(): pl.pallas_call(functools.partial(gather_kernel, count, inner_slot, extra...  147 us
    pallas_call x2, Pallas kernels, swap_band(): pl.pallas_call(functools.partial(swap_kernel, size, positions is not None...  109 us
    pallas_call x3, Pallas kernels, scatter_tp(): pl.pallas_call(functools.partial(scatter_kernel, count), out_shape=jax.Sh...  107 us
    dot_general x7, matrix products, nn(): return jnp.dot(left, right, preferred_element_type=f32)  68.2 us
    dot_general x4, matrix products, nt(): lax.dot_general(left, right, (((1,), (1,)), ((), ())), preferred_element_...  45.6 us
    dot_general x4, matrix products, tn(): lax.dot_general(left, right, (((0,), (0,)), ((), ())), preferred_element_...  37.7 us
    unnamed x168, local copies, waits for them, and re-layouts  37.3 us
    pallas_call x1, Pallas kernels, attend_back(): pl.pallas_call(functools.partial(attend_back_kernel, block), out_shape=ja...  35.7 us
  transfers between devices with their start and end apart: 13, of which 3 were waited for; matrix products, arithmetic and copies ran while one was open for 23% of the time, Pallas kernels for 57%

profile of v1, /device:TPU:9, one launch (start us, length us, event | category | flops | bytes accessed | tf_op | source)
XLA Modules:
  0.0 797.2 jit_solution(9059907454160552639)
XLA Ops:
  16.4 58.5 %swap_band.2 = (bf16[8,32,2048]{2,1,0:T(8,128)(2,1)}, s32[8,4,256]{2,1,0:T(4,128)}) custom-call(bf16[8,32,2048]{2,1,0:T(8,128)(2,1)} %bitcast.163, s32[4,256]{1,0:T(4,128)} %refs_1_.1), custom_call_target="tpu_custom_call" | custom-call | flops 30000001024 | bytes 60000000 | tf_op jit(solution)/shard_map/swap_band/pallas_call | solution.py:360
  87.0 37.5 %gather_tp.4 = bf16[4,256,2048]{2,1,0:T(8,128)(2,1)} custom-call(bf16[256,2048]{1,0:T(8,128)(2,1)} %fusion.31.refs_0_), custom_call_target="tpu_custom_call" | custom-call | flops 35999997952 | bytes 72000000 | tf_op jit(solution)/shard_map/gather_tp/pallas_call | solution.py:177
  130.5 8.5 %project.1.x_ref = bf16[2,1024,768]{2,1,0:T(8,128)(2,1)S(1)} custom-call(bf16[1024,2048]{1,0:T(8,128)(2,1)S(1)} %bitcast.147, bf16[2048,1536]{1,0:T(8,128)(2,1)S(1)} %copy-done.7, f32[1,1536]{1,0:T(1,128)S(1)} %broadcast_in_dim_reshape.2.bias_ref, f32[1,1536]{1,0:T(1,128)S(1)} %copy-done.12), custom_call_target="tpu_custom_call" | custom-call | flops 6442450944 | bytes 12582912 | tf_op jit(solution)/shard_map/project/pallas_call | solution.py:429
  144.9 10.6 %fusion.14.q_ref.k_ref.v_ref = bf16[2048,768]{1,0:T(8,128)(2,1)} fusion(bf16[2048,768]{1,0:T(8,128)(2,1)} %bitcast.199, s32[2048]{0:T(1024)S(1)} %eq.28), kind=kOutput, calls=%fused_computation.28 | convolution fusion | flops 6448218112 | bytes 6299648 | tf_op jit(solution)/shard_map/dot_general | solution.py:38
  158.4 4.9 all-to-all-start.1
  165.5 31.6 %attend.1 = (bf16[2048,256]{1,0:T(8,128)(2,1)S(1)}, f32[2,8,2048]{2,1,0:T(8,128)S(1)}) custom-call(s32[9]{0:T(128)S(1)} %pad_add_fusion.info_ref, s32[1,2048]{1,0:T(1,128)S(1)} %bitcast.145, bf16[2048,768]{1,0:T(8,128)(2,1)S(1)} %copy-done.16, bf16[2048,768]{1,0:T(8,128)(2,1)S(1)} %copy-done.16, bf16[2048,768]{1,0:T(8,128)(2,1)S(1)} %copy-done.16), custom_call_target="tpu_custom_call" | custom-call | flops 35999997952 | bytes 72000000 | tf_op jit(solution)/shard_map/attend/pallas_call | solution.py:599
  197.1 13.4 %all-to-all-done.1 = bf16[4,256,2048]{2,1,0:T(8,128)(2,1)} async-done(((bf16[4,256,2048]{2,1,0:T(8,128)(2,1)}), bf16[4,256,2048]{2,1,0:T(8,128)(2,1)}, u32[]{:S(2)}, u32[]{:S(2)}) %all-to-all-start.1) | async-done | bytes 4194336 | tf_op jit(solution)/shard_map/all_to_all | solution.py:317
  223.4 36.3 %scatter_tp.3 = f32[256,2048]{1,0:T(8,128)S(1)} custom-call(bf16[4,256,2048]{2,1,0:T(8,128)(2,1)S(1)} %bitcast.151), custom_call_target="tpu_custom_call" | custom-call | flops 35999997952 | bytes 72000000 | tf_op jit(solution)/shard_map/scatter_tp/pallas_call | solution.py:293
  263.7 35.3 %gather_tp.5 = bf16[4,256,2048]{2,1,0:T(8,128)(2,1)} custom-call(bf16[256,2048]{1,0:T(8,128)(2,1)} %add_convert_fusion.refs_0_), custom_call_target="tpu_custom_call" | custom-call | flops 35999997952 | bytes 72000000 | tf_op jit(solution)/shard_map/gather_tp/pallas_call | solution.py:177
  299.0 15.9 %multiply_convert_fusion = (bf16[1024,2048]{1,0:T(8,128)(2,1)}, f32[1024,2048]{1,0:T(8,128)}) fusion(f32[2048]{0:T(1024)S(1)} %copy-done.70, bf16[1024,2048]{1,0:T(8,128)(2,1)} %bitcast.196, bf16[2048,2048]{1,0:T(8,128)(2,1)} %all-gather.11.cloned.1.call-done), kind=kOutput, calls=%fused_computation.13 | convolution fusion | flops 8602517504 | bytes 25174016 | tf_op jit(solution)/shard_map/dot_general | solution.py:38
  314.9 15.0 %convolution_convert_fusion.5 = bf16[1024,2048]{1,0:T(8,128)(2,1)} fusion(bf16[1024,2048]{1,0:T(8,128)(2,1)} %get-tuple-element.59, bf16[2048,2048]{0,1:T(8,128)(2,1)} %all-gather.9.cloned.1.call-done), kind=kOutput, calls=%fused_computation.25 | convolution fusion | flops 8592031744 | bytes 16777216 | tf_op jit(solution)/shard_map/dot_general | solution.py:42
  330.0 13.5 %convolution_convert_fusion.2 = bf16[2048,2048]{1,0:T(8,128)(2,1)} fusion(bf16[1024,2048]{1,0:T(8,128)(2,1)} %bitcast.24, bf16[1024,2048]{1,0:T(8,128)(2,1)S(1)} %copy-done.73), kind=kOutput, calls=%fused_computation.22 | convolution fusion | flops 8594128896 | bytes 16777216 | tf_op jit(solution)/shard_map/dot_general | solution.py:46
  343.5 17.2 %multiply_convert_fusion.1 = bf16[1024,2048]{1,0:T(8,128)(2,1)} fusion(bf16[1024,2048]{1,0:T(8,128)(2,1)} %bitcast.24, bf16[2048,2048]{0,1:T(8,128)(2,1)} %all-gather.9.cloned.1.call-done, f32[1024,2048]{1,0:T(8,128)} %get-tuple-element.213, f32[2048]{0:T(1024)S(1)} %copy-done.70), kind=kOutput, calls=%fused_computation.14 | convolution fusion | flops 8617197568 | bytes 25174016 | tf_op jit(solution)/shard_map/dot_general | solution.py:38
  360.7 5.2 all-to-all-start.2
  366.0 14.9 %convolution_convert_fusion.4 = bf16[1024,2048]{1,0:T(8,128)(2,1)} fusion(bf16[1024,2048]{1,0:T(8,128)(2,1)} %multiply_convert_fusion.1, bf16[2048,2048]{1,0:T(8,128)(2,1)} %all-gather.11.cloned.1.call-done), kind=kOutput, calls=%fused_computation.24 | convolution fusion | flops 8592031744 | bytes 16777216 | tf_op jit(solution)/shard_map/dot_general | solution.py:42
  380.9 11.4 %convolution_convert_fusion.1 = bf16[2048,2048]{1,0:T(8,128)(2,1)} fusion(bf16[1024,2048]{1,0:T(8,128)(2,1)S(1)} %bitcast.197, bf16[1024,2048]{1,0:T(8,128)(2,1)S(1)} %copy-done.28), kind=kOutput, calls=%fused_computation.21 | convolution fusion | flops 8594128896 | bytes 16777216 | tf_op jit(solution)/shard_map/dot_general | solution.py:46
  392.3 20.5 %all-to-all-done.2 = bf16[4,256,2048]{2,1,0:T(8,128)(2,1)} async-done(((bf16[4,256,2048]{2,1,0:T(8,128)(2,1)}), bf16[4,256,2048]{2,1,0:T(8,128)(2,1)}, u32[]{:S(2)}, u32[]{:S(2)}) %all-to-all-start.2) | async-done | bytes 4194336 | tf_op jit(solution)/shard_map/all_to_all | solution.py:741
  418.0 7.2 all-to-all-start.3
  427.4 36.3 %scatter_tp.4 = f32[256,2048]{1,0:T(8,128)S(1)} custom-call(bf16[4,256,2048]{2,1,0:T(8,128)(2,1)S(1)} %bitcast.149), custom_call_target="tpu_custom_call" | custom-call | flops 35999997952 | bytes 72000000 | tf_op jit(solution)/shard_map/scatter_tp/pallas_call | solution.py:293
  467.8 35.3 %gather_tp.6 = bf16[4,256,2048]{2,1,0:T(8,128)(2,1)} custom-call(bf16[256,2048]{1,0:T(8,128)(2,1)} %get-tuple-element.196.refs_0_), custom_call_target="tpu_custom_call" | custom-call | flops 35999997952 | bytes 72000000 | tf_op jit(solution)/shard_map/gather_tp/pallas_call | solution.py:177
  508.8 5.5 convolution_convert_fusion.8
  531.2 5.0 all-to-all-start.4
  538.2 35.7 %attend_back.1 = bf16[2048,768]{1,0:T(8,128)(2,1)S(1)} custom-call(s32[9]{0:T(128)S(1)} %pad_add_fusion.info_ref, s32[1,2048]{1,0:T(1,128)S(1)} %bitcast.146, bf16[2048,768]{1,0:T(8,128)(2,1)S(1)} %copy-done.17, bf16[2048,768]{1,0:T(8,128)(2,1)S(1)} %copy-done.17, bf16[2048,768]{1,0:T(8,128)(2,1)S(1)} %copy-done.17, bf16[2048,256]{1,0:T(8,128)(2,1)S(1)} %copy-done.15, ...), custom_call_target="tpu_custom_call" | custom-call | flops 40000000000 | bytes 80000000 | tf_op jit(solution)/shard_map/attend_back/pallas_call | solution.py:621
  575.6 7.7 all-to-all-done.4
  583.3 10.6 %fusion.13 = bf16[2048,768]{1,0:T(8,128)(2,1)} fusion(bf16[2048,768]{1,0:T(8,128)(2,1)} %copy-done.18, s32[2048]{0:T(1024)S(1)} %copy-done.67), kind=kOutput, calls=%fused_computation.27 | convolution fusion | flops 6448218112 | bytes 6299648 | tf_op jit(solution)/shard_map/dot_general | solution.py:38
  600.9 4.9 copy.111
  609.1 11.3 %convolution_convert_fusion.3 = bf16[1024,2048]{1,0:T(8,128)(2,1)} fusion(bf16[1024,1536]{0,1:T(8,128)(2,1)} %bitcast.157, bf16[2048,1536]{1,0:T(8,128)(2,1)} %all-gather.5.cloned.1.call-done.w_ref), kind=kOutput, calls=%fused_computation.23 | convolution fusion | flops 6444548096 | bytes 13631488 | tf_op jit(solution)/shard_map/dot_general | solution.py:42
  620.4 9.1 %convolution_convert_fusion = bf16[2048,1536]{1,0:T(8,128)(2,1)} fusion(bf16[1024,2048]{1,0:T(8,128)(2,1)S(1)} %bitcast.148, bf16[1024,1536]{0,1:T(8,128)(2,1)S(1)} %bitcast.158), kind=kOutput, calls=%fused_computation.20 | convolution fusion | flops 6445596672 | bytes 13631488 | tf_op jit(solution)/shard_map/dot_general | solution.py:46
  631.7 34.0 %scatter_tp.5 = f32[256,2048]{1,0:T(8,128)S(1)} custom-call(bf16[4,256,2048]{2,1,0:T(8,128)(2,1)S(1)} %bitcast.150), custom_call_target="tpu_custom_call" | custom-call | flops 35999997952 | bytes 72000000 | tf_op jit(solution)/shard_map/scatter_tp/pallas_call | solution.py:293
  680.3 50.7 %swap_band.3 = (bf16[8,32,2048]{2,1,0:T(8,128)(2,1)}, bf16[8,16,1024]{2,1,0:T(8,128)(2,1)}) custom-call(bf16[8,32,2048]{2,1,0:T(8,128)(2,1)} %bitcast.173, bf16[16,1024]{1,0:T(8,128)(2,1)} %reshape.309.refs_1_), custom_call_target="tpu_custom_call" | custom-call | flops 30000001024 | bytes 60000000 | tf_op jit(solution)/shard_map/swap_band/pallas_call | solution.py:360
  733.3 39.2 %gather_tp.7 = (bf16[8,4,32,2048]{3,2,1,0:T(8,128)(2,1)}, f32[6,2048]{1,0:T(8,128)}) custom-call(bf16[8,32,2048]{2,1,0:T(8,128)(2,1)} %get-tuple-element.70.refs_0_, f32[6,2048]{1,0:T(8,128)} %reshape.310.refs_1_), custom_call_target="tpu_custom_call" | custom-call | flops 35999997952 | bytes 72000000 | tf_op jit(solution)/shard_map/gather_tp/pallas_call | solution.py:177
  772.6 6.7 convert.52
  (270 shorter events, 131.6 us)
Async XLA Ops:
  7.2 74.3 %copy-start = (s32[4,4]{1,0:T(4,128)S(1)}, s32[4,4]{1,0:T(4,128)}, u32[]{:S(2)}) copy-start(s32[4,4]{1,0:T(4,128)} %param.22) | copy-start | bytes 196
  7.2 118.1 %all-gather.5.cloned.1.call-start = ((), (), s32[]{:S(2)}) async-start(), calls=%async_computation.9 | async-start | bytes 7077888 | tf_op jit(solution)/shard_map/all_gather | solution.py:679
  11.8 207.2 %all-gather.7.cloned.1.call-start = ((), (), s32[]{:S(2)}) async-start(), calls=%async_computation.10 | async-start | bytes 2359296 | tf_op jit(solution)/shard_map/all_gather | solution.py:680
  12.6 286.4 %all-gather.11.cloned.1.call-start = ((), (), s32[]{:S(2)}) async-start(), calls=%async_computation.12 | async-start | bytes 9437184 | tf_op jit(solution)/shard_map/all_gather | solution.py:681
  75.0 80.5 %all-to-all-start = ((bf16[8,32,2048]{2,1,0:T(8,128)(2,1)}), bf16[8,32,2048]{2,1,0:T(8,128)(2,1)S(1)}, u32[]{:S(2)}, u32[]{:S(2)}) async-start(bf16[8,32,2048]{2,1,0:T(8,128)(2,1)} %bitcast.8), calls=%async_computation | async-start | bytes 2097152 | tf_op jit(solution)/shard_map/all_to_all | solution.py:690
  78.7 236.2 %all-gather.9.cloned.1.call-start = ((), (), s32[]{:S(2)}) async-start(), calls=%async_computation.11 | async-start | bytes 9437184 | tf_op jit(solution)/shard_map/all_gather | solution.py:682
  79.6 45.0 %copy-start.53 = (f32[256]{0:T(256)}, f32[256]{0:T(256)S(1)}, u32[]{:S(2)}) copy-start(f32[256]{0:T(256)S(1)} %div.54) | copy-start | bytes 3076
  82.9 41.7 %copy-start.55 = (f32[256]{0:T(256)}, f32[256]{0:T(256)S(1)}, u32[]{:S(2)}) copy-start(f32[256]{0:T(256)S(1)} %rsqrt.20) | copy-start | bytes 3076
  85.5 70.1 %copy-start.57 = (f32[256]{0:T(256)}, f32[256]{0:T(256)S(1)}, u32[]{:S(2)}) copy-start(f32[256]{0:T(256)S(1)} %reshape.314) | copy-start | bytes 3076
  85.6 125.0 %copy-start.66 = (s32[2048]{0:T(1024)}, s32[2048]{0:T(1024)S(1)}, u32[]{:S(2)}) copy-start(s32[2048]{0:T(1024)S(1)} %eq.28) | copy-start | bytes 24580
  87.0 38.3 %copy-start.12 = (f32[1,1536]{1,0:T(1,128)S(1)}, f32[1,1536]{1,0:T(1,128)}, u32[]{:S(2)}) copy-start(f32[1,1536]{1,0:T(1,128)} %constant.114.clone.1.scale_ref) | copy-start | bytes 18436
  158.4 52.2 %all-to-all-start.1 = ((bf16[4,256,2048]{2,1,0:T(8,128)(2,1)}), bf16[4,256,2048]{2,1,0:T(8,128)(2,1)}, u32[]{:S(2)}, u32[]{:S(2)}) async-start(bf16[4,256,2048]{2,1,0:T(8,128)(2,1)} %broadcast_in_dim.21), calls=%async_computation.1 | async-start | bytes 8388608 | tf_op jit(solution)/shard_map/all_to_all | solution.py:317
  163.4 339.8 %reduce-scatter.5.cloned.1.call-start = ((), (), s32[]{:S(2)}) async-start(), calls=%async_computation.13 | async-start | bytes 9437184 | tf_op jit(solution)/shard_map/reduce_scatter | solution.py:677
  197.1 17.3 %copy-start.14 = (bf16[2048,256]{1,0:T(8,128)(2,1)}, bf16[2048,256]{1,0:T(8,128)(2,1)S(1)}, u32[]{:S(2)}) copy-start(bf16[2048,256]{1,0:T(8,128)(2,1)S(1)} %get-tuple-element.57.o_ref) | copy-start | bytes 3145732
  223.4 36.3 %copy-start.22 = (bf16[8,32,2048]{2,1,0:T(8,128)(2,1)S(1)}, bf16[8,32,2048]{2,1,0:T(8,128)(2,1)}, u32[]{:S(2)}) copy-start(bf16[8,32,2048]{2,1,0:T(8,128)(2,1)} %get-tuple-element.52) | copy-start | bytes 3145732
  223.4 36.3 %copy-start.44 = (f32[2048]{0:T(1024)S(1)}, f32[2048]{0:T(1024)}, u32[]{:S(2)}) copy-start(f32[2048]{0:T(1024)} %param.32) | copy-start | bytes 24580
  263.7 35.3 %copy-start.70 = (f32[2048]{0:T(1024)S(1)}, f32[2048]{0:T(1024)}, u32[]{:S(2)}) copy-start(f32[2048]{0:T(1024)} %param.33) | copy-start | bytes 24580
  314.9 15.0 %copy-start.73 = (bf16[1024,2048]{1,0:T(8,128)(2,1)S(1)}, bf16[1024,2048]{1,0:T(8,128)(2,1)}, u32[]{:S(2)}) copy-start(bf16[1024,2048]{1,0:T(8,128)(2,1)} %get-tuple-element.59) | copy-start | bytes 12582916
  360.7 52.1 %all-to-all-start.2 = ((bf16[4,256,2048]{2,1,0:T(8,128)(2,1)}), bf16[4,256,2048]{2,1,0:T(8,128)(2,1)}, u32[]{:S(2)}, u32[]{:S(2)}) async-start(bf16[4,256,2048]{2,1,0:T(8,128)(2,1)} %bitcast.156), calls=%async_computation.2 | async-start | bytes 8388608 | tf_op jit(solution)/shard_map/all_to_all | solution.py:741
  418.0 85.2 %all-to-all-start.3 = ((bf16[8,32,2048]{2,1,0:T(8,128)(2,1)}), bf16[8,32,2048]{2,1,0:T(8,128)(2,1)S(1)}, u32[]{:S(2)}, u32[]{:S(2)}) async-start(bf16[8,32,2048]{2,1,0:T(8,128)(2,1)} %bitcast.30), calls=%async_computation.3 | async-start | bytes 2097152 | tf_op jit(solution)/shard_map/all_to_all | solution.py:751
  425.2 173.3 %reduce-scatter.7.cloned.1.call-start = ((), (), s32[]{:S(2)}) async-start(), calls=%async_computation.14 | async-start | bytes 9437184 | tf_op jit(solution)/shard_map/reduce_scatter | solution.py:677
  427.4 36.3 %copy-start.20 = (f32[256,2048]{1,0:T(8,128)S(1)}, f32[256,2048]{1,0:T(8,128)}, u32[]{:S(2)}) copy-start(f32[256,2048]{1,0:T(8,128)} %copy-done.19) | copy-start | bytes 6291460
  427.4 36.3 %copy-start.36 = (f32[2048]{0:T(1024)S(1)}, f32[2048]{0:T(1024)}, u32[]{:S(2)}) copy-start(f32[2048]{0:T(1024)} %param.37) | copy-start | bytes 24580
  427.4 36.3 %copy-start.42 = (f32[256]{0:T(256)S(1)}, f32[256]{0:T(256)}, u32[]{:S(2)}) copy-start(f32[256]{0:T(256)} %copy-done.41) | copy-start | bytes 3076
  427.4 36.3 %copy-start.47 = (f32[256]{0:T(256)S(1)}, f32[256]{0:T(256)}, u32[]{:S(2)}) copy-start(f32[256]{0:T(256)} %copy-done.46) | copy-start | bytes 3076
  531.2 52.1 %all-to-all-start.4 = ((bf16[4,8,32,2048]{3,2,1,0:T(8,128)(2,1)}), bf16[4,8,32,2048]{3,2,1,0:T(8,128)(2,1)}, u32[]{:S(2)}, u32[]{:S(2)}) async-start(bf16[4,8,32,2048]{3,2,1,0:T(8,128)(2,1)} %broadcast_in_dim.22), calls=%async_computation.4 | async-start | bytes 8388608 | tf_op jit(solution)/shard_map/all_to_all | solution.py:317
  536.2 93.3 %reduce-scatter.9.cloned.1.call-start = ((), (), s32[]{:S(2)}) async-start(), calls=%async_computation.15 | async-start | bytes 2359296 | tf_op jit(solution)/shard_map/reduce_scatter | solution.py:677
  598.5 186.8 %reduce-scatter.11.cloned.1.call-start = ((), (), s32[]{:S(2)}) async-start(), calls=%async_computation.16 | async-start | bytes 7077888 | tf_op jit(solution)/shard_map/reduce_scatter | solution.py:677
  631.7 35.4 %copy-start.24 = (bf16[8,32,2048]{2,1,0:T(8,128)(2,1)S(1)}, bf16[8,32,2048]{2,1,0:T(8,128)(2,1)}, u32[]{:S(2)}) copy-start(bf16[8,32,2048]{2,1,0:T(8,128)(2,1)} %get-tuple-element.52) | copy-start | bytes 3145732
  631.7 35.4 %copy-start.39 = (f32[2048]{0:T(1024)S(1)}, f32[2048]{0:T(1024)}, u32[]{:S(2)}) copy-start(f32[2048]{0:T(1024)} %param.35) | copy-start | bytes 24580
  631.7 35.4 %copy-start.54 = (f32[256]{0:T(256)S(1)}, f32[256]{0:T(256)}, u32[]{:S(2)}) copy-start(f32[256]{0:T(256)} %copy-done.53) | copy-start | bytes 3076
  631.7 35.4 %copy-start.56 = (f32[256]{0:T(256)S(1)}, f32[256]{0:T(256)}, u32[]{:S(2)}) copy-start(f32[256]{0:T(256)} %copy-done.55) | copy-start | bytes 3076
  (55 other events, 265.5 us)
Sparse Core Ops, SparseCore 0:
  11.9 103.7 all-gather.4
  117.3 36.2 all-gather.6
  155.2 76.6 all-gather.10
  233.4 80.6 all-gather.8
  360.8 111.7 reduce-scatter.4
  503.4 89.3 reduce-scatter.6
  598.6 30.1 reduce-scatter.8
  631.1 98.7 reduce-scatter.10

commit v2 on v1

v2 whole, which is shorter than its diff:
```python
import functools
import math

import jax
import jax.numpy as jnp
from jax import lax
from jax.experimental import pallas as pl
from jax.experimental.pallas import tpu as pltpu
from jax.sharding import PartitionSpec as P

HEAD_DIM = 64
LAYER = 12
MESH = pl.DeviceIdType.MESH

epsilon = 1e-05
masked_score = -1e30
bf16 = jnp.bfloat16
f32 = jnp.float32


def layer_norm(values, gain, shift):
    center = values - jnp.mean(values, axis=-1, keepdims=True)
    inverse = lax.rsqrt(jnp.mean(center * center, axis=-1, keepdims=True) + epsilon)
    normed = center * inverse
    return (normed * gain + shift, normed, inverse)


def norm_back(grad_out, normed, inverse, gain):
    scaled = grad_out * gain
    return inverse * (
        scaled
        - jnp.mean(scaled, axis=-1, keepdims=True)
        - normed * jnp.mean(scaled * normed, axis=-1, keepdims=True)
    )


def nn(left, right):
    return jnp.dot(left, right, preferred_element_type=f32)


def nt(left, right):
    return lax.dot_general(left, right, (((1,), (1,)), ((), ())), preferred_element_type=f32)


def tn(left, right):
    return lax.dot_general(left, right, (((0,), (0,)), ((), ())), preferred_element_type=f32)


def gelu_exact(values):
    return jax.nn.gelu(values, approximate=False)


def halves(count):
    return (count // 2, 2) if count % 2 == 0 else (count, 1)


def takes(microseconds):
    return pl.CostEstimate(
        flops=int(microseconds * 1e9), bytes_accessed=int(microseconds * 2e6), transcendentals=0
    )


class Sems:
    def __init__(self, send_sem, recv_sem, local_sem):
        self.send_sem, self.recv_sem, self.local_sem = send_sem, recv_sem, local_sem
        self.sent = self.local = 0

    def send(self, source, target, device):
        k = self.sent
        self.sent += 1
        copy = pltpu.make_async_remote_copy(
            source, target, self.send_sem.at[k], self.recv_sem.at[k],
            device_id=device, device_id_type=MESH,
        )
        copy.start()
        return copy

    def copy(self, source, target):
        k = self.local
        self.local += 1
        copy = pltpu.make_async_copy(source, target, self.local_sem.at[k])
        copy.start()
        return copy


class Grid:
    def __init__(self, count):
        self.na, self.nb = na, nb = halves(count)
        self.me, band = lax.axis_index("tp"), lax.axis_index("band")
        self.a, self.b = a, b = self.me // nb, lax.rem(self.me, nb)
        self.along_b = [(band, a * nb + lax.rem(b + d, nb)) for d in range(1, nb)]
        self.along_a = [(band, lax.rem(a + d, na) * nb + b) for d in range(1, na)]
        self.from_b = [a * nb + lax.rem(b + nb - d, nb) for d in range(1, nb)]
        self.from_a = [lax.rem(a + na - d, na) * nb + b for d in range(1, na)]


def tp_peers():
    grid = Grid(lax.axis_size("tp"))
    return grid.along_a + grid.along_b


def band_peers():
    size = lax.axis_size("band")
    me, tp = lax.axis_index("band"), lax.axis_index("tp")
    return [(lax.rem(me + d, size), tp) for d in range(1, size)]


anywhere = pl.BlockSpec(memory_space=pl.ANY)
vmem = pl.BlockSpec(memory_space=pltpu.VMEM)


class Gather:
    peers = "tp"

    def __init__(self, x, inner_slot=False, extra=None):
        self.count = count = lax.axis_size("tp")
        na, nb = halves(count)
        self.inner_slot, self.extra = inner_slot, extra is not None
        self.sends = 2 * (na - 1 + nb - 1) + 2 * (na - 1) * (nb - 1)
        self.locals = 2
        shape = (x.shape[0], count) + x.shape[1:] if inner_slot else (count,) + x.shape
        self.operands, self.in_specs = [x], [anywhere]
        self.shapes, self.out_specs = [jax.ShapeDtypeStruct(shape, x.dtype)], [anywhere]
        self.scratch = [pltpu.VMEM(x.shape, x.dtype)]
        if self.extra:
            self.operands.append(extra)
            self.in_specs.append(vmem)
            self.shapes.append(jax.ShapeDtypeStruct(extra.shape, extra.dtype))
            self.out_specs.append(vmem)
            self.sends += na - 1 + nb - 1
            self.scratch += [
                pltpu.VMEM(extra.shape, extra.dtype),
                pltpu.VMEM((max(nb - 1, 1),) + extra.shape, extra.dtype),
                pltpu.VMEM((max(na - 1, 1),) + extra.shape, extra.dtype),
            ]

    def slot(self, index, which):
        part = self.part[which]
        return self.out.at[part, index] if self.inner_slot else self.out.at[index, part]

    def begin(self, ins, outs, scratch, sems):
        self.grid = grid = Grid(self.count)
        self.sems = sems
        x, self.out = ins[0], outs[0]
        half = x.shape[0] // 2
        self.part = part = (pl.ds(0, half), pl.ds(half, half))
        self.through = scratch[0]
        self.load = sems.copy(x, self.through)
        me = grid.me
        if self.extra:
            self.more = (ins[1], outs[1], *scratch[1:])
            self.extra_b = [
                sems.send(ins[1], scratch[2].at[k], device) for k, device in enumerate(grid.along_b)
            ]
        top, low = x.at[part[0]], x.at[part[1]]
        self.first_b = [sems.send(top, self.slot(me, 0), device) for device in grid.along_b]
        self.first_a = [sems.send(low, self.slot(me, 1), device) for device in grid.along_a]
        self.second = [sems.send(top, self.slot(me, 0), device) for device in grid.along_a]
        self.second += [sems.send(low, self.slot(me, 1), device) for device in grid.along_b]

    def middle(self):
        grid, sems = self.grid, self.sems
        self.load.wait()
        whole = self.out.at[:, grid.me] if self.inner_slot else self.out.at[grid.me]
        self.store = sems.copy(self.through, whole)
        if self.extra:
            own, _, part_ref, in_b, in_a = self.more
            total = own[...]
            for k, copy in enumerate(self.extra_b):
                copy.wait_recv()
                total = total + in_b[k]
            part_ref[...] = total
            self.extra_a = [
                sems.send(part_ref, in_a.at[k], device) for k, device in enumerate(grid.along_a)
            ]
        for copy, source in zip(self.first_b, grid.from_b):
            copy.wait_recv()
            held = self.slot(source, 0)
            self.second += [sems.send(held, held, device) for device in grid.along_a]
        for copy, source in zip(self.first_a, grid.from_a):
            copy.wait_recv()
            held = self.slot(source, 1)
            self.second += [sems.send(held, held, device) for device in grid.along_b]

    def end(self):
        if self.extra:
            _, total_ref, part_ref, _, in_a = self.more
            total = part_ref[...]
            for k, copy in enumerate(self.extra_a):
                copy.wait_recv()
                total = total + in_a[k]
            total_ref[...] = total
            for copy in self.extra_a + self.extra_b:
                copy.wait_send()
        for copy in self.first_a + self.first_b:
            copy.wait_send()
        for copy in self.second:
            copy.wait()
        self.store.wait()


class Scatter:
    peers = "tp"

    def __init__(self, partial):
        self.count, rows, width = partial.shape
        na, nb = halves(self.count)
        block = (rows // 2, width)
        self.sends = 2 * (na - 1) * (nb - 1) + 2 * (na - 1 + nb - 1)
        self.locals = na + nb
        self.operands, self.in_specs = [partial], [anywhere]
        self.shapes, self.out_specs = [jax.ShapeDtypeStruct((rows, width), f32)], [vmem]

        def buffer(*lead):
            return pltpu.VMEM(tuple(max(n, 1) for n in lead) + block, partial.dtype)

        self.scratch = [
            buffer(na), buffer(nb), buffer(nb - 1, na), buffer(na - 1, nb),
            buffer(na - 1), buffer(nb - 1), buffer(na - 1), buffer(nb - 1),
        ]

    def begin(self, ins, outs, scratch, sems):
        self.grid = grid = Grid(self.count)
        self.sems, self.out, self.scratch_refs = sems, outs[0], scratch
        own_a, own_b, one_a, one_b = scratch[:4]
        part = ins[0]
        na, nb, a, b = grid.na, grid.nb, grid.a, grid.b
        half = part.shape[1] // 2
        self.top, self.low = top, low = pl.ds(0, half), pl.ds(half, half)
        self.order_a = order_a = list(range(1, na)) + [0]
        self.order_b = order_b = list(range(1, nb)) + [0]
        self.first_a, self.first_b = {}, {}
        for step in range(max(na, nb)):
            if step < na:
                e = order_a[step]
                row = lax.rem(a + e, na) * nb
                for d in range(1, nb):
                    source = part.at[row + lax.rem(b + d, nb), top]
                    self.first_b[d, e] = sems.send(source, one_a.at[d - 1, e], grid.along_b[d - 1])
            if step < nb:
                e = order_b[step]
                column = lax.rem(b + e, nb)
                for d in range(1, na):
                    source = part.at[lax.rem(a + d, na) * nb + column, low]
                    self.first_a[d, e] = sems.send(source, one_b.at[d - 1, e], grid.along_a[d - 1])
        self.local_a = {
            e: sems.copy(part.at[lax.rem(a + e, na) * nb + b, top], own_a.at[e]) for e in order_a
        }
        self.local_b = {
            e: sems.copy(part.at[a * nb + lax.rem(b + e, nb), low], own_b.at[e]) for e in order_b
        }

    def sum_a(self, e):
        own_a, _, one_a = self.scratch_refs[:3]
        self.local_a[e].wait()
        total = own_a[e].astype(f32)
        for d in range(1, self.grid.nb):
            self.first_b[d, e].wait_recv()
            total = total + one_a[d - 1, e].astype(f32)
        return total

    def sum_b(self, e):
        _, own_b, _, one_b = self.scratch_refs[:4]
        self.local_b[e].wait()
        total = own_b[e].astype(f32)
        for d in range(1, self.grid.na):
            self.first_a[d, e].wait_recv()
            total = total + one_b[d - 1, e].astype(f32)
        return total

    def middle(self):
        grid, sems = self.grid, self.sems
        out_a, out_b, two_a, two_b = self.scratch_refs[4:]
        self.second_a, self.second_b = {}, {}
        for e in self.order_a[:-1]:
            out_a[e - 1] = self.sum_a(e).astype(out_a.dtype)
            self.second_a[e] = sems.send(out_a.at[e - 1], two_a.at[e - 1], grid.along_a[e - 1])
        for e in self.order_b[:-1]:
            out_b[e - 1] = self.sum_b(e).astype(out_b.dtype)
            self.second_b[e] = sems.send(out_b.at[e - 1], two_b.at[e - 1], grid.along_b[e - 1])

    def end(self):
        _, _, two_a, two_b = self.scratch_refs[4:]
        total = self.sum_a(0)
        for e in self.order_a[:-1]:
            self.second_a[e].wait_recv()
            total = total + two_a[e - 1].astype(f32)
        self.out[self.top] = total
        total = self.sum_b(0)
        for e in self.order_b[:-1]:
            self.second_b[e].wait_recv()
            total = total + two_b[e - 1].astype(f32)
        self.out[self.low] = total
        for group in (self.first_a, self.first_b, self.second_a, self.second_b):
            for copy in group.values():
                copy.wait_send()


class Swap:
    peers = "band"

    def __init__(self, x, extra=None):
        size = lax.axis_size("band")
        arrays = [x] if extra is None else [x, extra]
        self.operands, self.in_specs = arrays, [anywhere] * len(arrays)
        self.shapes = [jax.ShapeDtypeStruct(x.shape, x.dtype)]
        self.scratch = [pltpu.VMEM(x.shape[1:], x.dtype)]
        if extra is not None:
            self.shapes.append(jax.ShapeDtypeStruct((size,) + extra.shape, extra.dtype))
            self.scratch.append(pltpu.VMEM(extra.shape, extra.dtype))
        self.out_specs = [anywhere] * len(arrays)
        self.sends = (size - 1) * len(arrays)
        self.locals = 2 * len(arrays)

    def begin(self, ins, outs, scratch, sems):
        me = lax.axis_index("band")
        self.sems, self.scratch_refs = sems, scratch
        self.slots = [out.at[me] for out in outs]
        self.loads = [sems.copy(ins[0].at[me], scratch[0])]
        if len(ins) > 1:
            self.loads.append(sems.copy(ins[1], scratch[1]))
        self.copies = []
        for peer in band_peers():
            if len(ins) > 1:
                self.copies.append(sems.send(ins[1], self.slots[1], peer))
            self.copies.append(sems.send(ins[0].at[peer[0]], self.slots[0], peer))

    def middle(self):
        self.stores = []
        for load, through, slot in zip(self.loads, self.scratch_refs, self.slots):
            load.wait()
            self.stores.append(self.sems.copy(through, slot))

    def end(self):
        for copy in self.copies + self.stores:
            copy.wait()


class Work:
    def __init__(self, operands, tasks, early):
        self.tasks, self.early = tasks, early
        self.operands = operands
        self.shapes = []
        for kind, left, right, _, _ in tasks:
            if kind == "sum":
                self.shapes.append(jax.ShapeDtypeStruct((1, operands[left].shape[1]), f32))
                continue
            rows = operands[left].shape[1 if kind == "tn" else 0]
            self.shapes.append(jax.ShapeDtypeStruct((rows, operands[right].shape[1]), bf16))
        self.scratch = [pltpu.VMEM(x.shape, x.dtype) for x in [*operands, *self.shapes]]
        self.locals = len(operands) + len(tasks)

    def begin(self, ins, outs, scratch, sems):
        self.sems, self.outs = sems, outs
        self.held, self.made = scratch[: len(ins)], scratch[len(ins) :]
        self.loads = [sems.copy(source, target) for source, target in zip(ins, self.held)]
        self.stores = []

    def ready(self, k):
        if self.loads[k] is not None:
            self.loads[k].wait()
            self.loads[k] = None

    def run(self, tasks):
        for kind, left, right, scale, out in tasks:
            for k in (left, right, scale):
                if k is not None:
                    self.ready(k)
            x, made = self.held[left], self.made[out]
            if kind == "sum":
                rows = min(128, x.shape[0])
                made[...] = jnp.zeros_like(made)

                def add(k, _, x=x, made=made, rows=rows):
                    r = pl.ds(pl.multiple_of(k * rows, rows), rows)
                    made[...] += jnp.sum(x[r, :].astype(f32), axis=0, keepdims=True)
                    return 0

                lax.fori_loop(0, x.shape[0] // rows, add, 0)
                self.stores.append(self.sems.copy(made, self.outs[out]))
                continue
            y = self.held[right]
            factor = None if scale is None else self.held[scale]
            tile_r, tile_c = min(512, made.shape[0]), min(512, made.shape[1])
            columns = made.shape[1] // tile_c

            def tile(k, _, kind=kind, x=x, y=y, made=made, factor=factor):
                i, j = k // columns, lax.rem(k, columns)
                r = pl.ds(pl.multiple_of(i * tile_r, tile_r), tile_r)
                c = pl.ds(pl.multiple_of(j * tile_c, tile_c), tile_c)
                total = tn(x[:, r], y[:, c]) if kind == "tn" else nn(x[r, :], y[:, c])
                if factor is not None:
                    total = total * factor[r, c].astype(f32)
                made[r, c] = total.astype(made.dtype)
                return 0

            lax.fori_loop(0, (made.shape[0] // tile_r) * columns, tile, 0)
            self.stores.append(self.sems.copy(made, self.outs[out]))

    def end(self):
        for store in self.stores:
            store.wait()


def transfer(parts, cid, work=None, name="transfer", time=36):
    items = list(parts) + ([work] if work is not None else [])
    sends = sum(part.sends for part in parts)
    locals_ = sum(item.locals for item in items)

    def kernel(*refs):
        refs = list(refs)

        def take(number):
            taken = refs[:number]
            del refs[:number]
            return taken

        ins = [take(len(item.operands)) for item in items]
        outs = [take(len(item.shapes)) for item in items]
        scratch = [take(len(item.scratch)) for item in items]
        sems = Sems(*refs)
        devices = []
        if any(part.peers == "tp" for part in parts):
            devices += tp_peers()
        if any(part.peers == "band" for part in parts):
            devices += band_peers()
        barrier = pltpu.get_barrier_semaphore()
        for device in devices:
            pl.semaphore_signal(barrier, inc=1, device_id=device, device_id_type=MESH)
        if work is not None:
            work.begin(ins[-1], outs[-1], scratch[-1], sems)
        pl.semaphore_wait(barrier, len(devices))
        for part, i, o, t in zip(parts, ins, outs, scratch):
            part.begin(i, o, t, sems)
        if work is not None:
            work.run(work.tasks[: work.early])
        for part in parts:
            part.middle()
        if work is not None:
            work.run(work.tasks[work.early :])
        for part in parts:
            part.end()
        if work is not None:
            work.end()

    in_specs = [spec for part in parts for spec in part.in_specs]
    out_specs = [spec for part in parts for spec in part.out_specs]
    if work is not None:
        in_specs += [anywhere] * len(work.operands)
        out_specs += [anywhere] * len(work.shapes)
    return pl.pallas_call(
        kernel,
        out_shape=tuple(shape for item in items for shape in item.shapes),
        in_specs=in_specs,
        out_specs=tuple(out_specs),
        scratch_shapes=[
            *(scratch for item in items for scratch in item.scratch),
            pltpu.SemaphoreType.DMA((sends,)),
            pltpu.SemaphoreType.DMA((sends,)),
            pltpu.SemaphoreType.DMA((locals_,)),
        ],
        compiler_params=pltpu.CompilerParams(
            collective_id=cid, has_side_effects=True, vmem_limit_bytes=(56 if work else 32) * 2**20
        ),
        cost_estimate=takes(time),
        name=name,
    )(*(operand for item in items for operand in item.operands))


def gather_later(x):
    count = lax.axis_size("tp")
    return lax.all_to_all(jnp.broadcast_to(x[None], (count,) + x.shape), "tp", 0, 0)


class Block:
    def __init__(self, order, shift, grid, size):
        band = lax.axis_index("band")
        self.order, self.shift = order, shift
        self.to, self.source = lax.rem(band + shift, size), lax.rem(band + size - shift, size)
        if order % 2 == 0:
            self.n1, self.n2 = grid.nb, grid.na
            self.first, self.second, self.origin = grid.along_b, grid.along_a, grid.from_b
            self.index = lambda d, e: lax.rem(grid.a + e, grid.na) * grid.nb + lax.rem(
                grid.b + d, grid.nb
            )
        else:
            self.n1, self.n2 = grid.na, grid.nb
            self.first, self.second, self.origin = grid.along_a, grid.along_b, grid.from_a
            self.index = lambda d, e: lax.rem(grid.a + d, grid.na) * grid.nb + lax.rem(
                grid.b + e, grid.nb
            )


def finish_kernel(
    count, size, part, unit, above, resid, inverse, gain, wide, narrow,
    out, wide_out, narrow_out,
    own, one, two_out, two, made, arrived, late, late_in, wide_in, narrow_in, pair, pair_b, pair_a,
    send_sem, recv_sem, local_sem,
):
    grid = Grid(count)
    sems = Sems(send_sem, recv_sem, local_sem)
    band = lax.axis_index("band")
    peers = band_peers()
    devices = grid.along_a + grid.along_b + peers
    barrier = pltpu.get_barrier_semaphore()
    for device in devices:
        pl.semaphore_signal(barrier, inc=1, device_id=device, device_id_type=MESH)
    shifts = list(range(1, size)) + [0]
    blocks = [Block(k, shift, grid, size) for k, shift in enumerate(shifts)]
    late[...] = jnp.zeros_like(late)
    pl.semaphore_wait(barrier, len(devices))
    done = []

    for blk in blocks:
        k = blk.order
        seconds = list(range(1, blk.n2)) + [0]
        blk.one = {
            (d, e): sems.send(
                part.at[blk.index(d, e), blk.to], one.at[k, d - 1, e], blk.first[d - 1]
            )
            for e in seconds
            for d in range(1, blk.n1)
        }
        blk.own = {e: sems.copy(part.at[blk.index(0, e), blk.to], own.at[k, e]) for e in seconds}
    early = []
    for peer in peers:
        early.append(sems.send(wide, wide_in.at[band], peer))
        early.append(sems.send(narrow, narrow_in.at[band], peer))

    def first_sum(blk, e):
        k = blk.order
        blk.own[e].wait()
        total = own[k, e].astype(f32)
        for d in range(1, blk.n1):
            blk.one[d, e].wait_recv()
            total = total + one[k, d - 1, e].astype(f32)
        return total

    def pass_on(blk):
        k = blk.order
        blk.two = []
        for e in range(1, blk.n2):
            two_out[k, e - 1] = first_sum(blk, e).astype(bf16)
            blk.two.append(sems.send(two_out.at[k, e - 1], two.at[k, e - 1], blk.second[e - 1]))

    def complete(blk):
        k = blk.order
        grad = first_sum(blk, 0)
        for e, copy in enumerate(blk.two):
            copy.wait_recv()
            grad = grad + two[k, e].astype(f32)
        normed = unit[blk.to]
        scaled = grad * gain[...]
        mean = jnp.mean(scaled, axis=-1, keepdims=True)
        along = jnp.mean(scaled * normed, axis=-1, keepdims=True)
        base = above[blk.to].astype(f32) + resid[blk.to]
        token = base + inverse[blk.to] * (scaled - mean - normed * along)
        made[k] = token.astype(bf16)
        sums = (jnp.sum(grad * normed, axis=0, keepdims=True), jnp.sum(grad, axis=0, keepdims=True))
        quarter = late.shape[1]
        for which, total in enumerate(sums):
            for i in range(4):
                row = slice(4 * which + i, 4 * which + i + 1)
                late[row, :] = late[row, :] + total[:, i * quarter : (i + 1) * quarter]
        if blk.shift:
            blk.swap = sems.send(made.at[k], arrived.at[k], (blk.to, lax.axis_index("tp")))

    def relay(blk):
        k = blk.order
        if blk.shift:
            blk.swap.wait_recv()
            held = arrived.at[k]
        else:
            held = made.at[k]
        slot = out.at[blk.source, grid.me]
        blk.near = [sems.send(held, slot, device) for device in blk.first]
        blk.far = [sems.send(held, slot, device) for device in blk.second]
        done.append(sems.copy(held, slot))

    def forward(blk):
        for copy, source in zip(blk.near, blk.origin):
            copy.wait_recv()
            held = out.at[blk.source, source]
            blk.far += [sems.send(held, held, device) for device in blk.second]

    pairs = [blocks[k : k + 2] for k in range(0, size, 2)]
    stages = (pass_on, complete, relay, forward)
    for step in range(len(pairs) + len(stages) - 1):
        for behind, stage in enumerate(stages):
            if 0 <= step - behind < len(pairs):
                for blk in pairs[step - behind]:
                    stage(blk)
        if step == len(pairs):
            last = [sems.send(late, late_in.at[band], peer) for peer in peers]

    for copy in early + last:
        copy.wait_recv()
    wide_in[band] = wide[...]
    narrow_in[band] = narrow[...]
    late_in[band] = late[...]
    total, narrow_total, late_total = (
        sum(array[k].astype(f32) for k in range(size)) for array in (wide_in, narrow_in, late_in)
    )
    narrow_out[...] = narrow_total
    pair[0:16, :] = total
    pair[16:24, :] = late_total
    near = [sems.send(pair, pair_b.at[k], device) for k, device in enumerate(grid.along_b)]
    total = pair[...]
    for k, copy in enumerate(near):
        copy.wait_recv()
        total = total + pair_b[k]
    for copy in near:
        copy.wait_send()
    pair[...] = total
    far = [sems.send(pair, pair_a.at[k], device) for k, device in enumerate(grid.along_a)]
    for k, copy in enumerate(far):
        copy.wait_recv()
        total = total + pair_a[k]
    wide_out[...] = total

    for copy in early + last + far:
        copy.wait_send()
    for blk in blocks:
        for copy in [*blk.one.values(), *blk.two, *blk.near]:
            copy.wait_send()
        if blk.shift:
            blk.swap.wait_send()
        for copy in blk.far:
            copy.wait()
    for copy in done:
        copy.wait()


def finish(part, unit, above, resid, inverse, gain, wide, narrow, cid):
    count, size, rows, width = part.shape
    na, nb = halves(count)
    most = max(na, nb)
    sends = locals_ = 0
    for k in range(size):
        n1, n2 = (nb, na) if k % 2 == 0 else (na, nb)
        sends += (n1 - 1) * n2 + 2 * (n2 - 1) + (n1 - 1) + (n1 - 1) * (n2 - 1)
        locals_ += n2 + 1
    sends += 4 * (size - 1) + na - 1 + nb - 1
    lanes = wide.shape[1]

    def blocks(*lead):
        return pltpu.VMEM(tuple(max(n, 1) for n in lead) + (rows, width), bf16)

    return pl.pallas_call(
        functools.partial(finish_kernel, count, size),
        out_shape=(
            jax.ShapeDtypeStruct((size, count, rows, width), bf16),
            jax.ShapeDtypeStruct((24, lanes), f32),
            jax.ShapeDtypeStruct(narrow.shape, f32),
        ),
        in_specs=[anywhere] + [vmem] * 7,
        out_specs=(anywhere, vmem, vmem),
        scratch_shapes=[
            blocks(size, most), blocks(size, most - 1, most),
            blocks(size, most - 1), blocks(size, most - 1),
            blocks(size), blocks(size),
            pltpu.VMEM((8, lanes), f32),
            pltpu.VMEM((size, 8, lanes), f32),
            pltpu.VMEM((size,) + wide.shape, bf16),
            pltpu.VMEM((size,) + narrow.shape, bf16),
            pltpu.VMEM((24, lanes), f32),
            pltpu.VMEM((max(nb - 1, 1), 24, lanes), f32),
            pltpu.VMEM((max(na - 1, 1), 24, lanes), f32),
            pltpu.SemaphoreType.DMA((sends,)),
            pltpu.SemaphoreType.DMA((sends,)),
            pltpu.SemaphoreType.DMA((locals_,)),
        ],
        compiler_params=pltpu.CompilerParams(
            collective_id=cid, has_side_effects=True, vmem_limit_bytes=48 * 2**20
        ),
        cost_estimate=takes(90),
        name="finish",
    )(part, unit, above, resid, inverse, gain, wide, narrow)


def heads_kernel(group, kind, x_ref, o_ref, through, local_sem, send_sem, recv_sem):
    band, tp = lax.axis_index("band"), lax.axis_index("tp")
    mine = lax.rem(band, group)
    base = band - mine
    others = [lax.rem(mine + d, group) for d in range(1, group)]
    sems = Sems(send_sem, recv_sem, local_sem)
    width = through.shape[1]

    def columns(index):
        return pl.ds(pl.multiple_of(index * width, width), width)

    def source(index):
        return x_ref.at[:, columns(index)] if kind == "cut" else x_ref.at[index]

    target = o_ref.at[:, columns(mine)] if kind == "join" else o_ref.at[mine]
    barrier = pltpu.get_barrier_semaphore()
    for other in others:
        pl.semaphore_signal(barrier, inc=1, device_id=(base + other, tp), device_id_type=MESH)
    load = sems.copy(source(mine), through)
    pl.semaphore_wait(barrier, group - 1)
    copies = [sems.send(source(other), target, (base + other, tp)) for other in others]
    load.wait()
    for copy in [sems.copy(through, target), *copies]:
        copy.wait()


def swap_heads(x, group, cid, kind):
    if kind == "cut":
        rows, width = x.shape[0], x.shape[1] // group
    else:
        rows, width = x.shape[1:]
    if width % 128 and kind == "cut":
        x = x.reshape(rows, group, width).transpose(1, 0, 2)
        return swap_heads(x, group, cid, "plain")
    if width % 128 and kind == "join":
        x = swap_heads(x, group, cid, "plain")
        return x.transpose(1, 0, 2).reshape(rows, group * width)
    shape = (rows, group * width) if kind == "join" else (group, rows, width)
    return pl.pallas_call(
        functools.partial(heads_kernel, group, kind),
        out_shape=jax.ShapeDtypeStruct(shape, x.dtype),
        in_specs=[anywhere],
        out_specs=anywhere,
        scratch_shapes=[
            pltpu.VMEM((rows, width), x.dtype),
            pltpu.SemaphoreType.DMA((2,)),
            pltpu.SemaphoreType.DMA((group - 1,)),
            pltpu.SemaphoreType.DMA((group - 1,)),
        ],
        compiler_params=pltpu.CompilerParams(collective_id=cid, has_side_effects=True),
        cost_estimate=takes(4),
        name="swap_heads",
    )(x)


def project_kernel(x_ref, w_ref, bias_ref, scale_ref, o_ref):
    total = nn(x_ref[...], w_ref[...]) + bias_ref[...]
    o_ref[0] = total.astype(bf16) * scale_ref[...].astype(bf16)


def project(x, weight, bias, scale, group):
    rows, depth = x.shape
    total_width = bias.shape[0]
    width = total_width // group
    if width % 128:
        total = (nn(x, weight[:, :total_width]) + bias).astype(bf16) * scale.astype(bf16)
        return total.reshape(rows, group, width).transpose(1, 0, 2)
    block = min(256, rows)
    return pl.pallas_call(
        project_kernel,
        out_shape=jax.ShapeDtypeStruct((group, rows, width), bf16),
        grid=(group, rows // block),
        in_specs=[
            pl.BlockSpec((block, depth), lambda g, i: (i, 0)),
            pl.BlockSpec((depth, width), lambda g, i: (0, g)),
            pl.BlockSpec((1, width), lambda g, i: (0, g)),
            pl.BlockSpec((1, width), lambda g, i: (0, g)),
        ],
        out_specs=pl.BlockSpec((1, block, width), lambda g, i: (g, i, 0)),
        compiler_params=pltpu.CompilerParams(vmem_limit_bytes=40 * 2**20),
        cost_estimate=pl.CostEstimate(
            flops=2 * rows * depth * width * group, bytes_accessed=12 * 2**20, transcendentals=0
        ),
        name="project",
    )(x, weight, bias[None], scale[None])


def permitted(first, limit, row, column):
    return ((column >= first) & (column <= limit)) | (column == row)


def head_mask(head, shape):
    lane = lax.broadcasted_iota(jnp.int32, shape, 1)
    return (lane >= head * HEAD_DIM) & (lane < (head + 1) * HEAD_DIM)


def attend_kernel(qb, kb, info_ref, first_ref, q_ref, k_ref, v_ref, o_ref, log_ref, vt_ref):
    length, width = q_ref.shape
    heads = width // HEAD_DIM
    live_end = info_ref[0]
    count = lax.div(live_end + qb - 1, qb)
    vt_ref[...] = v_ref[...].T
    o_ref[...] = jnp.zeros_like(o_ref)
    log_ref[...] = jnp.zeros_like(log_ref)

    def queries(i, _):
        rows = pl.ds(pl.multiple_of(i * qb, qb), qb)
        q = q_ref[rows, :]
        first = first_ref[0:1, rows]
        row = i * qb + lax.broadcasted_iota(jnp.int32, (1, qb), 1)
        limit = jnp.minimum(row, live_end - 1)
        q_heads = [
            jnp.where(head_mask(h, (qb, width)), q, jnp.zeros_like(q)) for h in range(heads)
        ]
        def keys(j, carry):
            columns = pl.ds(pl.multiple_of(j * kb, kb), kb)
            k = k_ref[columns, :]
            column = j * kb + lax.broadcasted_iota(jnp.int32, (kb, 1), 0)
            allowed = permitted(first, limit, row, column)
            out = []
            for h in range(heads):
                top, total, summed = carry[h]
                scores = jnp.where(allowed, nt(k, q_heads[h]), masked_score)
                new_top = jnp.maximum(top, jnp.max(scores, axis=0, keepdims=True))
                weights = jnp.exp(scores - new_top)
                scale = jnp.exp(top - new_top)
                total = total * scale + jnp.sum(weights, axis=0, keepdims=True)
                vt = vt_ref[h * HEAD_DIM : (h + 1) * HEAD_DIM, columns]
                summed = summed * scale + nn(vt, weights.astype(bf16))
                out.append((new_top, total, summed))
            return tuple(out)
        start = tuple(
            (
                jnp.full((1, qb), masked_score, f32),
                jnp.zeros((1, qb), f32),
                jnp.zeros((HEAD_DIM, qb), f32),
            )
            for _ in range(heads)
        )
        lo = lax.div(info_ref[1 + i], kb)
        hi = lax.div(i * qb + qb - 1, kb) + 1
        done = lax.fori_loop(lo, hi, keys, start)
        mixed = jnp.concatenate([summed / total for _, total, summed in done], axis=0)
        o_ref[rows, :] = mixed.T.astype(o_ref.dtype)
        for h, (top, total, _) in enumerate(done):
            log_ref[0, h : h + 1, rows] = top + jnp.log(total)
        return 0
    lax.fori_loop(0, count, queries, 0)


def attend_back_kernel(
    qb, kb, info_ref, first_ref, q_ref, k_ref, v_ref, o_ref, do_ref, log_ref, out_ref, sum_ref,
    dk_acc, dv_acc,
):
    length, width = q_ref.shape
    heads = width // HEAD_DIM
    features = out_ref.shape[1] // 3
    slab = pl.program_id(0)
    factor = HEAD_DIM ** (-0.5)
    live_end = info_ref[0]
    count = lax.div(live_end + qb - 1, qb)

    def lanes(which):
        if features == width:
            return pl.ds(which * features, width)
        return pl.ds(pl.multiple_of(which * features + slab * width, width), width)
    dk_acc[...] = jnp.zeros_like(dk_acc)
    dv_acc[...] = jnp.zeros_like(dv_acc)
    out_ref[:, lanes(0)] = jnp.zeros((length, width), out_ref.dtype)

    def queries(i, _):
        rows = pl.ds(pl.multiple_of(i * qb, qb), qb)
        q, do = q_ref[rows, :], do_ref[rows, :]
        first = first_ref[0:1, rows]
        row = i * qb + lax.broadcasted_iota(jnp.int32, (1, qb), 1)
        limit = jnp.minimum(row, live_end - 1)
        dots = (do.astype(f32) * o_ref[rows, :].astype(f32)).T
        masks = [head_mask(h, (qb, width)) for h in range(heads)]
        kmasks = [head_mask(h, (kb, width)) for h in range(heads)]
        zero = jnp.zeros_like(q)
        q_heads = [jnp.where(mask, q, zero) for mask in masks]
        do_heads = [jnp.where(mask, do, zero) for mask in masks]
        logs = [log_ref[0, h : h + 1, rows] for h in range(heads)]
        deltas = [
            jnp.sum(dots[h * HEAD_DIM : (h + 1) * HEAD_DIM], axis=0, keepdims=True)
            for h in range(heads)
        ]
        def keys(j, dq):
            columns = pl.ds(pl.multiple_of(j * kb, kb), kb)
            k, v = k_ref[columns, :], v_ref[columns, :]
            column = j * kb + lax.broadcasted_iota(jnp.int32, (kb, 1), 0)
            allowed = permitted(first, limit, row, column)
            dk, dv = dk_acc[columns, :], dv_acc[columns, :]
            for h in range(heads):
                scores = jnp.where(allowed, nt(k, q_heads[h]) - logs[h], masked_score)
                probs = jnp.exp(scores)
                prob_grad = nt(v, do_heads[h])
                score_grad = (probs * (prob_grad - deltas[h])).astype(bf16)
                dv = dv + nn(probs.astype(bf16), do_heads[h])
                dk = dk + nn(score_grad, q_heads[h])
                dq = dq + tn(score_grad, jnp.where(kmasks[h], k, jnp.zeros_like(k)))
            dk_acc[columns, :] = dk
            dv_acc[columns, :] = dv
            return dq
        lo = lax.div(info_ref[1 + i], kb)
        hi = lax.div(i * qb + qb - 1, kb) + 1
        dq = lax.fori_loop(lo, hi, keys, jnp.zeros((qb, width), f32))
        out_ref[rows, lanes(0)] = (dq * factor).astype(out_ref.dtype)
        return 0
    lax.fori_loop(0, count, queries, 0)
    sum_ref[...] = jnp.zeros_like(sum_ref)

    def store(i, _):
        rows = pl.ds(pl.multiple_of(i * kb, kb), kb)
        dv = dv_acc[rows, :].astype(out_ref.dtype)
        out_ref[rows, lanes(1)] = dk_acc[rows, :].astype(out_ref.dtype)
        out_ref[rows, lanes(2)] = dv
        dq = out_ref[rows, lanes(0)].astype(f32)
        sum_ref[0, 0:1, :] += jnp.sum(dq, axis=0, keepdims=True)
        sum_ref[0, 1:2, :] += jnp.sum(dv.astype(f32), axis=0, keepdims=True)
        return 0
    lax.fori_loop(0, length // kb, store, 0)


def attention_specs(length, features):
    width = min(256, features)
    slabs = features // width

    plain = pl.BlockSpec((length, width), lambda i, info: (0, i))

    def piece(which):
        if features % 128:
            return plain
        return pl.BlockSpec((length, width), lambda i, info, w=which: (0, w * slabs + i))

    logs = pl.BlockSpec((1, 8, length), lambda i, info: (i, 0, 0))
    first = pl.BlockSpec((1, length), lambda i, info: (0, 0))
    return width, slabs, piece, plain, logs, first


def three(qkv, features):
    if features % 128:
        return [qkv[:, w * features : (w + 1) * features] for w in range(3)]
    return [qkv] * 3


def attend(qkv, info, first, qb, kb):
    length, features = qkv.shape[0], qkv.shape[1] // 3
    width, slabs, piece, plain, logs, first_spec = attention_specs(length, features)
    return pl.pallas_call(
        functools.partial(attend_kernel, qb, kb),
        out_shape=(
            jax.ShapeDtypeStruct((length, features), bf16),
            jax.ShapeDtypeStruct((slabs, 8, length), f32),
        ),
        grid_spec=pltpu.PrefetchScalarGridSpec(
            num_scalar_prefetch=1,
            grid=(slabs,),
            in_specs=[first_spec, piece(0), piece(1), piece(2)],
            out_specs=(plain, logs),
            scratch_shapes=[pltpu.VMEM((width, length), bf16)],
        ),
        compiler_params=pltpu.CompilerParams(vmem_limit_bytes=48 * 2**20),
        cost_estimate=takes(30),
        name="attend",
    )(info, first, *three(qkv, features))


def attend_back(qkv, mixed, grad, log_total, info, first, qb, kb):
    length, features = qkv.shape[0], qkv.shape[1] // 3
    width, slabs, piece, plain, logs, first_spec = attention_specs(length, features)
    return pl.pallas_call(
        functools.partial(attend_back_kernel, qb, kb),
        out_shape=(
            jax.ShapeDtypeStruct((length, 3 * features), bf16),
            jax.ShapeDtypeStruct((slabs, 8, width), f32),
        ),
        grid_spec=pltpu.PrefetchScalarGridSpec(
            num_scalar_prefetch=1,
            grid=(slabs,),
            in_specs=[first_spec, piece(0), piece(1), piece(2), plain, plain, logs],
            out_specs=(
                pl.BlockSpec((length, 3 * features), lambda i, info: (0, 0)),
                pl.BlockSpec((1, 8, width), lambda i, info: (i, 0, 0)),
            ),
            scratch_shapes=[pltpu.VMEM((length, width), f32), pltpu.VMEM((length, width), f32)],
        ),
        compiler_params=pltpu.CompilerParams(vmem_limit_bytes=48 * 2**20),
        cost_estimate=takes(34),
        name="attend_back",
    )(info, first, *three(qkv, features), mixed, grad, log_total)


def body(
    tokens,
    positions,
    doc_lengths,
    exit_depth,
    w_query,
    w_key,
    w_value,
    w_out,
    w_up,
    w_down,
    b_query,
    b_value,
    b_out,
    b_up,
    b_down,
    attn_gain,
    attn_bias,
    ffn_gain,
    ffn_bias,
    cotangent,
):
    seqs, local_rows, width = tokens.shape
    inner = b_query.shape[0]
    bands, tps = lax.axis_size("band"), lax.axis_size("tp")
    group = bands // seqs
    piece = local_rows // (group * tps)
    band, tp = lax.axis_index("band"), lax.axis_index("tp")
    seq, member = band // group, lax.rem(band, group)
    features = inner // group
    length = exit_depth.shape[1]
    own = bands * piece
    rows = tps * own
    block, half_block = min(512, length), min(256, length)

    def by_group(*parts):
        split = [p.reshape(p.shape[:-1] + (group, features)) for p in parts]
        return jnp.stack(split, axis=-2).reshape(parts[0].shape[:-1] + (-1,))

    def share(grad):
        return lax.psum_scatter(grad, "band", scatter_dimension=0, tiled=True)

    w_in_out = jnp.concatenate([by_group(w_query, w_key, w_value), w_out.T], axis=1)
    w_in_out = lax.all_gather(w_in_out, "band", axis=0, tiled=True)
    w_in, w_out_t = w_in_out[:, : 3 * inner], w_in_out[:, 3 * inner :]
    w_up_all = lax.all_gather(w_up, "band", axis=0, tiled=True)
    w_down_t = lax.all_gather(w_down.T, "band", axis=0, tiled=True)

    def my_share(array):
        split = array.reshape(seqs, group, tps, piece, width)
        return lax.dynamic_index_in_dim(split, tp, 2, keepdims=False).reshape(bands, piece, width)

    token_own, all_pos = transfer([Swap(my_share(tokens), positions)], 0, name="swap_in")
    seq_pos = lax.dynamic_index_in_dim(all_pos, seq, 1, keepdims=False)
    seq_pos = seq_pos.reshape(bands, group, tps, piece).transpose(1, 2, 0, 3)
    row_pos = seq_pos.reshape(length)
    member_pos = lax.dynamic_index_in_dim(seq_pos, member, 0, keepdims=False)
    own_pos = lax.dynamic_index_in_dim(member_pos, tp, 0, keepdims=False).reshape(own)
    depths = lax.dynamic_index_in_dim(exit_depth, seq, 0, keepdims=False)
    live_end = jnp.sum((depths > LAYER).astype(jnp.int32))
    live_own = (own_pos < live_end).astype(f32)[:, None]
    ends = jnp.cumsum(lax.dynamic_index_in_dim(doc_lengths, seq, 0, keepdims=False))
    places = jnp.arange(length, dtype=jnp.int32)
    first = jnp.max(jnp.where(ends[:, None] <= places[None, :], ends[:, None], 0), axis=0)
    info = jnp.concatenate([live_end[None], first[::block]]).astype(jnp.int32)
    first = first[None, :].astype(jnp.int32)
    to_sorted = (row_pos[None, :] == places[:, None]).astype(bf16)
    to_rows = (row_pos[:, None] == places[None, :]).astype(bf16)

    inputs = token_own.reshape(own, width).astype(f32)
    normed_in, unit_in, inverse_in = layer_norm(inputs, attn_gain, attn_bias)
    z1, grad_low = transfer([Gather(normed_in.astype(bf16)), Swap(my_share(cotangent))], 1, name="gather_in")
    z1 = z1.reshape(rows, width)
    grad_own = grad_low.reshape(own, width).astype(f32)
    down_grad_own = (live_own * grad_own).astype(bf16)
    down_grad = gather_later(down_grad_own)

    bias_in = by_group(b_query, jnp.zeros_like(b_query), b_value)
    scale_in = by_group(
        jnp.full_like(b_query, HEAD_DIM ** (-0.5)), jnp.ones_like(b_query), jnp.ones_like(b_query)
    )
    qkv = project(z1, w_in_out, bias_in, scale_in, group)
    qkv = swap_heads(qkv, group, 4, "plain").reshape(length, 3 * features)
    qkv = nn(to_sorted, qkv).astype(bf16)
    mixed_sorted, log_total = attend(qkv, info, first, block, block)
    mixed_sorted, down_grad = lax.optimization_barrier((mixed_sorted, down_grad))
    down_grad = down_grad.reshape(rows, width)
    mixed = nn(to_rows, mixed_sorted).astype(bf16).reshape(group, rows, features)
    mixed = swap_heads(mixed, group, 5, "join")

    attn_part = nt(mixed, w_out_t).astype(bf16).reshape(tps, own, width)
    (attn_out,) = transfer([Scatter(attn_part)], 6, name="scatter_attn")
    attn_out = attn_out + b_out
    residual = inputs + attn_out
    normed_mid, unit_mid, inverse_mid = layer_norm(residual, ffn_gain, ffn_bias)
    (z2,) = transfer([Gather(normed_mid.astype(bf16))], 7, name="gather_mid")
    z2 = z2.reshape(rows, width)
    pre_act = nn(z2, w_up_all) + b_up
    below = 0.5 * (1.0 + lax.erf(pre_act * 0.5**0.5))
    act = (pre_act * below).astype(bf16)
    slope = (below + pre_act * jnp.exp(-0.5 * pre_act * pre_act) * (2 * math.pi) ** -0.5).astype(bf16)

    grad_w_down_t = tn(down_grad, act).astype(bf16)
    grad_w_down_t, act, w_down_t = lax.optimization_barrier((grad_w_down_t, act, w_down_t))
    shared_down = share(grad_w_down_t)
    ffn_part = nt(act, w_down_t).astype(bf16).reshape(tps, own, width)
    ffn_out, up_grad = transfer(
        [Scatter(ffn_part)],
        8,
        Work([down_grad, w_down_t, slope], [("nn", 0, 1, 2, 0)], 1),
        name="scatter_ffn",
    )
    output = (inputs + live_own * (attn_out + ffn_out + b_down)).astype(bf16)
    output = output.reshape(bands, piece, width)

    mid_part = nt(up_grad, w_up_all).astype(bf16).reshape(tps, own, width)
    mid_grad, output, grad_w_up, up_sums = transfer(
        [Scatter(mid_part), Swap(output)],
        9,
        Work([z2, up_grad], [("tn", 0, 1, None, 0), ("sum", 1, None, None, 1)], 1),
        name="scatter_mid",
    )
    resid_grad = norm_back(mid_grad, unit_mid, inverse_mid, ffn_gain)
    attn_grad_own = (live_own * grad_own + resid_grad).astype(bf16)
    (attn_grad,) = transfer([Gather(attn_grad_own)], 10, name="gather_back")
    attn_grad = attn_grad.reshape(rows, width)
    attn_grad, output = lax.optimization_barrier((attn_grad, output))
    output = gather_later(output)

    grad_w_out_t = tn(attn_grad, mixed).astype(bf16)
    mixed_grad = nn(attn_grad, w_out_t).astype(bf16)
    mixed_grad = swap_heads(mixed_grad, group, 13, "cut").reshape(length, features)
    mixed_grad = nn(to_sorted, mixed_grad).astype(bf16)
    grad_w_up, shared_down = lax.optimization_barrier((grad_w_up, shared_down))
    shared_up = share(grad_w_up)
    mixed_grad, grad_w_out_t = lax.optimization_barrier((mixed_grad, grad_w_out_t))
    in_grad, in_sums = attend_back(
        qkv, mixed_sorted, mixed_grad, log_total, info, first, block, half_block
    )
    in_sums = in_sums.transpose(1, 0, 2).reshape(8, features)
    mine = (jnp.arange(group) == member).astype(f32)[:, None]
    in_grad, output = lax.optimization_barrier((in_grad, output))
    output = output.transpose(1, 0, 2, 3).reshape(tokens.shape)
    in_grad = nn(to_rows, in_grad).astype(bf16).reshape(group, rows, 3 * features)
    in_grad = swap_heads(in_grad, group, 14, "join")
    in_part = nt(in_grad, w_in).astype(bf16).reshape(tps, bands, piece, width)
    in_part, in_grad = lax.optimization_barrier((in_part, in_grad))
    grad_w_in = tn(z1, in_grad).astype(bf16)
    grad_w_in_out = jnp.concatenate([grad_w_in, grad_w_out_t], axis=1)
    grad_w_in_out, shared_up, in_part = lax.optimization_barrier((grad_w_in_out, shared_up, in_part))
    shared_in_out = share(grad_w_in_out)

    def over_rows(array):
        return jnp.sum(array.astype(f32), axis=0)

    wide = [
        over_rows(attn_grad_own),
        over_rows(down_grad_own),
        over_rows(mid_grad * unit_mid),
        over_rows(mid_grad),
    ]
    wide = jnp.concatenate(wide).astype(bf16).reshape(16, width // 4)
    narrow = jnp.concatenate(
        [(mine * in_sums[0]).reshape(-1), (mine * in_sums[1]).reshape(-1), up_sums[0]]
    )
    count = narrow.shape[0]
    narrow = jnp.pad(narrow, (0, -count % 2048)).astype(bf16).reshape(16, -1)
    token_grad, wide, narrow = finish(
        in_part,
        unit_in.reshape(bands, piece, width),
        grad_low,
        resid_grad.reshape(bands, piece, width),
        inverse_in.reshape(bands, piece, 1),
        attn_gain[None],
        wide,
        narrow,
        15,
    )
    token_grad = token_grad.reshape(tokens.shape).astype(f32)
    wide, late = wide[:16].reshape(4, width), wide[16:].reshape(2, width)
    narrow = narrow.reshape(-1)[:count]
    shared_in = shared_in_out[:, : 3 * inner].astype(f32).reshape(-1, group, 3, features)
    shared_down, shared_out = shared_down.astype(f32).T, shared_in_out[:, 3 * inner :].astype(f32).T
    shared_up = shared_up.astype(f32)
    shared_q, shared_k, shared_v = (
        shared_in[:, :, which].reshape(-1, inner) for which in range(3)
    )

    return (
        output,
        token_grad,
        shared_q,
        shared_k,
        shared_v,
        shared_out,
        shared_up,
        shared_down,
        narrow[:inner],
        narrow[inner : 2 * inner],
        wide[0],
        narrow[2 * inner :],
        wide[1],
        late[0],
        late[1],
        wide[2],
        wide[3],
    )


def solution(mesh):
    return jax.shard_map(
        body,
        mesh=mesh,
        in_specs=(
            P(None, "band", None),
            P(None, "band"),
            P(),
            P(),
            P("band", "tp"),
            P("band", "tp"),
            P("band", "tp"),
            P("tp", "band"),
            P("band", "tp"),
            P("tp", "band"),
            P("tp"),
            P("tp"),
            P(),
            P("tp"),
            P(),
            P(),
            P(),
            P(),
            P(),
            P(None, "band", None),
        ),
        out_specs=(
            P(None, "band", None),
            P(None, "band", None),
            P("band", "tp"),
            P("band", "tp"),
            P("band", "tp"),
            P("tp", "band"),
            P("band", "tp"),
            P("tp", "band"),
            P("tp"),
            P("tp"),
            P(),
            P("tp"),
            P(),
            P(),
            P(),
            P(),
            P(),
        ),
        check_vma=False,
    )
```

time: 806 us -> 726 us (0.901)
  matrix products: 151 us -> 129 us
  starting transfers between devices: 26.5 us -> 10.1 us
  waiting for transfers between devices: 43.8 us -> 27.7 us
  Pallas kernels: 455 us -> 441 us
    all_to_all x3 -> x0, waiting for transfers between devices: 20.5 us -> none  [the longest x1 20.5 us: body(): ffn_part = lax.all_to_all(ffn_part, 'tp', 0, 0)]
    dot_general x7 -> x6, matrix products: 68.2 us -> 49.7 us  [nn(): return jnp.dot(left, right, preferred_element_type=f32)]
    pallas_call x15 -> x14, Pallas kernels: 447 us -> 430 us  [the longest x7 294 us: transfer(): pl.pallas_call(kernel, out_shape=tuple((shape for item in items for shape...]
    all_to_all x3 -> x0, starting transfers between devices: 16.1 us -> none  [the longest x1 7.23 us: body(): lax.all_to_all(output_own.reshape(bands, piece, width), 'band', 0, 0)]
    concatenate x1 -> x5, other arithmetic: 0.72 us -> 9.75 us  [the longest x1 7.91 us: body(): grad_w_in_out = jnp.concatenate([grad_w_in, grad_w_out_t], axis=1)]
    unnamed x168 -> x144, local copies, waits for them, and re-layouts: 37.3 us -> 35.6 us
    dot_general x4 -> x3, matrix products: 37.7 us -> 36.5 us  [tn(): lax.dot_general(left, right, (((0,), (0,)), ((), ())), preferred_element_...]
  transfers between devices with their start and end apart: 13 -> 8, of which waited for: 3 -> 3; matrix products, arithmetic and copies ran while one was open for 23% -> 26% of each run, Pallas kernels for 57% -> 61%
where the time goes in v2:
time: 726 us; the launch traced here: 718 us
  Pallas kernels  441 us (61%)
  matrix products  129 us (18%)
  local copies, waits for them, and re-layouts  58 us (8%)
  other arithmetic  37.4 us (5%)
  waiting for transfers between devices  27.7 us (4%)
  between operations  15.2 us (2%)
  starting transfers between devices  10.1 us (1%)
    pallas_call x7, Pallas kernels, transfer(): pl.pallas_call(kernel, out_shape=tuple((shape for item in items for shape...  294 us
    pallas_call x1, Pallas kernels, finish(): pl.pallas_call(functools.partial(finish_kernel, count, size), out_shape=(...  91.4 us
    dot_general x6, matrix products, nn(): return jnp.dot(left, right, preferred_element_type=f32)  49.7 us
    dot_general x4, matrix products, nt(): lax.dot_general(left, right, (((1,), (1,)), ((), ())), preferred_element_...  42.4 us
    dot_general x3, matrix products, tn(): lax.dot_general(left, right, (((0,), (0,)), ((), ())), preferred_element_...  36.5 us
    unnamed x144, local copies, waits for them, and re-layouts  35.6 us
    all_to_all x2, waiting for transfers between devices, gather_later(): lax.all_to_all(jnp.broadcast_to(x[None], (count,) + x.shape), 'tp', 0, 0)  25.4 us
    pallas_call x1, Pallas kernels, attend_back(): pl.pallas_call(functools.partial(attend_back_kernel, qb, kb), out_shape=(...  17.8 us
  transfers between devices with their start and end apart: 8, of which 3 were waited for; matrix products, arithmetic and copies ran while one was open for 26% of the time, Pallas kernels for 61%

profile of v2, /device:TPU:9, one launch (start us, length us, event | category | flops | bytes accessed | tf_op | source)
XLA Modules:
  0.0 717.8 jit_solution(10025926870991222268)
XLA Ops:
  14.8 59.2 %swap_in.1 = (bf16[8,32,2048]{2,1,0:T(8,128)(2,1)S(1)}, s32[8,4,256]{2,1,0:T(4,128)S(1)}) custom-call(bf16[8,32,2048]{2,1,0:T(8,128)(2,1)S(1)} %bitcast.135, s32[4,256]{1,0:T(4,128)S(1)} %copy-done.12), custom_call_target="tpu_custom_call" | custom-call | flops 35999997952 | bytes 72000000 | tf_op jit(solution)/shard_map/swap_in/pallas_call | solution.py:451
  79.9 47.1 %gather_in.1 = (bf16[4,256,2048]{2,1,0:T(8,128)(2,1)S(1)}, bf16[8,32,2048]{2,1,0:T(8,128)(2,1)S(1)}) custom-call(bf16[256,2048]{1,0:T(8,128)(2,1)S(1)} %fusion.28.refs_0_, bf16[8,32,2048]{2,1,0:T(8,128)(2,1)S(1)} %bitcast.134), custom_call_target="tpu_custom_call" | custom-call | flops 35999997952 | bytes 72000000 | tf_op jit(solution)/shard_map/gather_in/pallas_call | solution.py:451
  132.8 5.0 all-to-all-start
  142.9 11.2 %project.1.x_ref = bf16[2,1024,768]{2,1,0:T(8,128)(2,1)S(1)} custom-call(bf16[1024,2048]{1,0:T(8,128)(2,1)S(1)} %bitcast.139, bf16[2048,2048]{1,0:T(8,128)(2,1)} %all-gather.4.cloned.1.call-done.w_ref, f32[1,1536]{1,0:T(1,128)S(1)} %broadcast_in_dim_reshape.2.bias_ref, f32[1,1536]{1,0:T(1,128)S(1)} %copy-done.19), custom_call_target="tpu_custom_call" | custom-call | flops 6442450944 | bytes 12582912 | tf_op jit(solution)/shard_map/project/pallas_call | solution.py:749
  155.8 3.8 swap_heads.4
  159.5 9.4 %fusion.19.q_ref.k_ref.v_ref = bf16[2048,768]{1,0:T(8,128)(2,1)S(1)} fusion(bf16[2048,768]{1,0:T(8,128)(2,1)} %bitcast.183, s32[2048]{0:T(1024)S(1)} %eq.38), kind=kOutput, calls=%fused_computation.28 | convolution fusion | flops 6448218112 | bytes 6299648 | tf_op jit(solution)/shard_map/dot_general | solution.py:38
  169.0 13.2 %attend.1 = (bf16[2048,256]{1,0:T(8,128)(2,1)S(1)}, f32[1,8,2048]{2,1,0:T(8,128)S(1)}) custom-call(s32[5]{0:T(128)S(1)} %pad_add_fusion.info_ref, s32[1,2048]{1,0:T(1,128)S(1)} %bitcast.137, bf16[2048,768]{1,0:T(8,128)(2,1)S(1)} %fusion.19.q_ref.k_ref.v_ref, bf16[2048,768]{1,0:T(8,128)(2,1)S(1)} %fusion.19.q_ref.k_ref.v_ref, ...), custom_call_target="tpu_custom_call" | custom-call | flops 30000001024 | bytes 60000000 | tf_op jit(solution)/shard_map/attend/pallas_call | solution.py:930
  185.4 3.8 fusion.21
  191.9 4.4 convolution_convert_fusion.4
  196.3 36.1 %scatter_attn.1 = f32[256,2048]{1,0:T(8,128)S(1)} custom-call(bf16[4,256,2048]{2,1,0:T(8,128)(2,1)S(1)} %bitcast.145), custom_call_target="tpu_custom_call" | custom-call | flops 35999997952 | bytes 72000000 | tf_op jit(solution)/shard_map/scatter_attn/pallas_call | solution.py:451
  235.2 34.9 %gather_mid.1 = bf16[4,256,2048]{2,1,0:T(8,128)(2,1)S(1)} custom-call(bf16[256,2048]{1,0:T(8,128)(2,1)S(1)} %add_convert_fusion.1.refs_0_), custom_call_target="tpu_custom_call" | custom-call | flops 35999997952 | bytes 72000000 | tf_op jit(solution)/shard_map/gather_mid/pallas_call | solution.py:451
  272.2 16.5 %fusion.8 = (bf16[1024,2048]{1,0:T(8,128)(2,1)}, bf16[1024,2048]{1,0:T(8,128)(2,1)S(1)}) fusion(f32[2048]{0:T(1024)S(1)} %copy-done.57, bf16[1024,2048]{1,0:T(8,128)(2,1)} %bitcast.141, bf16[2048,2048]{1,0:T(8,128)(2,1)} %all-gather.6.cloned.1.call-done), kind=kOutput, calls=%fused_computation.11 | convolution fusion | flops 8615100416 | bytes 20979712 | tf_op jit(solution)/shard_map/dot_general | solution.py:38
  290.7 23.9 %convolution_convert_fusion.1 = bf16[2048,2048]{1,0:T(8,128)(2,1)} fusion(bf16[1024,2048]{1,0:T(8,128)(2,1)} %bitcast.22.refs_1_, bf16[1024,2048]{1,0:T(8,128)(2,1)S(1)} %get-tuple-element.59), kind=kOutput, calls=%fused_computation.20 | convolution fusion | flops 8594128896 | bytes 16777216 | tf_op jit(solution)/shard_map/dot_general | solution.py:46
  314.6 14.0 %convolution_convert_fusion.3 = bf16[1024,2048]{1,0:T(8,128)(2,1)} fusion(bf16[1024,2048]{1,0:T(8,128)(2,1)} %copy-done.60, bf16[2048,2048]{1,0:T(8,128)(2,1)} %all-gather.8.cloned.1.call-done.refs_2_), kind=kOutput, calls=%fused_computation.25 | convolution fusion | flops 8592031744 | bytes 16777216 | tf_op jit(solution)/shard_map/dot_general | solution.py:42
  328.6 35.9 %scatter_ffn.1 = (f32[256,2048]{1,0:T(8,128)}, bf16[1024,2048]{1,0:T(8,128)(2,1)}) custom-call(bf16[4,256,2048]{2,1,0:T(8,128)(2,1)} %bitcast.181, bf16[1024,2048]{1,0:T(8,128)(2,1)} %bitcast.22.refs_1_, bf16[2048,2048]{1,0:T(8,128)(2,1)} %all-gather.8.cloned.1.call-done.refs_2_, bf16[1024,2048]{1,0:T(8,128)(2,1)} %get-tuple-element.200.refs_3_), custom_call_target="tpu_custom_call" | custom-call | flops 35999997952 | bytes 72000000 | tf_op jit(solution)/shard_map/scatter_ffn/pallas_call | solution.py:451
  367.9 12.8 %convolution_convert_fusion.2 = bf16[1024,2048]{1,0:T(8,128)(2,1)} fusion(bf16[1024,2048]{1,0:T(8,128)(2,1)S(1)} %copy-done.61, bf16[2048,2048]{1,0:T(8,128)(2,1)} %all-gather.6.cloned.1.call-done), kind=kOutput, calls=%fused_computation.24 | convolution fusion | flops 8592031744 | bytes 16777216 | tf_op jit(solution)/shard_map/dot_general | solution.py:42
  380.7 45.7 %scatter_mid.1 = (f32[256,2048]{1,0:T(8,128)}, bf16[8,32,2048]{2,1,0:T(8,128)(2,1)}, bf16[2048,2048]{1,0:T(8,128)(2,1)}, f32[1,2048]{1,0:T(1,128)}) custom-call(bf16[4,256,2048]{2,1,0:T(8,128)(2,1)} %bitcast.180, bf16[8,32,2048]{2,1,0:T(8,128)(2,1)} %bitcast.157, bf16[1024,2048]{1,0:T(8,128)(2,1)} %bitcast.142, bf16[1024,2048]{1,0:T(8,128)(2,1)} %get-tuple-element.61.refs_3_), custom_call_target="tpu_custom_call" | custom-call | flops 35999997952 | bytes 72000000 | tf_op jit(solution)/shard_map/scatter_mid/pallas_call | solution.py:451
  434.4 35.2 %gather_back.1 = bf16[4,256,2048]{2,1,0:T(8,128)(2,1)S(1)} custom-call(bf16[256,2048]{1,0:T(8,128)(2,1)S(1)} %get-tuple-element.194.refs_0_), custom_call_target="tpu_custom_call" | custom-call | flops 35999997952 | bytes 72000000 | tf_op jit(solution)/shard_map/gather_back/pallas_call | solution.py:451
  471.7 5.0 fusion.34.x_ref
  479.0 4.5 fusion.20.do_ref
  489.8 4.9 all-to-all-start.1
  494.8 4.1 copy.119
  498.9 17.8 %attend_back.1 = (bf16[2048,768]{1,0:T(8,128)(2,1)S(1)}, f32[1,8,256]{2,1,0:T(8,128)S(1)}) custom-call(s32[5]{0:T(128)S(1)} %pad_add_fusion.info_ref, s32[1,2048]{1,0:T(1,128)S(1)} %bitcast.138, bf16[2048,768]{1,0:T(8,128)(2,1)} %copy-done.23, bf16[2048,768]{1,0:T(8,128)(2,1)} %copy-done.23, bf16[2048,768]{1,0:T(8,128)(2,1)} %copy-done.23, ...), custom_call_target="tpu_custom_call" | custom-call | flops 33999998976 | bytes 68000000 | tf_op jit(solution)/shard_map/attend_back/pallas_call | solution.py:952
  518.4 23.8 %all-to-all-done.1 = bf16[4,8,32,2048]{3,2,1,0:T(8,128)(2,1)} async-done(((bf16[4,8,32,2048]{3,2,1,0:T(8,128)(2,1)}), bf16[4,8,32,2048]{3,2,1,0:T(8,128)(2,1)}, u32[]{:S(2)}, u32[]{:S(2)}) %all-to-all-start.1) | async-done | bytes 4194336 | tf_op jit(solution)/shard_map/all_to_all | solution.py:472
  542.2 10.5 %fusion.18 = bf16[2048,768]{1,0:T(8,128)(2,1)} fusion(bf16[2048,768]{1,0:T(8,128)(2,1)} %copy-done.24, s32[2048]{0:T(1024)S(1)} %copy-done.53), kind=kOutput, calls=%fused_computation.27 | convolution fusion | flops 6448218112 | bytes 6299648 | tf_op jit(solution)/shard_map/dot_general | solution.py:38
  552.6 4.4 swap_heads.7
  557.0 11.3 %fusion.15 = bf16[1024,2048]{1,0:T(8,128)(2,1)} fusion(bf16[1024,1536]{1,0:T(8,128)(2,1)} %swap_heads.7, bf16[2048,2048]{1,0:T(8,128)(2,1)} %all-gather.4.cloned.1.call-done.w_ref), kind=kOutput, calls=%fused_computation.23 | convolution fusion | flops 6444548096 | bytes 13631488 | tf_op jit(solution)/shard_map/dot_general | solution.py:42
  568.4 9.0 %convolution_convert_fusion = bf16[2048,1536]{0,1:T(8,128)(2,1)} fusion(bf16[1024,2048]{1,0:T(8,128)(2,1)S(1)} %bitcast.140, bf16[1024,1536]{1,0:T(8,128)(2,1)S(1)} %copy-done.58), kind=kOutput, calls=%fused_computation.19 | convolution fusion | flops 6445596672 | bytes 13631488 | tf_op jit(solution)/shard_map/dot_general | solution.py:46
  577.4 7.9 %pad_maximum_fusion = bf16[2048,2048]{0,1:T(8,128)(2,1)} fusion(bf16[2048,512]{0,1:T(8,128)(2,1)S(1)} %copy-done.28, bf16[2048,1536]{0,1:T(8,128)(2,1)} %convolution_convert_fusion), kind=kLoop, calls=%fused_computation.12 | loop fusion | flops 16777216 | bytes 16777216 | tf_op jit(solution)/shard_map/concatenate | solution.py:1122
  588.4 5.6 copy.118
  599.5 91.4 %finish.1 = (bf16[8,4,32,2048]{3,2,1,0:T(8,128)(2,1)}, f32[24,512]{1,0:T(8,128)S(1)}, f32[16,256]{1,0:T(8,128)S(1)}) custom-call(bf16[4,8,32,2048]{3,2,1,0:T(8,128)(2,1)} %bitcast.179, f32[8,32,2048]{2,1,0:T(8,128)S(1)} %copy-done.7, bf16[8,32,2048]{2,1,0:T(8,128)(2,1)S(1)} %copy-done.5, f32[8,32,2048]{2,1,0:T(8,128)S(1)} %bitcast.133, ...), custom_call_target="tpu_custom_call" | custom-call | flops 89999998976 | bytes 180000000 | tf_op jit(solution)/shard_map/finish/pallas_call | solution.py:649
  690.9 6.8 convert.48
  (228 shorter events, 83.8 us)
Async XLA Ops:
  7.2 132.4 %copy-start = (s32[4,4]{1,0:T(4,128)S(1)}, s32[4,4]{1,0:T(4,128)}, u32[]{:S(2)}) copy-start(s32[4,4]{1,0:T(4,128)} %param.22) | copy-start | bytes 196
  7.2 133.5 %all-gather.4.cloned.1.call-start = ((), (), s32[]{:S(2)}) async-start(), calls=%async_computation.5 | async-start | bytes 9437184 | tf_op jit(solution)/shard_map/all_gather | solution.py:1017
  12.2 259.9 %all-gather.6.cloned.1.call-start = ((), (), s32[]{:S(2)}) async-start(), calls=%async_computation.6 | async-start | bytes 9437184 | tf_op jit(solution)/shard_map/all_gather | solution.py:1019
  14.8 64.6 %copy-start.8 = (f32[2048]{0:T(1024)S(1)}, f32[2048]{0:T(1024)}, u32[]{:S(2)}) copy-start(f32[2048]{0:T(1024)} %param.35) | copy-start | bytes 24580
  14.8 64.6 %copy-start.49 = (f32[2048]{0:T(1024)S(1)}, f32[2048]{0:T(1024)}, u32[]{:S(2)}) copy-start(f32[2048]{0:T(1024)} %param.36) | copy-start | bytes 24580
  73.9 290.5 %copy-start.2 = (bf16[8,32,2048]{2,1,0:T(8,128)(2,1)}, bf16[8,32,2048]{2,1,0:T(8,128)(2,1)S(1)}, u32[]{:S(2)}) copy-start(bf16[8,32,2048]{2,1,0:T(8,128)(2,1)S(1)} %get-tuple-element.53) | copy-start | bytes 3145732
  74.3 52.7 %copy-start.36 = (f32[8,32]{1,0:T(8,128)}, f32[8,32]{1,0:T(8,128)S(1)}, u32[]{:S(2)}) copy-start(f32[8,32]{1,0:T(8,128)S(1)} %broadcast_multiply_fusion) | copy-start | bytes 3076
  75.4 51.6 %copy-start.38 = (f32[8,32]{1,0:T(8,128)}, f32[8,32]{1,0:T(8,128)S(1)}, u32[]{:S(2)}) copy-start(f32[8,32]{1,0:T(8,128)S(1)} %get-tuple-element.216) | copy-start | bytes 3076
  79.4 49.6 %copy-start.47 = (f32[256]{0:T(256)}, f32[256]{0:T(256)S(1)}, u32[]{:S(2)}) copy-start(f32[256]{0:T(256)S(1)} %reshape.357) | copy-start | bytes 3076
  132.8 5.1 copy-start.32
  132.8 6.7 copy-start.55
  132.8 6.7 copy-start.56
  132.8 8.0 %copy-start.19 = (f32[1,1536]{1,0:T(1,128)S(1)}, f32[1,1536]{1,0:T(1,128)}, u32[]{:S(2)}) copy-start(f32[1,1536]{1,0:T(1,128)} %constant.99.clone.1.scale_ref) | copy-start | bytes 18436
  132.8 52.6 %all-to-all-start = ((bf16[4,256,2048]{2,1,0:T(8,128)(2,1)}), bf16[4,256,2048]{2,1,0:T(8,128)(2,1)}, u32[]{:S(2)}, u32[]{:S(2)}) async-start(bf16[4,256,2048]{2,1,0:T(8,128)(2,1)} %broadcast_in_dim.23), calls=%async_computation | async-start | bytes 8388608 | tf_op jit(solution)/shard_map/all_to_all | solution.py:472
  137.8 176.8 %all-gather.8.cloned.1.call-start = ((), (), s32[]{:S(2)}) async-start(), calls=%async_computation.7 | async-start | bytes 9437184 | tf_op jit(solution)/shard_map/all_gather | solution.py:1020
  139.3 288.6 %reduce-scatter.4.cloned.1.call-start = ((), (), s32[]{:S(2)}) async-start(), calls=%async_computation.8 | async-start | bytes 9437184 | tf_op jit(solution)/shard_map/reduce_scatter | solution.py:1014
  139.4 46.0 %copy-start.52 = (s32[2048]{0:T(1024)}, s32[2048]{0:T(1024)S(1)}, u32[]{:S(2)}) copy-start(s32[2048]{0:T(1024)S(1)} %eq.38) | copy-start | bytes 24580
  139.9 29.1 %copy-start.10 = (s32[2048]{0:T(1024)}, s32[2048]{0:T(1024)S(1)}, u32[]{:S(2)}) copy-start(s32[2048]{0:T(1024)S(1)} %select_reduce_fusion) | copy-start | bytes 24580
  183.8 5.4 copy-start.21
  196.3 36.2 %copy-start.40 = (f32[2048]{0:T(1024)S(1)}, f32[2048]{0:T(1024)}, u32[]{:S(2)}) copy-start(f32[2048]{0:T(1024)} %param.32) | copy-start | bytes 24580
  235.2 37.0 %copy-start.57 = (f32[2048]{0:T(1024)S(1)}, f32[2048]{0:T(1024)}, u32[]{:S(2)}) copy-start(f32[2048]{0:T(1024)} %param.33) | copy-start | bytes 24580
  314.6 270.7 %reduce-scatter.6.cloned.1.call-start = ((), (), s32[]{:S(2)}) async-start(), calls=%async_computation.9 | async-start | bytes 9437184 | tf_op jit(solution)/shard_map/reduce_scatter | solution.py:1014
  328.6 35.9 %copy-start.48 = (f32[256]{0:T(256)S(1)}, f32[256]{0:T(256)}, u32[]{:S(2)}) copy-start(f32[256]{0:T(256)} %copy-done.47) | copy-start | bytes 3076
  328.6 35.9 %copy-start.51 = (f32[2048]{0:T(1024)S(1)}, f32[2048]{0:T(1024)}, u32[]{:S(2)}) copy-start(f32[2048]{0:T(1024)} %param.34) | copy-start | bytes 24580
  489.8 52.3 %all-to-all-start.1 = ((bf16[4,8,32,2048]{3,2,1,0:T(8,128)(2,1)}), bf16[4,8,32,2048]{3,2,1,0:T(8,128)(2,1)}, u32[]{:S(2)}, u32[]{:S(2)}) async-start(bf16[4,8,32,2048]{3,2,1,0:T(8,128)(2,1)} %broadcast_in_dim.24), calls=%async_computation.1 | async-start | bytes 8388608 | tf_op jit(solution)/shard_map/all_to_all | solution.py:472
  494.8 209.9 %reduce-scatter.8.cloned.1.call-start = ((), (), s32[]{:S(2)}) async-start(), calls=%async_computation.10 | async-start | bytes 9437184 | tf_op jit(solution)/shard_map/reduce_scatter | solution.py:1014
  557.0 11.4 %copy-start.15 = (bf16[4,256,2048]{2,1,0:T(8,128)(2,1)S(1)}, bf16[4,256,2048]{2,1,0:T(8,128)(2,1)}, u32[]{:S(2)}) copy-start(bf16[4,256,2048]{2,1,0:T(8,128)(2,1)} %copy-done.13) | copy-start | bytes 12582916
  557.0 11.4 %copy-start.58 = (bf16[1024,1536]{1,0:T(8,128)(2,1)S(1)}, bf16[1024,1536]{1,0:T(8,128)(2,1)}, u32[]{:S(2)}) copy-start(bf16[1024,1536]{1,0:T(8,128)(2,1)} %swap_heads.7) | copy-start | bytes 9437188
  568.4 9.0 %copy-start.28 = (bf16[2048,512]{0,1:T(8,128)(2,1)S(1)}, bf16[2048,512]{0,1:T(8,128)(2,1)}, u32[]{:S(2)}) copy-start(bf16[2048,512]{0,1:T(8,128)(2,1)} %copy.119) | copy-start | bytes 6291460
  588.4 5.6 copy-start.30
  690.9 12.2 %copy-start.29 = (bf16[256,2048]{1,0:T(8,128)(2,1)S(1)}, bf16[256,2048]{1,0:T(8,128)(2,1)}, u32[]{:S(2)}) copy-start(bf16[256,2048]{1,0:T(8,128)(2,1)} %reduce-scatter.6.cloned.1.call-done) | copy-start | bytes 3145732
  703.1 7.7 %copy-start.1 = (s32[4,4]{1,0:T(4,128)S(1)}, s32[4,4]{1,0:T(4,128)}, u32[]{:S(2)}) copy-start(s32[4,4]{1,0:T(4,128)} %param.22) | copy-start | bytes 196
  (38 other events, 86.7 us)
Sparse Core Ops, SparseCore 0:
  12.4 119.3 all-gather.3
  133.4 83.1 all-gather.5
  218.7 80.5 all-gather.7
  314.7 113.1 reduce-scatter.3
  430.0 87.0 reduce-scatter.5
  585.5 115.7 reduce-scatter.7

commit v3 on v2

--- a/solution.py
+++ b/solution.py
@@ -342,11 +342,13 @@
         self.operands = operands
         self.shapes = []
         for kind, left, right, _, _ in tasks:
+            known = [*operands, *self.shapes]
             if kind == "sum":
-                self.shapes.append(jax.ShapeDtypeStruct((1, operands[left].shape[1]), f32))
+                self.shapes.append(jax.ShapeDtypeStruct((1, known[left].shape[1]), f32))
                 continue
-            rows = operands[left].shape[1 if kind == "tn" else 0]
-            self.shapes.append(jax.ShapeDtypeStruct((rows, operands[right].shape[1]), bf16))
+            rows = known[left].shape[1 if kind == "tn" else 0]
+            columns = known[right].shape[0 if kind == "nt" else 1]
+            self.shapes.append(jax.ShapeDtypeStruct((rows, columns), bf16))
         self.scratch = [pltpu.VMEM(x.shape, x.dtype) for x in [*operands, *self.shapes]]
         self.locals = len(operands) + len(tasks)
 
@@ -357,7 +359,7 @@
         self.stores = []
 
     def ready(self, k):
-        if self.loads[k] is not None:
+        if k < len(self.loads) and self.loads[k] is not None:
             self.loads[k].wait()
             self.loads[k] = None
 
@@ -366,7 +368,8 @@
             for k in (left, right, scale):
                 if k is not None:
                     self.ready(k)
-            x, made = self.held[left], self.made[out]
+            known = [*self.held, *self.made]
+            x, made = known[left], self.made[out]
             if kind == "sum":
                 rows = min(128, x.shape[0])
                 made[...] = jnp.zeros_like(made)
@@ -379,7 +382,7 @@
                 lax.fori_loop(0, x.shape[0] // rows, add, 0)
                 self.stores.append(self.sems.copy(made, self.outs[out]))
                 continue
-            y = self.held[right]
+            y = known[right]
             factor = None if scale is None else self.held[scale]
             tile_r, tile_c = min(512, made.shape[0]), min(512, made.shape[1])
             columns = made.shape[1] // tile_c
@@ -388,7 +391,12 @@
                 i, j = k // columns, lax.rem(k, columns)
                 r = pl.ds(pl.multiple_of(i * tile_r, tile_r), tile_r)
                 c = pl.ds(pl.multiple_of(j * tile_c, tile_c), tile_c)
-                total = tn(x[:, r], y[:, c]) if kind == "tn" else nn(x[r, :], y[:, c])
+                if kind == "tn":
+                    total = tn(x[:, r], y[:, c])
+                elif kind == "nt":
+                    total = nt(x[r, :], y[c, :])
+                else:
+                    total = nn(x[r, :], y[:, c])
                 if factor is not None:
                     total = total * factor[r, c].astype(f32)
                 made[r, c] = total.astype(made.dtype)
@@ -460,7 +468,7 @@
             pltpu.SemaphoreType.DMA((locals_,)),
         ],
         compiler_params=pltpu.CompilerParams(
-            collective_id=cid, has_side_effects=True, vmem_limit_bytes=(56 if work else 32) * 2**20
+            collective_id=cid, has_side_effects=True, vmem_limit_bytes=(58 if work else 32) * 2**20
         ),
         cost_estimate=takes(time),
         name=name,
@@ -763,6 +771,48 @@
         ),
         name="project",
     )(x, weight, bias[None], scale[None])
+
+
+def products_kernel(split, left_ref, right_ref, other_ref, last_ref, o_ref):
+    tile = min(512, o_ref.shape[0])
+
+    def fill(x_ref, y_ref):
+        def step(k, _):
+            rows = pl.ds(pl.multiple_of(k * tile, tile), tile)
+            o_ref[rows, :] = tn(x_ref[:, rows], y_ref[...]).astype(o_ref.dtype)
+            return 0
+
+        lax.fori_loop(0, o_ref.shape[0] // tile, step, 0)
+
+    @pl.when(pl.program_id(0) < split)
+    def _():
+        fill(left_ref, right_ref)
+
+    @pl.when(pl.program_id(0) >= split)
+    def _():
+        fill(other_ref, last_ref)
+
+
+def two_products(left, right, other, last):
+    rows, depth = left.shape
+    width = last.shape[1]
+    split = right.shape[1] // width
+    whole = pl.BlockSpec((rows, depth), lambda j: (0, 0))
+    return pl.pallas_call(
+        functools.partial(products_kernel, split),
+        out_shape=jax.ShapeDtypeStruct((depth, right.shape[1] + width), bf16),
+        grid=(split + 1,),
+        in_specs=[
+            whole,
+            pl.BlockSpec((rows, width), lambda j: (0, jnp.minimum(j, split - 1))),
+            whole,
+            pl.BlockSpec((rows, width), lambda j: (0, 0)),
+        ],
+        out_specs=pl.BlockSpec((depth, width), lambda j: (0, j)),
+        compiler_params=pltpu.CompilerParams(vmem_limit_bytes=48 * 2**20),
+        cost_estimate=takes(12),
+        name="two_products",
+    )(left, right, other, last)
 
 
 def permitted(first, limit, row, column):
@@ -1073,20 +1123,22 @@
     act = (pre_act * below).astype(bf16)
     slope = (below + pre_act * jnp.exp(-0.5 * pre_act * pre_act) * (2 * math.pi) ** -0.5).astype(bf16)
 
-    grad_w_down_t = tn(down_grad, act).astype(bf16)
-    grad_w_down_t, act, w_down_t = lax.optimization_barrier((grad_w_down_t, act, w_down_t))
-    shared_down = share(grad_w_down_t)
     ffn_part = nt(act, w_down_t).astype(bf16).reshape(tps, own, width)
-    ffn_out, up_grad = transfer(
+    ffn_out, up_grad, mid_part, grad_w_down_t = transfer(
         [Scatter(ffn_part)],
         8,
-        Work([down_grad, w_down_t, slope], [("nn", 0, 1, 2, 0)], 1),
+        Work(
+            [down_grad, w_down_t, slope, w_up_all, act],
+            [("nn", 0, 1, 2, 0), ("nt", 5, 3, None, 1), ("tn", 0, 4, None, 2)],
+            1,
+        ),
         name="scatter_ffn",
     )
+    shared_down = share(grad_w_down_t)
     output = (inputs + live_own * (attn_out + ffn_out + b_down)).astype(bf16)
     output = output.reshape(bands, piece, width)
 
-    mid_part = nt(up_grad, w_up_all).astype(bf16).reshape(tps, own, width)
+    mid_part = mid_part.reshape(tps, own, width)
     mid_grad, output, grad_w_up, up_sums = transfer(
         [Scatter(mid_part), Swap(output)],
         9,
@@ -1100,27 +1152,26 @@
     attn_grad, output = lax.optimization_barrier((attn_grad, output))
     output = gather_later(output)
 
-    grad_w_out_t = tn(attn_grad, mixed).astype(bf16)
     mixed_grad = nn(attn_grad, w_out_t).astype(bf16)
     mixed_grad = swap_heads(mixed_grad, group, 13, "cut").reshape(length, features)
     mixed_grad = nn(to_sorted, mixed_grad).astype(bf16)
+    mixed_grad, grad_w_up = lax.optimization_barrier((mixed_grad, grad_w_up))
     grad_w_up, shared_down = lax.optimization_barrier((grad_w_up, shared_down))
     shared_up = share(grad_w_up)
-    mixed_grad, grad_w_out_t = lax.optimization_barrier((mixed_grad, grad_w_out_t))
     in_grad, in_sums = attend_back(
         qkv, mixed_sorted, mixed_grad, log_total, info, first, block, half_block
     )
     in_sums = in_sums.transpose(1, 0, 2).reshape(8, features)
     mine = (jnp.arange(group) == member).astype(f32)[:, None]
-    in_grad, output = lax.optimization_barrier((in_grad, output))
-    output = output.transpose(1, 0, 2, 3).reshape(tokens.shape)
     in_grad = nn(to_rows, in_grad).astype(bf16).reshape(group, rows, 3 * features)
     in_grad = swap_heads(in_grad, group, 14, "join")
     in_part = nt(in_grad, w_in).astype(bf16).reshape(tps, bands, piece, width)
     in_part, in_grad = lax.optimization_barrier((in_part, in_grad))
-    grad_w_in = tn(z1, in_grad).astype(bf16)
-    grad_w_in_out = jnp.concatenate([grad_w_in, grad_w_out_t], axis=1)
-    grad_w_in_out, shared_up, in_part = lax.optimization_barrier((grad_w_in_out, shared_up, in_part))
+    grad_w_in_out = two_products(z1, in_grad, attn_grad, mixed)
+    grad_w_in_out, shared_up, in_part, output = lax.optimization_barrier(
+        (grad_w_in_out, shared_up, in_part, output)
+    )
+    output = output.transpose(1, 0, 2, 3).reshape(tokens.shape)
     shared_in_out = share(grad_w_in_out)
 
     def over_rows(array):

time: 726 us -> 707 us (0.974)
  matrix products: 129 us -> 79 us
  Pallas kernels: 441 us -> 478 us
  local copies, waits for them, and re-layouts: 58 us -> 48.7 us
    dot_general x3 -> x0, matrix products: 36.5 us -> none  [tn(): lax.dot_general(left, right, (((0,), (0,)), ((), ())), preferred_element_...]
    all_to_all x2, waiting for transfers between devices: 25.4 us -> 0.01 us  [gather_later(): lax.all_to_all(jnp.broadcast_to(x[None], (count,) + x.shape), 'tp', 0, 0)]
    reduce_scatter x3, waiting for transfers between devices: 1.51 us -> 23.6 us  [share(): return lax.psum_scatter(grad, 'band', scatter_dimension=0, tiled=True)]
    pallas_call x0 -> x1, Pallas kernels: none -> 17.5 us  [two_products(): pl.pallas_call(functools.partial(products_kernel, split), out_shape=jax.S...]
    dot_general x4 -> x3, matrix products: 42.4 us -> 30.6 us  [nt(): lax.dot_general(left, right, (((1,), (1,)), ((), ())), preferred_element_...]
    pallas_call x7, Pallas kernels: 294 us -> 305 us  [transfer(): pl.pallas_call(kernel, out_shape=tuple((shape for item in items for shape...]
    concatenate x1 -> x0, other arithmetic: 7.91 us -> none  [body(): grad_w_in_out = jnp.concatenate([grad_w_in, grad_w_out_t], axis=1)]
    all_gather x1, waiting for transfers between devices: 0.01 us -> 7.71 us  [body(): w_down_t = lax.all_gather(w_down.T, 'band', axis=0, tiled=True)]
  transfers between devices with their start and end apart: 8 -> 8, of which waited for: 3 -> 3; matrix products, arithmetic and copies ran while one was open for 26% -> 16% of each run, Pallas kernels for 61% -> 63%
where the time goes in v3:
time: 707 us; the launch traced here: 694 us
  Pallas kernels  478 us (68%)
  matrix products  79 us (11%)
  local copies, waits for them, and re-layouts  48.7 us (7%)
  waiting for transfers between devices  32.1 us (5%)
  other arithmetic  31.1 us (4%)
  between operations  15.5 us (2%)
  starting transfers between devices  10.2 us (1%)
    pallas_call x7, Pallas kernels, transfer(): pl.pallas_call(kernel, out_shape=tuple((shape for item in items for shape...  305 us
    pallas_call x1, Pallas kernels, finish(): pl.pallas_call(functools.partial(finish_kernel, count, size), out_shape=(...  94.3 us
    dot_general x6, matrix products, nn(): return jnp.dot(left, right, preferred_element_type=f32)  48.4 us
    unnamed x134, local copies, waits for them, and re-layouts  34.6 us
    dot_general x3, matrix products, nt(): lax.dot_general(left, right, (((1,), (1,)), ((), ())), preferred_element_...  30.6 us
    reduce_scatter x3, waiting for transfers between devices, share(): return lax.psum_scatter(grad, 'band', scatter_dimension=0, tiled=True)  23.6 us
    pallas_call x1, Pallas kernels, attend_back(): pl.pallas_call(functools.partial(attend_back_kernel, qb, kb), out_shape=(...  21.5 us
    pallas_call x1, Pallas kernels, two_products(): pl.pallas_call(functools.partial(products_kernel, split), out_shape=jax.S...  17.5 us
  transfers between devices with their start and end apart: 8, of which 3 were waited for; matrix products, arithmetic and copies ran while one was open for 16% of the time, Pallas kernels for 63%

profile of v3, /device:TPU:9, one launch (start us, length us, event | category | flops | bytes accessed | tf_op | source)
XLA Modules:
  0.0 694.5 jit_solution(9363905566428673301)
XLA Ops:
  14.8 59.2 %swap_in.1 = (bf16[8,32,2048]{2,1,0:T(8,128)(2,1)S(1)}, s32[8,4,256]{2,1,0:T(4,128)S(1)}) custom-call(bf16[8,32,2048]{2,1,0:T(8,128)(2,1)S(1)} %bitcast.126, s32[4,256]{1,0:T(4,128)S(1)} %copy-done.12), custom_call_target="tpu_custom_call" | custom-call | flops 35999997952 | bytes 72000000 | tf_op jit(solution)/shard_map/swap_in/pallas_call | solution.py:459
  79.9 47.1 %gather_in.1 = (bf16[4,256,2048]{2,1,0:T(8,128)(2,1)S(1)}, bf16[8,32,2048]{2,1,0:T(8,128)(2,1)S(1)}) custom-call(bf16[256,2048]{1,0:T(8,128)(2,1)S(1)} %fusion.28.refs_0_, bf16[8,32,2048]{2,1,0:T(8,128)(2,1)S(1)} %bitcast.125), custom_call_target="tpu_custom_call" | custom-call | flops 35999997952 | bytes 72000000 | tf_op jit(solution)/shard_map/gather_in/pallas_call | solution.py:459
  132.8 5.0 all-to-all-start
  143.0 11.2 %project.1.x_ref = bf16[2,1024,768]{2,1,0:T(8,128)(2,1)S(1)} custom-call(bf16[1024,2048]{1,0:T(8,128)(2,1)S(1)} %bitcast.131, bf16[2048,2048]{1,0:T(8,128)(2,1)} %all-gather.4.cloned.1.call-done.w_ref, f32[1,1536]{1,0:T(1,128)S(1)} %broadcast_in_dim_reshape.2.bias_ref, f32[1,1536]{1,0:T(1,128)S(1)} %copy-done.17), custom_call_target="tpu_custom_call" | custom-call | flops 6442450944 | bytes 12582912 | tf_op jit(solution)/shard_map/project/pallas_call | solution.py:757
  155.8 3.8 swap_heads.4
  159.6 9.4 %fusion.19.q_ref.k_ref.v_ref = bf16[2048,768]{1,0:T(8,128)(2,1)S(1)} fusion(bf16[2048,768]{1,0:T(8,128)(2,1)} %bitcast.174, s32[2048]{0:T(1024)S(1)} %eq.38), kind=kOutput, calls=%fused_computation.24 | convolution fusion | flops 6448218112 | bytes 6299648 | tf_op jit(solution)/shard_map/dot_general | solution.py:38
  169.1 15.8 %attend.1 = (bf16[2048,256]{1,0:T(8,128)(2,1)S(1)}, f32[1,8,2048]{2,1,0:T(8,128)S(1)}) custom-call(s32[5]{0:T(128)S(1)} %pad_add_fusion.info_ref, s32[1,2048]{1,0:T(1,128)S(1)} %bitcast.128, bf16[2048,768]{1,0:T(8,128)(2,1)S(1)} %fusion.19.q_ref.k_ref.v_ref, bf16[2048,768]{1,0:T(8,128)(2,1)S(1)} %fusion.19.q_ref.k_ref.v_ref, ...), custom_call_target="tpu_custom_call" | custom-call | flops 30000001024 | bytes 60000000 | tf_op jit(solution)/shard_map/attend/pallas_call | solution.py:980
  186.5 3.8 fusion.20
  192.6 4.3 convolution_convert_fusion.1
  197.0 37.5 %scatter_attn.1 = f32[256,2048]{1,0:T(8,128)S(1)} custom-call(bf16[4,256,2048]{2,1,0:T(8,128)(2,1)S(1)} %bitcast.136), custom_call_target="tpu_custom_call" | custom-call | flops 35999997952 | bytes 72000000 | tf_op jit(solution)/shard_map/scatter_attn/pallas_call | solution.py:459
  237.2 35.2 %gather_mid.1 = bf16[4,256,2048]{2,1,0:T(8,128)(2,1)S(1)} custom-call(bf16[256,2048]{1,0:T(8,128)(2,1)S(1)} %add_convert_fusion.1.refs_0_), custom_call_target="tpu_custom_call" | custom-call | flops 35999997952 | bytes 72000000 | tf_op jit(solution)/shard_map/gather_mid/pallas_call | solution.py:459
  274.4 17.2 %fusion.8 = (bf16[1024,2048]{1,0:T(8,128)(2,1)}, bf16[1024,2048]{1,0:T(8,128)(2,1)}) fusion(f32[2048]{0:T(1024)S(1)} %copy-done.54, bf16[1024,2048]{1,0:T(8,128)(2,1)} %bitcast.134, bf16[2048,2048]{1,0:T(8,128)(2,1)} %all-gather.6.cloned.1.call-done.refs_4_), kind=kOutput, calls=%fused_computation.11 | convolution fusion | flops 8615100416 | bytes 20979712 | tf_op jit(solution)/shard_map/dot_general | solution.py:38
  291.6 7.7 %all-gather.8.cloned.1.call-done.refs_2_ = bf16[2048,2048]{1,0:T(8,128)(2,1)} async-done(((bf16[256,2048]{1,0:T(8,128)(2,1)}), bf16[2048,2048]{1,0:T(8,128)(2,1)}) %all-gather.8.cloned.1.call-update) | async-done | bytes 8388624 | tf_op jit(solution)/shard_map/all_gather | solution.py:1070
  299.3 14.3 %convolution_convert_fusion = bf16[1024,2048]{1,0:T(8,128)(2,1)} fusion(bf16[1024,2048]{1,0:T(8,128)(2,1)} %get-tuple-element.197.refs_5_, bf16[2048,2048]{1,0:T(8,128)(2,1)} %all-gather.8.cloned.1.call-done.refs_2_), kind=kOutput, calls=%fused_computation.21 | convolution fusion | flops 8592031744 | bytes 16777216 | tf_op jit(solution)/shard_map/dot_general | solution.py:42
  313.6 43.3 %scatter_ffn.1 = (f32[256,2048]{1,0:T(8,128)}, bf16[1024,2048]{1,0:T(8,128)(2,1)}, bf16[1024,2048]{1,0:T(8,128)(2,1)}, bf16[2048,2048]{1,0:T(8,128)(2,1)}) custom-call(bf16[4,256,2048]{2,1,0:T(8,128)(2,1)} %bitcast.172, bf16[1024,2048]{1,0:T(8,128)(2,1)} %bitcast.25.refs_1_, bf16[2048,2048]{1,0:T(8,128)(2,1)} %all-gather.8.cloned.1.call-done.refs_2_, ...), custom_call_target="tpu_custom_call" | custom-call | flops 35999997952 | bytes 72000000 | tf_op jit(solution)/shard_map/scatter_ffn/pallas_call | solution.py:459
  357.7 3.3 fusion.29
  361.0 46.8 %scatter_mid.1 = (f32[256,2048]{1,0:T(8,128)}, bf16[8,32,2048]{2,1,0:T(8,128)(2,1)}, bf16[2048,2048]{1,0:T(8,128)(2,1)}, f32[1,2048]{1,0:T(1,128)}) custom-call(bf16[4,256,2048]{2,1,0:T(8,128)(2,1)} %bitcast.171, bf16[8,32,2048]{2,1,0:T(8,128)(2,1)} %bitcast.148, bf16[1024,2048]{1,0:T(8,128)(2,1)} %bitcast.135, bf16[1024,2048]{1,0:T(8,128)(2,1)} %get-tuple-element.59.refs_3_), custom_call_target="tpu_custom_call" | custom-call | flops 35999997952 | bytes 72000000 | tf_op jit(solution)/shard_map/scatter_mid/pallas_call | solution.py:459
  407.9 2.7 multiply_reduce_fusion
  412.9 36.4 %gather_back.1 = bf16[4,256,2048]{2,1,0:T(8,128)(2,1)S(1)} custom-call(bf16[256,2048]{1,0:T(8,128)(2,1)S(1)} %get-tuple-element.190.refs_0_), custom_call_target="tpu_custom_call" | custom-call | flops 35999997952 | bytes 72000000 | tf_op jit(solution)/shard_map/gather_back/pallas_call | solution.py:459
  451.4 4.9 fusion.34.x_ref
  458.6 4.4 fusion.21.do_ref
  463.0 5.8 reduce-scatter.4.cloned.1.call-done
  471.5 5.0 all-to-all-start.1
  476.5 21.5 %attend_back.1 = (bf16[2048,768]{1,0:T(8,128)(2,1)S(1)}, f32[1,8,256]{2,1,0:T(8,128)S(1)}) custom-call(s32[5]{0:T(128)S(1)} %pad_add_fusion.info_ref, s32[1,2048]{1,0:T(1,128)S(1)} %bitcast.129, bf16[2048,768]{1,0:T(8,128)(2,1)} %copy-done.23, bf16[2048,768]{1,0:T(8,128)(2,1)} %copy-done.23, bf16[2048,768]{1,0:T(8,128)(2,1)} %copy-done.23, ...), custom_call_target="tpu_custom_call" | custom-call | flops 33999998976 | bytes 68000000 | tf_op jit(solution)/shard_map/attend_back/pallas_call | solution.py:1002
  498.1 8.7 %fusion.18 = bf16[2048,768]{1,0:T(8,128)(2,1)} fusion(bf16[2048,768]{1,0:T(8,128)(2,1)S(1)} %get-tuple-element.66, s32[2048]{0:T(1024)S(1)} %copy-done.50), kind=kOutput, calls=%fused_computation.23 | convolution fusion | flops 6448218112 | bytes 6299648 | tf_op jit(solution)/shard_map/dot_general | solution.py:38
  506.7 3.8 swap_heads.7.right_ref
  510.6 11.9 %fusion.15 = bf16[1024,2048]{1,0:T(8,128)(2,1)} fusion(bf16[1024,1536]{1,0:T(8,128)(2,1)} %swap_heads.7.right_ref, bf16[2048,2048]{1,0:T(8,128)(2,1)} %all-gather.4.cloned.1.call-done.w_ref), kind=kOutput, calls=%fused_computation.20 | convolution fusion | flops 6444548096 | bytes 13631488 | tf_op jit(solution)/shard_map/dot_general | solution.py:42
  522.5 17.5 %two_products.1 = bf16[2048,2048]{1,0:T(8,128)(2,1)} custom-call(bf16[1024,2048]{1,0:T(8,128)(2,1)} %bitcast.130, bf16[1024,1536]{1,0:T(8,128)(2,1)S(1)} %copy-done.19, bf16[1024,2048]{1,0:T(8,128)(2,1)} %bitcast.133, bf16[1024,512]{1,0:T(8,128)(2,1)S(1)} %copy-done.20), custom_call_target="tpu_custom_call" | custom-call | flops 12000000000 | bytes 24000000 | tf_op jit(solution)/shard_map/two_products/pallas_call | solution.py:801
  540.0 17.8 %reduce-scatter.6.cloned.1.call-done = bf16[256,2048]{1,0:T(8,128)(2,1)} async-done(((bf16[2048,2048]{1,0:T(8,128)(2,1)}), bf16[256,2048]{1,0:T(8,128)(2,1)}) %reduce-scatter.6.cloned.1.call-update) | async-done | bytes 1048592 | tf_op jit(solution)/shard_map/reduce_scatter | solution.py:1064
  567.2 94.3 %finish.1 = (bf16[8,4,32,2048]{3,2,1,0:T(8,128)(2,1)}, f32[24,512]{1,0:T(8,128)S(1)}, f32[16,256]{1,0:T(8,128)S(1)}) custom-call(bf16[4,8,32,2048]{3,2,1,0:T(8,128)(2,1)} %bitcast.170, f32[8,32,2048]{2,1,0:T(8,128)S(1)} %copy-done.7, bf16[8,32,2048]{2,1,0:T(8,128)(2,1)S(1)} %copy-done.5, f32[8,32,2048]{2,1,0:T(8,128)S(1)} %bitcast.124, ...), custom_call_target="tpu_custom_call" | custom-call | flops 89999998976 | bytes 180000000 | tf_op jit(solution)/shard_map/finish/pallas_call | solution.py:657
  661.5 6.7 convert.47
  673.7 5.0 copy.119
  (211 shorter events, 67.8 us)
Async XLA Ops:
  7.2 132.5 %copy-start = (s32[4,4]{1,0:T(4,128)S(1)}, s32[4,4]{1,0:T(4,128)}, u32[]{:S(2)}) copy-start(s32[4,4]{1,0:T(4,128)} %param.22) | copy-start | bytes 196
  7.2 133.6 %all-gather.4.cloned.1.call-start = ((), (), s32[]{:S(2)}) async-start(), calls=%async_computation.5 | async-start | bytes 9437184 | tf_op jit(solution)/shard_map/all_gather | solution.py:1067
  12.2 262.2 %all-gather.6.cloned.1.call-start = ((), (), s32[]{:S(2)}) async-start(), calls=%async_computation.6 | async-start | bytes 9437184 | tf_op jit(solution)/shard_map/all_gather | solution.py:1069
  14.8 64.6 %copy-start.8 = (f32[2048]{0:T(1024)S(1)}, f32[2048]{0:T(1024)}, u32[]{:S(2)}) copy-start(f32[2048]{0:T(1024)} %param.35) | copy-start | bytes 24580
  14.8 64.6 %copy-start.46 = (f32[2048]{0:T(1024)S(1)}, f32[2048]{0:T(1024)}, u32[]{:S(2)}) copy-start(f32[2048]{0:T(1024)} %param.36) | copy-start | bytes 24580
  74.0 283.1 %copy-start.2 = (bf16[8,32,2048]{2,1,0:T(8,128)(2,1)}, bf16[8,32,2048]{2,1,0:T(8,128)(2,1)S(1)}, u32[]{:S(2)}) copy-start(bf16[8,32,2048]{2,1,0:T(8,128)(2,1)S(1)} %get-tuple-element.50) | copy-start | bytes 3145732
  74.3 52.7 %copy-start.33 = (f32[8,32]{1,0:T(8,128)}, f32[8,32]{1,0:T(8,128)S(1)}, u32[]{:S(2)}) copy-start(f32[8,32]{1,0:T(8,128)S(1)} %broadcast_multiply_fusion) | copy-start | bytes 3076
  75.4 51.6 %copy-start.35 = (f32[8,32]{1,0:T(8,128)}, f32[8,32]{1,0:T(8,128)S(1)}, u32[]{:S(2)}) copy-start(f32[8,32]{1,0:T(8,128)S(1)} %get-tuple-element.212) | copy-start | bytes 3076
  79.4 49.6 %copy-start.44 = (f32[256]{0:T(256)}, f32[256]{0:T(256)S(1)}, u32[]{:S(2)}) copy-start(f32[256]{0:T(256)S(1)} %reshape.357) | copy-start | bytes 3076
  132.8 53.7 %all-to-all-start = ((bf16[4,256,2048]{2,1,0:T(8,128)(2,1)}), bf16[4,256,2048]{2,1,0:T(8,128)(2,1)}, u32[]{:S(2)}, u32[]{:S(2)}) async-start(bf16[4,256,2048]{2,1,0:T(8,128)(2,1)} %broadcast_in_dim.23), calls=%async_computation | async-start | bytes 8388608 | tf_op jit(solution)/shard_map/all_to_all | solution.py:480
  137.8 161.5 %all-gather.8.cloned.1.call-start = ((), (), s32[]{:S(2)}) async-start(), calls=%async_computation.7 | async-start | bytes 9437184 | tf_op jit(solution)/shard_map/all_gather | solution.py:1070
  139.4 329.5 %reduce-scatter.4.cloned.1.call-start = ((), (), s32[]{:S(2)}) async-start(), calls=%async_computation.8 | async-start | bytes 9437184 | tf_op jit(solution)/shard_map/reduce_scatter | solution.py:1064
  139.5 47.0 %copy-start.49 = (s32[2048]{0:T(1024)}, s32[2048]{0:T(1024)S(1)}, u32[]{:S(2)}) copy-start(s32[2048]{0:T(1024)S(1)} %eq.38) | copy-start | bytes 24580
  140.0 29.1 %copy-start.10 = (s32[2048]{0:T(1024)}, s32[2048]{0:T(1024)S(1)}, u32[]{:S(2)}) copy-start(s32[2048]{0:T(1024)S(1)} %select_reduce_fusion) | copy-start | bytes 24580
  196.9 37.5 %copy-start.37 = (f32[2048]{0:T(1024)S(1)}, f32[2048]{0:T(1024)}, u32[]{:S(2)}) copy-start(f32[2048]{0:T(1024)} %param.32) | copy-start | bytes 24580
  237.2 37.3 %copy-start.54 = (f32[2048]{0:T(1024)S(1)}, f32[2048]{0:T(1024)}, u32[]{:S(2)}) copy-start(f32[2048]{0:T(1024)} %param.33) | copy-start | bytes 24580
  357.0 200.7 %reduce-scatter.6.cloned.1.call-start = ((), (), s32[]{:S(2)}) async-start(), calls=%async_computation.9 | async-start | bytes 9437184 | tf_op jit(solution)/shard_map/reduce_scatter | solution.py:1064
  361.0 46.8 %copy-start.25 = (f32[256,2048]{1,0:T(8,128)S(1)}, f32[256,2048]{1,0:T(8,128)}, u32[]{:S(2)}) copy-start(f32[256,2048]{1,0:T(8,128)} %copy-done.24) | copy-start | bytes 6291460
  361.0 46.9 %copy-start.32 = (f32[2048]{0:T(1024)S(1)}, f32[2048]{0:T(1024)}, u32[]{:S(2)}) copy-start(f32[2048]{0:T(1024)} %param.37) | copy-start | bytes 24580
  361.0 46.9 %copy-start.39 = (f32[256]{0:T(256)S(1)}, f32[256]{0:T(256)}, u32[]{:S(2)}) copy-start(f32[256]{0:T(256)} %copy-done.38) | copy-start | bytes 3076
  361.0 46.9 %copy-start.41 = (f32[256]{0:T(256)S(1)}, f32[256]{0:T(256)}, u32[]{:S(2)}) copy-start(f32[256]{0:T(256)} %copy-done.40) | copy-start | bytes 3076
  463.0 5.9 copy-start.28
  471.5 68.5 %all-to-all-start.1 = ((bf16[4,8,32,2048]{3,2,1,0:T(8,128)(2,1)}), bf16[4,8,32,2048]{3,2,1,0:T(8,128)(2,1)}, u32[]{:S(2)}, u32[]{:S(2)}) async-start(bf16[4,8,32,2048]{3,2,1,0:T(8,128)(2,1)} %broadcast_in_dim.24), calls=%async_computation.3 | async-start | bytes 8388608 | tf_op jit(solution)/shard_map/all_to_all | solution.py:480
  476.5 203.7 %reduce-scatter.8.cloned.1.call-start = ((), (), s32[]{:S(2)}) async-start(), calls=%async_computation.10 | async-start | bytes 9437184 | tf_op jit(solution)/shard_map/reduce_scatter | solution.py:1064
  510.5 11.9 %copy-start.19 = (bf16[1024,1536]{1,0:T(8,128)(2,1)S(1)}, bf16[1024,1536]{1,0:T(8,128)(2,1)}, u32[]{:S(2)}) copy-start(bf16[1024,1536]{1,0:T(8,128)(2,1)} %swap_heads.7.right_ref) | copy-start | bytes 9437188
  510.5 11.9 %copy-start.20 = (bf16[1024,512]{1,0:T(8,128)(2,1)S(1)}, bf16[1024,512]{1,0:T(8,128)(2,1)}, u32[]{:S(2)}) copy-start(bf16[1024,512]{1,0:T(8,128)(2,1)} %swap_heads.5.last_ref) | copy-start | bytes 3145732
  539.9 17.9 %copy-start.42 = (f32[8,1,1,32]{3,2,1,0:T(1,128)S(1)}, f32[8,1,1,32]{3,2,1,0:T(1,128)}, u32[]{:S(2)}) copy-start(f32[8,1,1,32]{3,2,1,0:T(1,128)} %get-tuple-element.195) | copy-start | bytes 3076
  539.9 18.2 %copy-start.43 = (f32[8,32,1]{1,0,2:T(8,128)S(1)}, f32[8,32,1]{1,0,2:T(8,128)}, u32[]{:S(2)}) copy-start(f32[8,32,1]{1,0,2:T(8,128)} %get-tuple-element.211) | copy-start | bytes 3076
  539.9 18.3 %copy-start.3 = (bf16[8,32,2048]{2,1,0:T(8,128)(2,1)S(1)}, bf16[8,32,2048]{2,1,0:T(8,128)(2,1)}, u32[]{:S(2)}) copy-start(bf16[8,32,2048]{2,1,0:T(8,128)(2,1)} %copy-done.2) | copy-start | bytes 3145732
  539.9 18.3 %copy-start.34 = (f32[8,32]{1,0:T(8,128)S(1)}, f32[8,32]{1,0:T(8,128)}, u32[]{:S(2)}) copy-start(f32[8,32]{1,0:T(8,128)} %copy-done.33) | copy-start | bytes 3076
  539.9 18.3 %copy-start.36 = (f32[8,32]{1,0:T(8,128)S(1)}, f32[8,32]{1,0:T(8,128)}, u32[]{:S(2)}) copy-start(f32[8,32]{1,0:T(8,128)} %copy-done.35) | copy-start | bytes 3076
  682.0 5.2 copy-start.1
  (31 other events, 75.5 us)
Sparse Core Ops, SparseCore 0:
  12.4 119.3 all-gather.3
  133.4 83.1 all-gather.5
  218.7 80.5 all-gather.7
  357.2 111.6 reduce-scatter.3
  471.0 86.7 reduce-scatter.5
  559.9 117.7 reduce-scatter.7

commit v4 on v3

--- a/solution.py
+++ b/solution.py
@@ -475,9 +475,10 @@
     )(*(operand for item in items for operand in item.operands))
 
 
-def gather_later(x):
-    count = lax.axis_size("tp")
-    return lax.all_to_all(jnp.broadcast_to(x[None], (count,) + x.shape), "tp", 0, 0)
+def gather_later(x, axis=0):
+    x = jnp.expand_dims(x, axis)
+    copies = jnp.broadcast_to(x, x.shape[:axis] + (lax.axis_size("tp"),) + x.shape[axis + 1 :])
+    return lax.all_to_all(copies, "tp", axis, axis)
 
 
 class Block:
@@ -741,6 +742,89 @@
     )(x)
 
 
+def settle_kernel(
+    wides, grad_ref, out_ref, up_ref, down_ref, wide_ref, narrow_ref,
+    grad_to, out_to, up_to, down_to, *small,
+):
+    grad_to[...] = grad_ref[...].astype(f32)
+    out_to[0] = out_ref[:, 0]
+    up_to[...] = up_ref[...].astype(f32)
+    down_to[...] = down_ref[...].astype(f32).T
+
+    @pl.when(pl.program_id(0) == 0)
+    def _():
+        for refs, source in ((small[:wides], wide_ref), (small[wides:], narrow_ref)):
+            lanes, row = source.shape[1], 0
+            for ref in refs:
+                for i in range(ref.shape[1] // lanes):
+                    ref[0:1, i * lanes : (i + 1) * lanes] = source[row : row + 1, :]
+                    row += 1
+
+
+def settle(grad, out, up, down, wide, narrow, widths):
+    size, count, rows, width = grad.shape
+    wides = wide.shape[0] * wide.shape[1] // width
+    slab = down.shape[1] // size
+    small = [width] * wides + list(widths)
+    block = pl.BlockSpec((1, count, rows, width), lambda i: (i, 0, 0, 0))
+    across = pl.BlockSpec((up.shape[0] // size, up.shape[1]), lambda i: (i, 0))
+    if up.shape[0] // size % 16:
+        across = pl.BlockSpec(up.shape, lambda i: (0, 0))
+    return pl.pallas_call(
+        functools.partial(settle_kernel, wides),
+        out_shape=(
+            jax.ShapeDtypeStruct(grad.shape, f32),
+            jax.ShapeDtypeStruct(grad.shape, out.dtype),
+            jax.ShapeDtypeStruct(up.shape, f32),
+            jax.ShapeDtypeStruct(down.shape[::-1], f32),
+            *(jax.ShapeDtypeStruct((1, n), f32) for n in small),
+        ),
+        grid=(size,),
+        in_specs=[
+            block,
+            pl.BlockSpec((count, 1, rows, width), lambda i: (0, i, 0, 0)),
+            across,
+            pl.BlockSpec((down.shape[0], slab), lambda i: (0, i)) if slab % 128 == 0 else vmem,
+            pl.BlockSpec(wide.shape, lambda i: (0, 0)),
+            pl.BlockSpec(narrow.shape, lambda i: (0, 0)),
+        ],
+        out_specs=(
+            block,
+            block,
+            across,
+            pl.BlockSpec((slab, down.shape[0]), lambda i: (i, 0)) if slab % 128 == 0 else vmem,
+            *(pl.BlockSpec((1, n), lambda i: (0, 0)) for n in small),
+        ),
+        compiler_params=pltpu.CompilerParams(vmem_limit_bytes=40 * 2**20),
+        cost_estimate=takes(10),
+        name="settle",
+    )(grad, out, up, down, wide, narrow)
+
+
+def split_kernel(group, features, x_ref, q_ref, k_ref, v_ref, out_ref):
+    for g in range(group):
+        for which, ref in enumerate((q_ref, k_ref, v_ref)):
+            start = (3 * g + which) * features
+            ref[:, g * features : (g + 1) * features] = x_ref[:, start : start + features].astype(f32)
+    out_ref[...] = x_ref[:, 3 * group * features :].astype(f32).T
+
+
+def split_shared(x, group, features):
+    rows, inner = x.shape[0], group * features
+    return pl.pallas_call(
+        functools.partial(split_kernel, group, features),
+        out_shape=(
+            *[jax.ShapeDtypeStruct((rows, inner), f32)] * 3,
+            jax.ShapeDtypeStruct((x.shape[1] - 3 * inner, rows), f32),
+        ),
+        in_specs=[vmem],
+        out_specs=(vmem,) * 4,
+        compiler_params=pltpu.CompilerParams(vmem_limit_bytes=32 * 2**20),
+        cost_estimate=takes(2),
+        name="split_shared",
+    )(x)
+
+
 def project_kernel(x_ref, w_ref, bias_ref, scale_ref, o_ref):
     total = nn(x_ref[...], w_ref[...]) + bias_ref[...]
     o_ref[0] = total.astype(bf16) * scale_ref[...].astype(bf16)
@@ -773,42 +857,34 @@
     )(x, weight, bias[None], scale[None])
 
 
-def products_kernel(split, left_ref, right_ref, other_ref, last_ref, o_ref):
-    tile = min(512, o_ref.shape[0])
-
-    def fill(x_ref, y_ref):
-        def step(k, _):
-            rows = pl.ds(pl.multiple_of(k * tile, tile), tile)
-            o_ref[rows, :] = tn(x_ref[:, rows], y_ref[...]).astype(o_ref.dtype)
-            return 0
-
-        lax.fori_loop(0, o_ref.shape[0] // tile, step, 0)
-
-    @pl.when(pl.program_id(0) < split)
-    def _():
-        fill(left_ref, right_ref)
-
-    @pl.when(pl.program_id(0) >= split)
-    def _():
-        fill(other_ref, last_ref)
+def products_kernel(left_ref, right_ref, other_ref, last_ref, o_ref):
+    tile, width = last_ref.shape[1], right_ref.shape[1]
+
+    def step(k, _):
+        columns = pl.ds(pl.multiple_of(k * tile, tile), tile)
+        o_ref[:, columns] = tn(left_ref[...], right_ref[:, columns]).astype(o_ref.dtype)
+        return 0
+
+    lax.fori_loop(0, width // tile, step, 0)
+    o_ref[:, width:] = tn(other_ref[...], last_ref[...]).astype(o_ref.dtype)
 
 
 def two_products(left, right, other, last):
     rows, depth = left.shape
-    width = last.shape[1]
-    split = right.shape[1] // width
-    whole = pl.BlockSpec((rows, depth), lambda j: (0, 0))
+    width, more = right.shape[1], last.shape[1]
+    tile = min(512, depth)
+    cut = pl.BlockSpec((rows, tile), lambda i: (0, i))
     return pl.pallas_call(
-        functools.partial(products_kernel, split),
-        out_shape=jax.ShapeDtypeStruct((depth, right.shape[1] + width), bf16),
-        grid=(split + 1,),
+        products_kernel,
+        out_shape=jax.ShapeDtypeStruct((depth, width + more), bf16),
+        grid=(depth // tile,),
         in_specs=[
-            whole,
-            pl.BlockSpec((rows, width), lambda j: (0, jnp.minimum(j, split - 1))),
-            whole,
-            pl.BlockSpec((rows, width), lambda j: (0, 0)),
+            cut,
+            pl.BlockSpec((rows, width), lambda i: (0, 0)),
+            cut,
+            pl.BlockSpec((rows, more), lambda i: (0, 0)),
         ],
-        out_specs=pl.BlockSpec((depth, width), lambda j: (0, j)),
+        out_specs=pl.BlockSpec((tile, width + more), lambda i: (i, 0)),
         compiler_params=pltpu.CompilerParams(vmem_limit_bytes=48 * 2**20),
         cost_estimate=takes(12),
         name="two_products",
@@ -1123,31 +1199,33 @@
     act = (pre_act * below).astype(bf16)
     slope = (below + pre_act * jnp.exp(-0.5 * pre_act * pre_act) * (2 * math.pi) ** -0.5).astype(bf16)
 
+    grad_w_down_t = tn(down_grad, act).astype(bf16)
+    grad_w_down_t, act = lax.optimization_barrier((grad_w_down_t, act))
+    shared_down = share(grad_w_down_t)
     ffn_part = nt(act, w_down_t).astype(bf16).reshape(tps, own, width)
-    ffn_out, up_grad, mid_part, grad_w_down_t = transfer(
+    ffn_out, up_grad, mid_part = transfer(
         [Scatter(ffn_part)],
         8,
         Work(
-            [down_grad, w_down_t, slope, w_up_all, act],
-            [("nn", 0, 1, 2, 0), ("nt", 5, 3, None, 1), ("tn", 0, 4, None, 2)],
+            [down_grad, w_down_t, slope, w_up_all],
+            [("nn", 0, 1, 2, 0), ("nt", 4, 3, None, 1)],
             1,
         ),
         name="scatter_ffn",
     )
-    shared_down = share(grad_w_down_t)
     output = (inputs + live_own * (attn_out + ffn_out + b_down)).astype(bf16)
     output = output.reshape(bands, piece, width)
 
     mid_part = mid_part.reshape(tps, own, width)
-    mid_grad, output, grad_w_up, up_sums = transfer(
-        [Scatter(mid_part), Swap(output)],
+    mid_grad, grad_w_up, up_sums = transfer(
+        [Scatter(mid_part)],
         9,
         Work([z2, up_grad], [("tn", 0, 1, None, 0), ("sum", 1, None, None, 1)], 1),
         name="scatter_mid",
     )
     resid_grad = norm_back(mid_grad, unit_mid, inverse_mid, ffn_gain)
     attn_grad_own = (live_own * grad_own + resid_grad).astype(bf16)
-    (attn_grad,) = transfer([Gather(attn_grad_own)], 10, name="gather_back")
+    attn_grad, output = transfer([Gather(attn_grad_own), Swap(output)], 10, name="gather_back")
     attn_grad = attn_grad.reshape(rows, width)
     attn_grad, output = lax.optimization_barrier((attn_grad, output))
     output = gather_later(output)
@@ -1155,7 +1233,6 @@
     mixed_grad = nn(attn_grad, w_out_t).astype(bf16)
     mixed_grad = swap_heads(mixed_grad, group, 13, "cut").reshape(length, features)
     mixed_grad = nn(to_sorted, mixed_grad).astype(bf16)
-    mixed_grad, grad_w_up = lax.optimization_barrier((mixed_grad, grad_w_up))
     grad_w_up, shared_down = lax.optimization_barrier((grad_w_up, shared_down))
     shared_up = share(grad_w_up)
     in_grad, in_sums = attend_back(
@@ -1165,14 +1242,12 @@
     mine = (jnp.arange(group) == member).astype(f32)[:, None]
     in_grad = nn(to_rows, in_grad).astype(bf16).reshape(group, rows, 3 * features)
     in_grad = swap_heads(in_grad, group, 14, "join")
+    in_grad, output = lax.optimization_barrier((in_grad, output))
+    grad_w_in_out = two_products(z1, in_grad, attn_grad, mixed)
+    grad_w_in_out, shared_up = lax.optimization_barrier((grad_w_in_out, shared_up))
+    shared_in_out = share(grad_w_in_out)
+    in_grad, grad_w_in_out = lax.optimization_barrier((in_grad, grad_w_in_out))
     in_part = nt(in_grad, w_in).astype(bf16).reshape(tps, bands, piece, width)
-    in_part, in_grad = lax.optimization_barrier((in_part, in_grad))
-    grad_w_in_out = two_products(z1, in_grad, attn_grad, mixed)
-    grad_w_in_out, shared_up, in_part, output = lax.optimization_barrier(
-        (grad_w_in_out, shared_up, in_part, output)
-    )
-    output = output.transpose(1, 0, 2, 3).reshape(tokens.shape)
-    shared_in_out = share(grad_w_in_out)
 
     def over_rows(array):
         return jnp.sum(array.astype(f32), axis=0)
@@ -1200,16 +1275,12 @@
         narrow,
         15,
     )
-    token_grad = token_grad.reshape(tokens.shape).astype(f32)
-    wide, late = wide[:16].reshape(4, width), wide[16:].reshape(2, width)
-    narrow = narrow.reshape(-1)[:count]
-    shared_in = shared_in_out[:, : 3 * inner].astype(f32).reshape(-1, group, 3, features)
-    shared_down, shared_out = shared_down.astype(f32).T, shared_in_out[:, 3 * inner :].astype(f32).T
-    shared_up = shared_up.astype(f32)
-    shared_q, shared_k, shared_v = (
-        shared_in[:, :, which].reshape(-1, inner) for which in range(3)
+    token_grad, output, shared_up, shared_down, *small = settle(
+        token_grad, output, shared_up, shared_down, wide, narrow, (inner, inner, b_up.shape[0])
     )
-
+    token_grad, output = token_grad.reshape(tokens.shape), output.reshape(tokens.shape)
+    small = [vector.reshape(-1) for vector in small]
+    shared_q, shared_k, shared_v, shared_out = split_shared(shared_in_out, group, features)
     return (
         output,
         token_grad,
@@ -1219,15 +1290,15 @@
         shared_out,
         shared_up,
         shared_down,
-        narrow[:inner],
-        narrow[inner : 2 * inner],
-        wide[0],
-        narrow[2 * inner :],
-        wide[1],
-        late[0],
-        late[1],
-        wide[2],
-        wide[3],
+        small[6],
+        small[7],
+        small[0],
+        small[8],
+        small[1],
+        small[4],
+        small[5],
+        small[2],
+        small[3],
     )
 
 

time: 707 us -> 687 us (0.972)
  matrix products: 79 us -> 103 us
  waiting for transfers between devices: 32.1 us -> 10.1 us
  local copies, waits for them, and re-layouts: 48.7 us -> 35.7 us
  other arithmetic: 31.1 us -> 19 us
    dot_general x0 -> x1, matrix products: none -> 24.4 us  [tn(): lax.dot_general(left, right, (((0,), (0,)), ((), ())), preferred_element_...]
    reduce_scatter x3, waiting for transfers between devices: 23.6 us -> 9.34 us  [share(): return lax.psum_scatter(grad, 'band', scatter_dimension=0, tiled=True)]
    pallas_call x7, Pallas kernels: 305 us -> 296 us  [transfer(): pl.pallas_call(kernel, out_shape=tuple((shape for item in items for shape...]
    convert_element_type x2 -> x0, other arithmetic: 8.28 us -> none  [the longest x1 6.73 us: body(): token_grad = token_grad.reshape(tokens.shape).astype(f32)]
    pallas_call x1 -> x3, Pallas kernels: 17.5 us -> 25.4 us  [the longest x1 14.8 us: two_products(): pl.pallas_call(products_kernel, out_shape=jax.ShapeDtypeStruct((depth, wi...]
    all_gather x1, waiting for transfers between devices: 7.71 us -> 0.02 us  [body(): w_down_t = lax.all_gather(w_down.T, 'band', axis=0, tiled=True)]
    unnamed x134 -> x129, local copies, waits for them, and re-layouts: 34.6 us -> 27.3 us
  transfers between devices with their start and end apart: 8 -> 8, of which waited for: 3 -> 2; matrix products, arithmetic and copies ran while one was open for 16% -> 19% of each run, Pallas kernels for 63% -> 71%
where the time goes in v4:
time: 687 us; the launch traced here: 676 us
  Pallas kernels  482 us (70%)
  matrix products  103 us (15%)
  local copies, waits for them, and re-layouts  35.7 us (5%)
  other arithmetic  19 us (3%)
  between operations  15.5 us (2%)
  starting transfers between devices  10.3 us (1%)
  waiting for transfers between devices  10.1 us (1%)
    pallas_call x7, Pallas kernels, transfer(): pl.pallas_call(kernel, out_shape=tuple((shape for item in items for shape...  296 us
    pallas_call x1, Pallas kernels, finish(): pl.pallas_call(functools.partial(finish_kernel, count, size), out_shape=(...  97.9 us
    dot_general x6, matrix products, nn(): return jnp.dot(left, right, preferred_element_type=f32)  49.2 us
    dot_general x3, matrix products, nt(): lax.dot_general(left, right, (((1,), (1,)), ((), ())), preferred_element_...  29.5 us
    unnamed x129, local copies, waits for them, and re-layouts  27.3 us
    dot_general x1, matrix products, tn(): lax.dot_general(left, right, (((0,), (0,)), ((), ())), preferred_element_...  24.4 us
    pallas_call x1, Pallas kernels, attend_back(): pl.pallas_call(functools.partial(attend_back_kernel, qb, kb), out_shape=(...  23.4 us
    pallas_call x1, Pallas kernels, attend(): pl.pallas_call(functools.partial(attend_kernel, qb, kb), out_shape=(jax.S...  15.9 us
  transfers between devices with their start and end apart: 8, of which 2 were waited for; matrix products, arithmetic and copies ran while one was open for 19% of the time, Pallas kernels for 71%

profile of v4, /device:TPU:9, one launch (start us, length us, event | category | flops | bytes accessed | tf_op | source)
XLA Modules:
  0.0 675.7 jit_solution(728260815775245862)
XLA Ops:
  14.8 59.2 %swap_in.1 = (bf16[8,32,2048]{2,1,0:T(8,128)(2,1)S(1)}, s32[8,4,256]{2,1,0:T(4,128)S(1)}) custom-call(bf16[8,32,2048]{2,1,0:T(8,128)(2,1)S(1)} %bitcast.99, s32[4,256]{1,0:T(4,128)S(1)} %copy-done.17), custom_call_target="tpu_custom_call" | custom-call | flops 35999997952 | bytes 72000000 | tf_op jit(solution)/shard_map/swap_in/pallas_call | solution.py:459
  79.9 47.1 %gather_in.1 = (bf16[4,256,2048]{2,1,0:T(8,128)(2,1)S(1)}, bf16[8,32,2048]{2,1,0:T(8,128)(2,1)S(1)}) custom-call(bf16[256,2048]{1,0:T(8,128)(2,1)S(1)} %fusion.28.refs_0_, bf16[8,32,2048]{2,1,0:T(8,128)(2,1)S(1)} %bitcast.98), custom_call_target="tpu_custom_call" | custom-call | flops 35999997952 | bytes 72000000 | tf_op jit(solution)/shard_map/gather_in/pallas_call | solution.py:459
  130.2 2.5 broadcast_in_dim.23
  132.8 5.0 all-to-all-start
  143.0 11.2 %project.1.x_ref = bf16[2,1024,768]{2,1,0:T(8,128)(2,1)S(1)} custom-call(bf16[1024,2048]{1,0:T(8,128)(2,1)S(1)} %bitcast.105, bf16[2048,2048]{1,0:T(8,128)(2,1)} %all-gather.4.cloned.1.call-done.w_ref, f32[1,1536]{1,0:T(1,128)S(1)} %broadcast_in_dim_reshape.2.bias_ref, f32[1,1536]{1,0:T(1,128)S(1)} %copy-done.22), custom_call_target="tpu_custom_call" | custom-call | flops 6442450944 | bytes 12582912 | tf_op jit(solution)/shard_map/project/pallas_call | solution.py:841
  155.8 3.8 swap_heads.4
  159.6 9.4 %fusion.19.q_ref.k_ref.v_ref = bf16[2048,768]{1,0:T(8,128)(2,1)S(1)} fusion(bf16[2048,768]{1,0:T(8,128)(2,1)} %bitcast.134, s32[2048]{0:T(1024)S(1)} %eq.38), kind=kOutput, calls=%fused_computation.25 | convolution fusion | flops 6448218112 | bytes 6299648 | tf_op jit(solution)/shard_map/dot_general | solution.py:38
  169.1 15.9 %attend.1 = (bf16[2048,256]{1,0:T(8,128)(2,1)S(1)}, f32[1,8,2048]{2,1,0:T(8,128)S(1)}) custom-call(s32[5]{0:T(128)S(1)} %pad_add_fusion.info_ref, s32[1,2048]{1,0:T(1,128)S(1)} %bitcast.102, bf16[2048,768]{1,0:T(8,128)(2,1)S(1)} %fusion.19.q_ref.k_ref.v_ref, bf16[2048,768]{1,0:T(8,128)(2,1)S(1)} %fusion.19.q_ref.k_ref.v_ref, ...), custom_call_target="tpu_custom_call" | custom-call | flops 30000001024 | bytes 60000000 | tf_op jit(solution)/shard_map/attend/pallas_call | solution.py:1056
  186.7 3.8 fusion.20
  192.8 4.3 convolution_convert_fusion.2
  197.1 37.5 %scatter_attn.1 = f32[256,2048]{1,0:T(8,128)S(1)} custom-call(bf16[4,256,2048]{2,1,0:T(8,128)(2,1)S(1)} %bitcast.110), custom_call_target="tpu_custom_call" | custom-call | flops 35999997952 | bytes 72000000 | tf_op jit(solution)/shard_map/scatter_attn/pallas_call | solution.py:459
  237.1 35.2 %gather_mid.1 = bf16[4,256,2048]{2,1,0:T(8,128)(2,1)S(1)} custom-call(bf16[256,2048]{1,0:T(8,128)(2,1)S(1)} %add_convert_fusion.1.refs_0_), custom_call_target="tpu_custom_call" | custom-call | flops 35999997952 | bytes 72000000 | tf_op jit(solution)/shard_map/gather_mid/pallas_call | solution.py:459
  274.3 16.5 %fusion.8 = (bf16[1024,2048]{1,0:T(8,128)(2,1)}, bf16[1024,2048]{1,0:T(8,128)(2,1)S(1)}) fusion(f32[2048]{0:T(1024)S(1)} %copy-done.59, bf16[1024,2048]{1,0:T(8,128)(2,1)} %bitcast.108, bf16[2048,2048]{1,0:T(8,128)(2,1)} %all-gather.6.cloned.1.call-done.refs_4_), kind=kOutput, calls=%fused_computation.11 | convolution fusion | flops 8615100416 | bytes 20979712 | tf_op jit(solution)/shard_map/dot_general | solution.py:38
  292.9 24.4 %convolution_convert_fusion = bf16[2048,2048]{1,0:T(8,128)(2,1)} fusion(bf16[1024,2048]{1,0:T(8,128)(2,1)} %bitcast.22.refs_1_, bf16[1024,2048]{1,0:T(8,128)(2,1)S(1)} %get-tuple-element.73), kind=kOutput, calls=%fused_computation.18 | convolution fusion | flops 8594128896 | bytes 16777216 | tf_op jit(solution)/shard_map/dot_general | solution.py:46
  317.4 14.0 %convolution_convert_fusion.1 = bf16[1024,2048]{1,0:T(8,128)(2,1)} fusion(bf16[1024,2048]{1,0:T(8,128)(2,1)} %copy-done.60, bf16[2048,2048]{1,0:T(8,128)(2,1)} %all-gather.8.cloned.1.call-done.refs_2_), kind=kOutput, calls=%fused_computation.22 | convolution fusion | flops 8592031744 | bytes 16777216 | tf_op jit(solution)/shard_map/dot_general | solution.py:42
  331.4 36.4 %scatter_ffn.1 = (f32[256,2048]{1,0:T(8,128)}, bf16[1024,2048]{1,0:T(8,128)(2,1)}, bf16[1024,2048]{1,0:T(8,128)(2,1)}) custom-call(bf16[4,256,2048]{2,1,0:T(8,128)(2,1)} %bitcast.132, bf16[1024,2048]{1,0:T(8,128)(2,1)} %bitcast.22.refs_1_, bf16[2048,2048]{1,0:T(8,128)(2,1)} %all-gather.8.cloned.1.call-done.refs_2_, ...), custom_call_target="tpu_custom_call" | custom-call | flops 35999997952 | bytes 72000000 | tf_op jit(solution)/shard_map/scatter_ffn/pallas_call | solution.py:459
  367.8 35.6 %scatter_mid.1 = (f32[256,2048]{1,0:T(8,128)}, bf16[2048,2048]{1,0:T(8,128)(2,1)}, f32[1,2048]{1,0:T(1,128)}) custom-call(bf16[4,256,2048]{2,1,0:T(8,128)(2,1)} %bitcast.130, bf16[1024,2048]{1,0:T(8,128)(2,1)} %bitcast.109, bf16[1024,2048]{1,0:T(8,128)(2,1)} %get-tuple-element.75.refs_2_), custom_call_target="tpu_custom_call" | custom-call | flops 35999997952 | bytes 72000000 | tf_op jit(solution)/shard_map/scatter_mid/pallas_call | solution.py:459
  403.4 9.2 %reduce-scatter.4.cloned.1.call-done.down_ref = bf16[256,2048]{1,0:T(8,128)(2,1)} async-done(((bf16[2048,2048]{1,0:T(8,128)(2,1)}), bf16[256,2048]{1,0:T(8,128)(2,1)}) %reduce-scatter.4.cloned.1.call-update) | async-done | bytes 1048592 | tf_op jit(solution)/shard_map/reduce_scatter | solution.py:1140
  413.4 3.4 multiply_reduce_fusion
  416.9 4.1 fusion.48
  421.7 45.1 %gather_back.1 = (bf16[4,256,2048]{2,1,0:T(8,128)(2,1)S(1)}, bf16[8,32,2048]{2,1,0:T(8,128)(2,1)S(1)}) custom-call(bf16[256,2048]{1,0:T(8,128)(2,1)S(1)} %get-tuple-element.120.refs_0_, bf16[8,32,2048]{2,1,0:T(8,128)(2,1)S(1)} %bitcast.100), custom_call_target="tpu_custom_call" | custom-call | flops 35999997952 | bytes 72000000 | tf_op jit(solution)/shard_map/gather_back/pallas_call | solution.py:459
  468.8 2.5 broadcast_in_dim.24
  471.3 4.8 all-to-all-start.1
  476.4 6.2 fusion.34.x_ref
  485.0 4.5 fusion.21.do_ref
  489.5 23.4 %attend_back.1 = (bf16[2048,768]{1,0:T(8,128)(2,1)S(1)}, f32[1,8,256]{2,1,0:T(8,128)S(1)}) custom-call(s32[5]{0:T(128)S(1)} %pad_add_fusion.info_ref, s32[1,2048]{1,0:T(1,128)S(1)} %bitcast.103, bf16[2048,768]{1,0:T(8,128)(2,1)} %copy-done.29, bf16[2048,768]{1,0:T(8,128)(2,1)} %copy-done.29, bf16[2048,768]{1,0:T(8,128)(2,1)} %copy-done.29, ...), custom_call_target="tpu_custom_call" | custom-call | flops 33999998976 | bytes 68000000 | tf_op jit(solution)/shard_map/attend_back/pallas_call | solution.py:1078
  512.9 8.7 %fusion.18 = bf16[2048,768]{1,0:T(8,128)(2,1)} fusion(bf16[2048,768]{1,0:T(8,128)(2,1)S(1)} %get-tuple-element.82, s32[2048]{0:T(1024)S(1)} %copy-done.55), kind=kOutput, calls=%fused_computation.24 | convolution fusion | flops 6448218112 | bytes 6299648 | tf_op jit(solution)/shard_map/dot_general | solution.py:38
  521.6 3.8 swap_heads.7.right_ref
  527.3 14.8 %two_products.1 = bf16[2048,2048]{1,0:T(8,128)(2,1)} custom-call(bf16[1024,2048]{1,0:T(8,128)(2,1)} %bitcast.104, bf16[1024,1536]{1,0:T(8,128)(2,1)S(1)} %copy-done.24, bf16[1024,2048]{1,0:T(8,128)(2,1)} %bitcast.107, bf16[1024,512]{1,0:T(8,128)(2,1)S(1)} %copy-done.25), custom_call_target="tpu_custom_call" | custom-call | flops 12000000000 | bytes 24000000 | tf_op jit(solution)/shard_map/two_products/pallas_call | solution.py:877
  545.2 11.2 %fusion.15 = bf16[1024,2048]{1,0:T(8,128)(2,1)} fusion(bf16[1024,1536]{1,0:T(8,128)(2,1)} %swap_heads.7.right_ref, bf16[2048,2048]{1,0:T(8,128)(2,1)} %all-gather.4.cloned.1.call-done.w_ref), kind=kOutput, calls=%fused_computation.21 | convolution fusion | flops 6444548096 | bytes 13631488 | tf_op jit(solution)/shard_map/dot_general | solution.py:42
  556.4 97.9 %finish.1 = (bf16[8,4,32,2048]{3,2,1,0:T(8,128)(2,1)}, f32[24,512]{1,0:T(8,128)S(1)}, f32[16,256]{1,0:T(8,128)S(1)}) custom-call(bf16[4,8,32,2048]{3,2,1,0:T(8,128)(2,1)} %bitcast.131, f32[8,32,2048]{2,1,0:T(8,128)S(1)} %copy-done.9, bf16[8,32,2048]{2,1,0:T(8,128)(2,1)S(1)} %copy-done.5, f32[8,32,2048]{2,1,0:T(8,128)S(1)} %bitcast.97, ...), custom_call_target="tpu_custom_call" | custom-call | flops 89999998976 | bytes 180000000 | tf_op jit(solution)/shard_map/finish/pallas_call | solution.py:658
  656.5 9.2 %settle.1 = (f32[8,4,32,2048]{3,2,1,0:T(8,128)}, bf16[8,4,32,2048]{3,2,1,0:T(8,128)(2,1)}, f32[256,2048]{1,0:T(8,128)}, f32[2048,256]{1,0:T(8,128)}, f32[1,2048]...) custom-call(bf16[8,4,32,2048]{3,2,1,0:T(8,128)(2,1)S(1)} %copy-done., ...), custom_call_target="tpu_custom_call" | custom-call | flops 10000000000 | bytes 20000000 | tf_op jit(solution)/shard_map/settle/pallas_call | solution.py:773
  (201 shorter events, 49.5 us)
Async XLA Ops:
  7.2 132.5 %copy-start = (s32[4,4]{1,0:T(4,128)S(1)}, s32[4,4]{1,0:T(4,128)}, u32[]{:S(2)}) copy-start(s32[4,4]{1,0:T(4,128)} %param.22) | copy-start | bytes 196
  7.2 133.6 %all-gather.4.cloned.1.call-start = ((), (), s32[]{:S(2)}) async-start(), calls=%async_computation.5 | async-start | bytes 9437184 | tf_op jit(solution)/shard_map/all_gather | solution.py:1143
  12.2 262.1 %all-gather.6.cloned.1.call-start = ((), (), s32[]{:S(2)}) async-start(), calls=%async_computation.6 | async-start | bytes 9437184 | tf_op jit(solution)/shard_map/all_gather | solution.py:1145
  14.8 64.6 %copy-start.10 = (f32[2048]{0:T(1024)S(1)}, f32[2048]{0:T(1024)}, u32[]{:S(2)}) copy-start(f32[2048]{0:T(1024)} %param.35) | copy-start | bytes 24580
  14.8 64.6 %copy-start.51 = (f32[2048]{0:T(1024)S(1)}, f32[2048]{0:T(1024)}, u32[]{:S(2)}) copy-start(f32[2048]{0:T(1024)} %param.36) | copy-start | bytes 24580
  74.0 160.6 %copy-start.2 = (bf16[8,32,2048]{2,1,0:T(8,128)(2,1)}, bf16[8,32,2048]{2,1,0:T(8,128)(2,1)S(1)}, u32[]{:S(2)}) copy-start(bf16[8,32,2048]{2,1,0:T(8,128)(2,1)S(1)} %get-tuple-element.67) | copy-start | bytes 3145732
  74.3 52.7 %copy-start.37 = (f32[8,32]{1,0:T(8,128)}, f32[8,32]{1,0:T(8,128)S(1)}, u32[]{:S(2)}) copy-start(f32[8,32]{1,0:T(8,128)S(1)} %broadcast_multiply_fusion) | copy-start | bytes 3076
  75.4 51.6 %copy-start.39 = (f32[8,32]{1,0:T(8,128)}, f32[8,32]{1,0:T(8,128)S(1)}, u32[]{:S(2)}) copy-start(f32[8,32]{1,0:T(8,128)S(1)} %get-tuple-element.131) | copy-start | bytes 3076
  79.4 49.6 %copy-start.49 = (f32[256]{0:T(256)}, f32[256]{0:T(256)S(1)}, u32[]{:S(2)}) copy-start(f32[256]{0:T(256)S(1)} %reshape.367) | copy-start | bytes 3076
  132.8 5.1 copy-start.33
  132.8 53.8 %all-to-all-start = ((bf16[4,256,2048]{2,1,0:T(8,128)(2,1)}), bf16[4,256,2048]{2,1,0:T(8,128)(2,1)}, u32[]{:S(2)}, u32[]{:S(2)}) async-start(bf16[4,256,2048]{2,1,0:T(8,128)(2,1)} %broadcast_in_dim.23), calls=%async_computation | async-start | bytes 8388608 | tf_op jit(solution)/shard_map/all_to_all | solution.py:481
  137.8 179.6 %all-gather.8.cloned.1.call-start = ((), (), s32[]{:S(2)}) async-start(), calls=%async_computation.7 | async-start | bytes 9437184 | tf_op jit(solution)/shard_map/all_gather | solution.py:1146
  139.3 273.3 %reduce-scatter.4.cloned.1.call-start = ((), (), s32[]{:S(2)}) async-start(), calls=%async_computation.8 | async-start | bytes 9437184 | tf_op jit(solution)/shard_map/reduce_scatter | solution.py:1140
  139.5 47.2 %copy-start.54 = (s32[2048]{0:T(1024)}, s32[2048]{0:T(1024)S(1)}, u32[]{:S(2)}) copy-start(s32[2048]{0:T(1024)S(1)} %eq.38) | copy-start | bytes 24580
  140.0 29.1 %copy-start.12 = (s32[2048]{0:T(1024)}, s32[2048]{0:T(1024)S(1)}, u32[]{:S(2)}) copy-start(s32[2048]{0:T(1024)S(1)} %select_reduce_fusion) | copy-start | bytes 24580
  197.1 37.5 %copy-start.41 = (f32[2048]{0:T(1024)S(1)}, f32[2048]{0:T(1024)}, u32[]{:S(2)}) copy-start(f32[2048]{0:T(1024)} %param.32) | copy-start | bytes 24580
  235.0 37.3 %copy-start.43 = (f32[256]{0:T(256)}, f32[256]{0:T(256)S(1)}, u32[]{:S(2)}) copy-start(f32[256]{0:T(256)S(1)} %broadcast_multiply_fusion.3) | copy-start | bytes 3076
  236.6 35.7 %copy-start.45 = (f32[256]{0:T(256)}, f32[256]{0:T(256)S(1)}, u32[]{:S(2)}) copy-start(f32[256]{0:T(256)S(1)} %add_rsqrt_fusion.1) | copy-start | bytes 3076
  237.1 37.2 %copy-start.59 = (f32[2048]{0:T(1024)S(1)}, f32[2048]{0:T(1024)}, u32[]{:S(2)}) copy-start(f32[2048]{0:T(1024)} %param.33) | copy-start | bytes 24580
  317.3 224.8 %reduce-scatter.6.cloned.1.call-start = ((), (), s32[]{:S(2)}) async-start(), calls=%async_computation.9 | async-start | bytes 9437184 | tf_op jit(solution)/shard_map/reduce_scatter | solution.py:1140
  416.8 4.1 copy-start.3
  416.9 4.1 copy-start.7
  471.3 54.1 %all-to-all-start.1 = ((bf16[4,8,32,2048]{3,2,1,0:T(8,128)(2,1)}), bf16[4,8,32,2048]{3,2,1,0:T(8,128)(2,1)}, u32[]{:S(2)}, u32[]{:S(2)}) async-start(bf16[4,8,32,2048]{3,2,1,0:T(8,128)(2,1)} %broadcast_in_dim.24), calls=%async_computation.1 | async-start | bytes 8388608 | tf_op jit(solution)/shard_map/all_to_all | solution.py:481
  476.2 189.6 %reduce-scatter.8.cloned.1.call-start = ((), (), s32[]{:S(2)}) async-start(), calls=%async_computation.10 | async-start | bytes 9437184 | tf_op jit(solution)/shard_map/reduce_scatter | solution.py:1140
  485.0 4.5 copy-start.13
  485.0 4.5 copy-start.28
  545.1 11.3 %copy-start.8 = (f32[256,2048]{1,0:T(8,128)S(1)}, f32[256,2048]{1,0:T(8,128)}, u32[]{:S(2)}) copy-start(f32[256,2048]{1,0:T(8,128)} %get-tuple-element.121) | copy-start | bytes 6291460
  545.1 11.2 %copy-start.9 = (f32[8,32,2048]{2,1,0:T(8,128)S(1)}, f32[8,32,2048]{2,1,0:T(8,128)}, u32[]{:S(2)}) copy-start(f32[8,32,2048]{2,1,0:T(8,128)} %fusion.22.unit) | copy-start | bytes 6291460
  545.1 11.2 %copy-start.11 = (f32[2048]{0:T(1024)S(1)}, f32[2048]{0:T(1024)}, u32[]{:S(2)}) copy-start(f32[2048]{0:T(1024)} %param.35) | copy-start | bytes 24580
  556.4 97.9 %copy-start.14 = (bf16[256,2048]{1,0:T(8,128)(2,1)S(1)}, bf16[256,2048]{1,0:T(8,128)(2,1)}, u32[]{:S(2)}) copy-start(bf16[256,2048]{1,0:T(8,128)(2,1)} %reduce-scatter.4.cloned.1.call-done.down_ref) | copy-start | bytes 3145732
  556.4 97.9 %copy-start.15 = (bf16[256,2048]{1,0:T(8,128)(2,1)S(1)}, bf16[256,2048]{1,0:T(8,128)(2,1)}, u32[]{:S(2)}) copy-start(bf16[256,2048]{1,0:T(8,128)(2,1)} %reduce-scatter.6.cloned.1.call-done.up_ref) | copy-start | bytes 3145732
  656.5 11.9 %copy-start.1 = (s32[4,4]{1,0:T(4,128)S(1)}, s32[4,4]{1,0:T(4,128)}, u32[]{:S(2)}) copy-start(s32[4,4]{1,0:T(4,128)} %param.22) | copy-start | bytes 196
  (37 other events, 83.1 us)
Sparse Core Ops, SparseCore 0:
  12.4 119.3 all-gather.3
  133.4 83.1 all-gather.5
  218.1 80.5 all-gather.7
  317.5 95.1 reduce-scatter.3
  414.8 110.7 reduce-scatter.5
  542.3 123.4 reduce-scatter.7

commit v5 on v4

--- a/solution.py
+++ b/solution.py
@@ -867,6 +867,36 @@
 
     lax.fori_loop(0, width // tile, step, 0)
     o_ref[:, width:] = tn(other_ref[...], last_ref[...]).astype(o_ref.dtype)
+
+
+def product_kernel(left_ref, right_ref, o_ref):
+    tile = min(512, o_ref.shape[1])
+
+    def step(k, _):
+        columns = pl.ds(pl.multiple_of(k * tile, tile), tile)
+        o_ref[:, columns] = tn(left_ref[...], right_ref[:, columns]).astype(o_ref.dtype)
+        return 0
+
+    lax.fori_loop(0, o_ref.shape[1] // tile, step, 0)
+
+
+def product(left, right):
+    rows, depth = left.shape
+    width = right.shape[1]
+    tile = min(512, depth)
+    return pl.pallas_call(
+        product_kernel,
+        out_shape=jax.ShapeDtypeStruct((depth, width), bf16),
+        grid=(depth // tile,),
+        in_specs=[
+            pl.BlockSpec((rows, tile), lambda i: (0, i)),
+            pl.BlockSpec((rows, width), lambda i: (0, 0)),
+        ],
+        out_specs=pl.BlockSpec((tile, width), lambda i: (i, 0)),
+        compiler_params=pltpu.CompilerParams(vmem_limit_bytes=40 * 2**20),
+        cost_estimate=takes(12),
+        name="product",
+    )(left, right)
 
 
 def two_products(left, right, other, last):
@@ -1199,7 +1229,7 @@
     act = (pre_act * below).astype(bf16)
     slope = (below + pre_act * jnp.exp(-0.5 * pre_act * pre_act) * (2 * math.pi) ** -0.5).astype(bf16)
 
-    grad_w_down_t = tn(down_grad, act).astype(bf16)
+    grad_w_down_t = product(down_grad, act)
     grad_w_down_t, act = lax.optimization_barrier((grad_w_down_t, act))
     shared_down = share(grad_w_down_t)
     ffn_part = nt(act, w_down_t).astype(bf16).reshape(tps, own, width)

time: 687 us -> 677 us (0.985)
  matrix products: 103 us -> 78.9 us
  Pallas kernels: 482 us -> 505 us
  waiting for transfers between devices: 10.1 us -> 2.88 us
    dot_general x1 -> x0, matrix products: 24.4 us -> none  [tn(): lax.dot_general(left, right, (((0,), (0,)), ((), ())), preferred_element_...]
    pallas_call x0 -> x1, Pallas kernels: none -> 14.8 us  [product(): pl.pallas_call(product_kernel, out_shape=jax.ShapeDtypeStruct((depth, wid...]
    pallas_call x1, Pallas kernels: 15.9 us -> 24.5 us  [attend(): pl.pallas_call(functools.partial(attend_kernel, qb, kb), out_shape=(jax.S...]
    reduce_scatter x3, waiting for transfers between devices: 9.34 us -> 2.07 us  [share(): return lax.psum_scatter(grad, 'band', scatter_dimension=0, tiled=True)]
  transfers between devices with their start and end apart: 8 -> 8, of which waited for: 2 -> 1; matrix products, arithmetic and copies ran while one was open for 19% -> 16% of each run, Pallas kernels for 71% -> 75%
where the time goes in v5:
time: 677 us; the launch traced here: 668 us
  Pallas kernels  505 us (75%)
  matrix products  78.9 us (12%)
  local copies, waits for them, and re-layouts  35.7 us (5%)
  other arithmetic  19 us (3%)
  between operations  15.5 us (2%)
  starting transfers between devices  10.5 us (2%)
    pallas_call x7, Pallas kernels, transfer(): pl.pallas_call(kernel, out_shape=tuple((shape for item in items for shape...  295 us
    pallas_call x1, Pallas kernels, finish(): pl.pallas_call(functools.partial(finish_kernel, count, size), out_shape=(...  92.5 us
    dot_general x6, matrix products, nn(): return jnp.dot(left, right, preferred_element_type=f32)  49.2 us
    dot_general x3, matrix products, nt(): lax.dot_general(left, right, (((1,), (1,)), ((), ())), preferred_element_...  29.8 us
    pallas_call x1, Pallas kernels, attend_back(): pl.pallas_call(functools.partial(attend_back_kernel, qb, kb), out_shape=(...  29.4 us
    unnamed x129, local copies, waits for them, and re-layouts  27.4 us
    pallas_call x1, Pallas kernels, attend(): pl.pallas_call(functools.partial(attend_kernel, qb, kb), out_shape=(jax.S...  24.5 us
    pallas_call x1, Pallas kernels, product(): pl.pallas_call(product_kernel, out_shape=jax.ShapeDtypeStruct((depth, wid...  14.8 us
  transfers between devices with their start and end apart: 8, of which 1 were waited for; matrix products, arithmetic and copies ran while one was open for 16% of the time, Pallas kernels for 75%

profile of v5, /device:TPU:9, one launch (start us, length us, event | category | flops | bytes accessed | tf_op | source)
XLA Modules:
  0.0 667.9 jit_solution(18293570878769211478)
XLA Ops:
  14.8 59.2 %swap_in.1 = (bf16[8,32,2048]{2,1,0:T(8,128)(2,1)S(1)}, s32[8,4,256]{2,1,0:T(4,128)S(1)}) custom-call(bf16[8,32,2048]{2,1,0:T(8,128)(2,1)S(1)} %bitcast.97, s32[4,256]{1,0:T(4,128)S(1)} %copy-done.17), custom_call_target="tpu_custom_call" | custom-call | flops 35999997952 | bytes 72000000 | tf_op jit(solution)/shard_map/swap_in/pallas_call | solution.py:459
  79.9 47.1 %gather_in.1 = (bf16[4,256,2048]{2,1,0:T(8,128)(2,1)S(1)}, bf16[8,32,2048]{2,1,0:T(8,128)(2,1)S(1)}) custom-call(bf16[256,2048]{1,0:T(8,128)(2,1)S(1)} %fusion.28.refs_0_, bf16[8,32,2048]{2,1,0:T(8,128)(2,1)S(1)} %bitcast.96), custom_call_target="tpu_custom_call" | custom-call | flops 35999997952 | bytes 72000000 | tf_op jit(solution)/shard_map/gather_in/pallas_call | solution.py:459
  130.2 2.5 broadcast_in_dim.23
  132.8 5.0 all-to-all-start
  143.0 11.2 %project.1.x_ref = bf16[2,1024,768]{2,1,0:T(8,128)(2,1)S(1)} custom-call(bf16[1024,2048]{1,0:T(8,128)(2,1)S(1)} %bitcast.103, bf16[2048,2048]{1,0:T(8,128)(2,1)} %all-gather.4.cloned.1.call-done.w_ref, f32[1,1536]{1,0:T(1,128)S(1)} %broadcast_in_dim_reshape.2.bias_ref, f32[1,1536]{1,0:T(1,128)S(1)} %copy-done.22), custom_call_target="tpu_custom_call" | custom-call | flops 6442450944 | bytes 12582912 | tf_op jit(solution)/shard_map/project/pallas_call | solution.py:841
  155.8 3.8 swap_heads.4
  159.6 9.4 %fusion.19.q_ref.k_ref.v_ref = bf16[2048,768]{1,0:T(8,128)(2,1)S(1)} fusion(bf16[2048,768]{1,0:T(8,128)(2,1)} %bitcast.132, s32[2048]{0:T(1024)S(1)} %eq.38), kind=kOutput, calls=%fused_computation.24 | convolution fusion | flops 6448218112 | bytes 6299648 | tf_op jit(solution)/shard_map/dot_general | solution.py:38
  169.1 24.5 %attend.1 = (bf16[2048,256]{1,0:T(8,128)(2,1)S(1)}, f32[1,8,2048]{2,1,0:T(8,128)S(1)}) custom-call(s32[5]{0:T(128)S(1)} %pad_add_fusion.info_ref, s32[1,2048]{1,0:T(1,128)S(1)} %bitcast.100, bf16[2048,768]{1,0:T(8,128)(2,1)S(1)} %fusion.19.q_ref.k_ref.v_ref, bf16[2048,768]{1,0:T(8,128)(2,1)S(1)} %fusion.19.q_ref.k_ref.v_ref, ...), custom_call_target="tpu_custom_call" | custom-call | flops 30000001024 | bytes 60000000 | tf_op jit(solution)/shard_map/attend/pallas_call | solution.py:1086
  195.3 3.8 fusion.20
  199.2 2.3 swap_heads.5.last_ref
  201.5 4.3 convolution_convert_fusion.1
  205.8 37.4 %scatter_attn.1 = f32[256,2048]{1,0:T(8,128)S(1)} custom-call(bf16[4,256,2048]{2,1,0:T(8,128)(2,1)S(1)} %bitcast.108), custom_call_target="tpu_custom_call" | custom-call | flops 35999997952 | bytes 72000000 | tf_op jit(solution)/shard_map/scatter_attn/pallas_call | solution.py:459
  245.7 35.1 %gather_mid.1 = bf16[4,256,2048]{2,1,0:T(8,128)(2,1)S(1)} custom-call(bf16[256,2048]{1,0:T(8,128)(2,1)S(1)} %add_convert_fusion.1.refs_0_), custom_call_target="tpu_custom_call" | custom-call | flops 35999997952 | bytes 72000000 | tf_op jit(solution)/shard_map/gather_mid/pallas_call | solution.py:459
  282.8 16.5 %fusion.8 = (bf16[1024,2048]{1,0:T(8,128)(2,1)}, bf16[1024,2048]{1,0:T(8,128)(2,1)S(1)}) fusion(f32[2048]{0:T(1024)S(1)} %copy-done.60, bf16[1024,2048]{1,0:T(8,128)(2,1)} %bitcast.106, bf16[2048,2048]{1,0:T(8,128)(2,1)} %all-gather.6.cloned.1.call-done.refs_4_), kind=kOutput, calls=%fused_computation.11 | convolution fusion | flops 8615100416 | bytes 20979712 | tf_op jit(solution)/shard_map/dot_general | solution.py:38
  299.3 14.8 %product.1 = bf16[2048,2048]{1,0:T(8,128)(2,1)} custom-call(bf16[1024,2048]{1,0:T(8,128)(2,1)} %bitcast.22.left_ref.refs_1_, bf16[1024,2048]{1,0:T(8,128)(2,1)S(1)} %get-tuple-element.73.right_ref), custom_call_target="tpu_custom_call" | custom-call | flops 12000000000 | bytes 24000000 | tf_op jit(solution)/shard_map/product/pallas_call | solution.py:887
  316.4 14.0 %convolution_convert_fusion = bf16[1024,2048]{1,0:T(8,128)(2,1)} fusion(bf16[1024,2048]{1,0:T(8,128)(2,1)} %copy-done.27, bf16[2048,2048]{1,0:T(8,128)(2,1)} %all-gather.8.cloned.1.call-done.refs_2_), kind=kOutput, calls=%fused_computation.21 | convolution fusion | flops 8592031744 | bytes 16777216 | tf_op jit(solution)/shard_map/dot_general | solution.py:42
  330.4 36.2 %scatter_ffn.1 = (f32[256,2048]{1,0:T(8,128)}, bf16[1024,2048]{1,0:T(8,128)(2,1)}, bf16[1024,2048]{1,0:T(8,128)(2,1)}) custom-call(bf16[4,256,2048]{2,1,0:T(8,128)(2,1)} %bitcast.130, bf16[1024,2048]{1,0:T(8,128)(2,1)} %bitcast.22.left_ref.refs_1_, bf16[2048,2048]{1,0:T(8,128)(2,1)} %all-gather.8.cloned.1.call-done.refs_2_, ...), custom_call_target="tpu_custom_call" | custom-call | flops 35999997952 | bytes 72000000 | tf_op jit(solution)/shard_map/scatter_ffn/pallas_call | solution.py:459
  366.6 35.4 %scatter_mid.1 = (f32[256,2048]{1,0:T(8,128)}, bf16[2048,2048]{1,0:T(8,128)(2,1)}, f32[1,2048]{1,0:T(1,128)}) custom-call(bf16[4,256,2048]{2,1,0:T(8,128)(2,1)} %bitcast.128, bf16[1024,2048]{1,0:T(8,128)(2,1)} %bitcast.107, bf16[1024,2048]{1,0:T(8,128)(2,1)} %get-tuple-element.75.refs_2_), custom_call_target="tpu_custom_call" | custom-call | flops 35999997952 | bytes 72000000 | tf_op jit(solution)/shard_map/scatter_mid/pallas_call | solution.py:459
  404.7 3.4 multiply_reduce_fusion
  408.3 4.1 fusion.48
  413.1 44.9 %gather_back.1 = (bf16[4,256,2048]{2,1,0:T(8,128)(2,1)S(1)}, bf16[8,32,2048]{2,1,0:T(8,128)(2,1)S(1)}) custom-call(bf16[256,2048]{1,0:T(8,128)(2,1)S(1)} %get-tuple-element.120.refs_0_, bf16[8,32,2048]{2,1,0:T(8,128)(2,1)S(1)} %bitcast.98), custom_call_target="tpu_custom_call" | custom-call | flops 35999997952 | bytes 72000000 | tf_op jit(solution)/shard_map/gather_back/pallas_call | solution.py:459
  460.0 2.5 broadcast_in_dim.24
  462.6 4.8 all-to-all-start.1
  467.7 6.3 fusion.34.x_ref
  476.3 4.5 fusion.21.do_ref
  480.8 29.4 %attend_back.1 = (bf16[2048,768]{1,0:T(8,128)(2,1)S(1)}, f32[1,8,256]{2,1,0:T(8,128)S(1)}) custom-call(s32[5]{0:T(128)S(1)} %pad_add_fusion.info_ref, s32[1,2048]{1,0:T(1,128)S(1)} %bitcast.101, bf16[2048,768]{1,0:T(8,128)(2,1)} %copy-done.30, bf16[2048,768]{1,0:T(8,128)(2,1)} %copy-done.30, bf16[2048,768]{1,0:T(8,128)(2,1)} %copy-done.30, ...), custom_call_target="tpu_custom_call" | custom-call | flops 33999998976 | bytes 68000000 | tf_op jit(solution)/shard_map/attend_back/pallas_call | solution.py:1108
  510.1 8.7 %fusion.18 = bf16[2048,768]{1,0:T(8,128)(2,1)} fusion(bf16[2048,768]{1,0:T(8,128)(2,1)S(1)} %get-tuple-element.82, s32[2048]{0:T(1024)S(1)} %copy-done.56), kind=kOutput, calls=%fused_computation.23 | convolution fusion | flops 6448218112 | bytes 6299648 | tf_op jit(solution)/shard_map/dot_general | solution.py:38
  518.8 3.8 swap_heads.7.right_ref
  524.5 14.8 %two_products.1 = bf16[2048,2048]{1,0:T(8,128)(2,1)} custom-call(bf16[1024,2048]{1,0:T(8,128)(2,1)} %bitcast.102, bf16[1024,1536]{1,0:T(8,128)(2,1)S(1)} %copy-done.24, bf16[1024,2048]{1,0:T(8,128)(2,1)} %bitcast.105, bf16[1024,512]{1,0:T(8,128)(2,1)S(1)} %copy-done.25), custom_call_target="tpu_custom_call" | custom-call | flops 12000000000 | bytes 24000000 | tf_op jit(solution)/shard_map/two_products/pallas_call | solution.py:907
  542.3 11.5 %fusion.15 = bf16[1024,2048]{1,0:T(8,128)(2,1)} fusion(bf16[1024,1536]{1,0:T(8,128)(2,1)} %swap_heads.7.right_ref, bf16[2048,2048]{1,0:T(8,128)(2,1)} %all-gather.4.cloned.1.call-done.w_ref), kind=kOutput, calls=%fused_computation.20 | convolution fusion | flops 6444548096 | bytes 13631488 | tf_op jit(solution)/shard_map/dot_general | solution.py:42
  553.9 92.5 %finish.1 = (bf16[8,4,32,2048]{3,2,1,0:T(8,128)(2,1)}, f32[24,512]{1,0:T(8,128)S(1)}, f32[16,256]{1,0:T(8,128)S(1)}) custom-call(bf16[4,8,32,2048]{3,2,1,0:T(8,128)(2,1)} %bitcast.129, f32[8,32,2048]{2,1,0:T(8,128)S(1)} %copy-done.9, bf16[8,32,2048]{2,1,0:T(8,128)(2,1)S(1)} %copy-done.5, f32[8,32,2048]{2,1,0:T(8,128)S(1)} %bitcast.95, ...), custom_call_target="tpu_custom_call" | custom-call | flops 89999998976 | bytes 180000000 | tf_op jit(solution)/shard_map/finish/pallas_call | solution.py:658
  648.6 9.3 %settle.1 = (f32[8,4,32,2048]{3,2,1,0:T(8,128)}, bf16[8,4,32,2048]{3,2,1,0:T(8,128)(2,1)}, f32[256,2048]{1,0:T(8,128)}, f32[2048,256]{1,0:T(8,128)}, f32[1,2048]...) custom-call(bf16[8,4,32,2048]{3,2,1,0:T(8,128)(2,1)S(1)} %copy-done., ...), custom_call_target="tpu_custom_call" | custom-call | flops 10000000000 | bytes 20000000 | tf_op jit(solution)/shard_map/settle/pallas_call | solution.py:773
  (201 shorter events, 49.4 us)
Async XLA Ops:
  7.2 132.5 %copy-start = (s32[4,4]{1,0:T(4,128)S(1)}, s32[4,4]{1,0:T(4,128)}, u32[]{:S(2)}) copy-start(s32[4,4]{1,0:T(4,128)} %param.22) | copy-start | bytes 196
  7.2 133.6 %all-gather.4.cloned.1.call-start = ((), (), s32[]{:S(2)}) async-start(), calls=%async_computation.5 | async-start | bytes 9437184 | tf_op jit(solution)/shard_map/all_gather | solution.py:1173
  12.2 270.6 %all-gather.6.cloned.1.call-start = ((), (), s32[]{:S(2)}) async-start(), calls=%async_computation.6 | async-start | bytes 9437184 | tf_op jit(solution)/shard_map/all_gather | solution.py:1175
  14.8 64.6 %copy-start.10 = (f32[2048]{0:T(1024)S(1)}, f32[2048]{0:T(1024)}, u32[]{:S(2)}) copy-start(f32[2048]{0:T(1024)} %param.35) | copy-start | bytes 24580
  14.8 64.6 %copy-start.52 = (f32[2048]{0:T(1024)S(1)}, f32[2048]{0:T(1024)}, u32[]{:S(2)}) copy-start(f32[2048]{0:T(1024)} %param.36) | copy-start | bytes 24580
  74.0 169.3 %copy-start.2 = (bf16[8,32,2048]{2,1,0:T(8,128)(2,1)}, bf16[8,32,2048]{2,1,0:T(8,128)(2,1)S(1)}, u32[]{:S(2)}) copy-start(bf16[8,32,2048]{2,1,0:T(8,128)(2,1)S(1)} %get-tuple-element.67) | copy-start | bytes 3145732
  74.3 52.7 %copy-start.38 = (f32[8,32]{1,0:T(8,128)}, f32[8,32]{1,0:T(8,128)S(1)}, u32[]{:S(2)}) copy-start(f32[8,32]{1,0:T(8,128)S(1)} %broadcast_multiply_fusion) | copy-start | bytes 3076
  75.4 51.6 %copy-start.40 = (f32[8,32]{1,0:T(8,128)}, f32[8,32]{1,0:T(8,128)S(1)}, u32[]{:S(2)}) copy-start(f32[8,32]{1,0:T(8,128)S(1)} %get-tuple-element.131) | copy-start | bytes 3076
  79.4 49.6 %copy-start.50 = (f32[256]{0:T(256)}, f32[256]{0:T(256)S(1)}, u32[]{:S(2)}) copy-start(f32[256]{0:T(256)S(1)} %reshape.367) | copy-start | bytes 3076
  132.8 5.1 copy-start.34
  132.8 62.5 %all-to-all-start = ((bf16[4,256,2048]{2,1,0:T(8,128)(2,1)}), bf16[4,256,2048]{2,1,0:T(8,128)(2,1)}, u32[]{:S(2)}, u32[]{:S(2)}) async-start(bf16[4,256,2048]{2,1,0:T(8,128)(2,1)} %broadcast_in_dim.23), calls=%async_computation | async-start | bytes 8388608 | tf_op jit(solution)/shard_map/all_to_all | solution.py:481
  137.8 178.6 %all-gather.8.cloned.1.call-start = ((), (), s32[]{:S(2)}) async-start(), calls=%async_computation.7 | async-start | bytes 9437184 | tf_op jit(solution)/shard_map/all_gather | solution.py:1176
  139.3 264.7 %reduce-scatter.4.cloned.1.call-start = ((), (), s32[]{:S(2)}) async-start(), calls=%async_computation.8 | async-start | bytes 9437184 | tf_op jit(solution)/shard_map/reduce_scatter | solution.py:1170
  139.5 55.9 %copy-start.55 = (s32[2048]{0:T(1024)}, s32[2048]{0:T(1024)S(1)}, u32[]{:S(2)}) copy-start(s32[2048]{0:T(1024)S(1)} %eq.38) | copy-start | bytes 24580
  140.0 29.1 %copy-start.12 = (s32[2048]{0:T(1024)}, s32[2048]{0:T(1024)S(1)}, u32[]{:S(2)}) copy-start(s32[2048]{0:T(1024)S(1)} %select_reduce_fusion) | copy-start | bytes 24580
  205.7 37.5 %copy-start.42 = (f32[2048]{0:T(1024)S(1)}, f32[2048]{0:T(1024)}, u32[]{:S(2)}) copy-start(f32[2048]{0:T(1024)} %param.32) | copy-start | bytes 24580
  243.7 37.2 %copy-start.44 = (f32[256]{0:T(256)}, f32[256]{0:T(256)S(1)}, u32[]{:S(2)}) copy-start(f32[256]{0:T(256)S(1)} %broadcast_multiply_fusion.3) | copy-start | bytes 3076
  245.2 35.6 %copy-start.46 = (f32[256]{0:T(256)}, f32[256]{0:T(256)S(1)}, u32[]{:S(2)}) copy-start(f32[256]{0:T(256)S(1)} %add_rsqrt_fusion.1) | copy-start | bytes 3076
  245.7 37.1 %copy-start.60 = (f32[2048]{0:T(1024)S(1)}, f32[2048]{0:T(1024)}, u32[]{:S(2)}) copy-start(f32[2048]{0:T(1024)} %param.33) | copy-start | bytes 24580
  316.1 223.2 %reduce-scatter.6.cloned.1.call-start = ((), (), s32[]{:S(2)}) async-start(), calls=%async_computation.9 | async-start | bytes 9437184 | tf_op jit(solution)/shard_map/reduce_scatter | solution.py:1170
  408.2 4.1 copy-start.3
  408.2 4.1 copy-start.7
  462.6 60.0 %all-to-all-start.1 = ((bf16[4,8,32,2048]{3,2,1,0:T(8,128)(2,1)}), bf16[4,8,32,2048]{3,2,1,0:T(8,128)(2,1)}, u32[]{:S(2)}, u32[]{:S(2)}) async-start(bf16[4,8,32,2048]{3,2,1,0:T(8,128)(2,1)} %broadcast_in_dim.24), calls=%async_computation.1 | async-start | bytes 8388608 | tf_op jit(solution)/shard_map/all_to_all | solution.py:481
  467.4 190.6 %reduce-scatter.8.cloned.1.call-start = ((), (), s32[]{:S(2)}) async-start(), calls=%async_computation.10 | async-start | bytes 9437184 | tf_op jit(solution)/shard_map/reduce_scatter | solution.py:1170
  476.2 4.5 copy-start.13
  476.2 4.5 copy-start.29
  542.3 11.6 %copy-start.8 = (f32[256,2048]{1,0:T(8,128)S(1)}, f32[256,2048]{1,0:T(8,128)}, u32[]{:S(2)}) copy-start(f32[256,2048]{1,0:T(8,128)} %get-tuple-element.121) | copy-start | bytes 6291460
  542.3 11.6 %copy-start.9 = (f32[8,32,2048]{2,1,0:T(8,128)S(1)}, f32[8,32,2048]{2,1,0:T(8,128)}, u32[]{:S(2)}) copy-start(f32[8,32,2048]{2,1,0:T(8,128)} %fusion.22.unit) | copy-start | bytes 6291460
  542.3 11.6 %copy-start.11 = (f32[2048]{0:T(1024)S(1)}, f32[2048]{0:T(1024)}, u32[]{:S(2)}) copy-start(f32[2048]{0:T(1024)} %param.35) | copy-start | bytes 24580
  553.9 92.5 %copy-start.14 = (bf16[256,2048]{1,0:T(8,128)(2,1)S(1)}, bf16[256,2048]{1,0:T(8,128)(2,1)}, u32[]{:S(2)}) copy-start(bf16[256,2048]{1,0:T(8,128)(2,1)} %reduce-scatter.4.cloned.1.call-done.down_ref) | copy-start | bytes 3145732
  553.9 92.5 %copy-start.15 = (bf16[256,2048]{1,0:T(8,128)(2,1)S(1)}, bf16[256,2048]{1,0:T(8,128)(2,1)}, u32[]{:S(2)}) copy-start(bf16[256,2048]{1,0:T(8,128)(2,1)} %reduce-scatter.6.cloned.1.call-done.up_ref) | copy-start | bytes 3145732
  648.6 12.0 %copy-start.1 = (s32[4,4]{1,0:T(4,128)S(1)}, s32[4,4]{1,0:T(4,128)}, u32[]{:S(2)}) copy-start(s32[4,4]{1,0:T(4,128)} %param.22) | copy-start | bytes 196
  (37 other events, 83.1 us)
Sparse Core Ops, SparseCore 0:
  12.4 119.3 all-gather.3
  133.4 83.1 all-gather.5
  218.2 80.5 all-gather.7
  316.3 87.7 reduce-scatter.3
  406.2 110.5 reduce-scatter.5
  539.5 116.6 reduce-scatter.7

commit v6 on v5

--- a/solution.py
+++ b/solution.py
@@ -1257,7 +1257,7 @@
     attn_grad_own = (live_own * grad_own + resid_grad).astype(bf16)
     attn_grad, output = transfer([Gather(attn_grad_own), Swap(output)], 10, name="gather_back")
     attn_grad = attn_grad.reshape(rows, width)
-    attn_grad, output = lax.optimization_barrier((attn_grad, output))
+    attn_grad, output, grad_w_up = lax.optimization_barrier((attn_grad, output, grad_w_up))
     output = gather_later(output)
 
     mixed_grad = nn(attn_grad, w_out_t).astype(bf16)
@@ -1274,10 +1274,10 @@
     in_grad = swap_heads(in_grad, group, 14, "join")
     in_grad, output = lax.optimization_barrier((in_grad, output))
     grad_w_in_out = two_products(z1, in_grad, attn_grad, mixed)
-    grad_w_in_out, shared_up = lax.optimization_barrier((grad_w_in_out, shared_up))
-    shared_in_out = share(grad_w_in_out)
     in_grad, grad_w_in_out = lax.optimization_barrier((in_grad, grad_w_in_out))
     in_part = nt(in_grad, w_in).astype(bf16).reshape(tps, bands, piece, width)
+    grad_w_in_out, shared_up, in_part = lax.optimization_barrier((grad_w_in_out, shared_up, in_part))
+    shared_in_out = share(grad_w_in_out)
 
     def over_rows(array):
         return jnp.sum(array.astype(f32), axis=0)

time: 677 us -> 681 us (level)
    pallas_call x7, Pallas kernels: 295 us -> 288 us  [transfer(): pl.pallas_call(kernel, out_shape=tuple((shape for item in items for shape...]
    unnamed x129 -> x131, local copies, waits for them, and re-layouts: 27.4 us -> 30.7 us
  transfers between devices with their start and end apart: 8 -> 8, of which waited for: 1 -> 1; matrix products, arithmetic and copies ran while one was open for 16% -> 15% of each run, Pallas kernels for 75% -> 75%
where the time goes in v6:
time: 681 us; the launch traced here: 674 us
  Pallas kernels  505 us (74%)
  matrix products  78.9 us (12%)
  local copies, waits for them, and re-layouts  39.2 us (6%)
  other arithmetic  16.5 us (2%)
  between operations  15.5 us (2%)
  starting transfers between devices  10.5 us (2%)
  waiting for transfers between devices  8.97 us (1%)
    pallas_call x7, Pallas kernels, transfer(): pl.pallas_call(kernel, out_shape=tuple((shape for item in items for shape...  288 us
    pallas_call x1, Pallas kernels, finish(): pl.pallas_call(functools.partial(finish_kernel, count, size), out_shape=(...  92.6 us
    dot_general x6, matrix products, nn(): return jnp.dot(left, right, preferred_element_type=f32)  49.6 us
    pallas_call x1, Pallas kernels, attend_back(): pl.pallas_call(functools.partial(attend_back_kernel, qb, kb), out_shape=(...  35 us
    unnamed x131, local copies, waits for them, and re-layouts  30.7 us
    dot_general x3, matrix products, nt(): lax.dot_general(left, right, (((1,), (1,)), ((), ())), preferred_element_...  29.3 us
    pallas_call x1, Pallas kernels, attend(): pl.pallas_call(functools.partial(attend_kernel, qb, kb), out_shape=(jax.S...  24.5 us
    pallas_call x1, Pallas kernels, product(): pl.pallas_call(product_kernel, out_shape=jax.ShapeDtypeStruct((depth, wid...  14.8 us
  transfers between devices with their start and end apart: 8, of which 1 were waited for; matrix products, arithmetic and copies ran while one was open for 15% of the time, Pallas kernels for 75%

profile of v6, /device:TPU:9, one launch (start us, length us, event | category | flops | bytes accessed | tf_op | source)
XLA Modules:
  0.0 674.4 jit_solution(14227187667255185322)
XLA Ops:
  14.8 59.2 %swap_in.1 = (bf16[8,32,2048]{2,1,0:T(8,128)(2,1)S(1)}, s32[8,4,256]{2,1,0:T(4,128)S(1)}) custom-call(bf16[8,32,2048]{2,1,0:T(8,128)(2,1)S(1)} %bitcast.97, s32[4,256]{1,0:T(4,128)S(1)} %copy-done.17), custom_call_target="tpu_custom_call" | custom-call | flops 35999997952 | bytes 72000000 | tf_op jit(solution)/shard_map/swap_in/pallas_call | solution.py:459
  79.9 47.1 %gather_in.1 = (bf16[4,256,2048]{2,1,0:T(8,128)(2,1)S(1)}, bf16[8,32,2048]{2,1,0:T(8,128)(2,1)S(1)}) custom-call(bf16[256,2048]{1,0:T(8,128)(2,1)S(1)} %fusion.28.refs_0_, bf16[8,32,2048]{2,1,0:T(8,128)(2,1)S(1)} %bitcast.96), custom_call_target="tpu_custom_call" | custom-call | flops 35999997952 | bytes 72000000 | tf_op jit(solution)/shard_map/gather_in/pallas_call | solution.py:459
  130.2 2.5 broadcast_in_dim.23
  132.8 5.0 all-to-all-start
  142.9 11.2 %project.1.x_ref = bf16[2,1024,768]{2,1,0:T(8,128)(2,1)S(1)} custom-call(bf16[1024,2048]{1,0:T(8,128)(2,1)S(1)} %bitcast.103, bf16[2048,2048]{1,0:T(8,128)(2,1)} %all-gather.4.cloned.1.call-done.w_ref, f32[1,1536]{1,0:T(1,128)S(1)} %broadcast_in_dim_reshape.2.bias_ref, f32[1,1536]{1,0:T(1,128)S(1)} %copy-done.22), custom_call_target="tpu_custom_call" | custom-call | flops 6442450944 | bytes 12582912 | tf_op jit(solution)/shard_map/project/pallas_call | solution.py:841
  155.8 3.8 swap_heads.4
  159.6 9.4 %fusion.19.q_ref.k_ref.v_ref = bf16[2048,768]{1,0:T(8,128)(2,1)S(1)} fusion(bf16[2048,768]{1,0:T(8,128)(2,1)} %bitcast.132, s32[2048]{0:T(1024)S(1)} %eq.38), kind=kOutput, calls=%fused_computation.24 | convolution fusion | flops 6448218112 | bytes 6299648 | tf_op jit(solution)/shard_map/dot_general | solution.py:38
  169.0 24.5 %attend.1 = (bf16[2048,256]{1,0:T(8,128)(2,1)S(1)}, f32[1,8,2048]{2,1,0:T(8,128)S(1)}) custom-call(s32[5]{0:T(128)S(1)} %pad_add_fusion.info_ref, s32[1,2048]{1,0:T(1,128)S(1)} %bitcast.100, bf16[2048,768]{1,0:T(8,128)(2,1)S(1)} %fusion.19.q_ref.k_ref.v_ref, bf16[2048,768]{1,0:T(8,128)(2,1)S(1)} %fusion.19.q_ref.k_ref.v_ref, ...), custom_call_target="tpu_custom_call" | custom-call | flops 30000001024 | bytes 60000000 | tf_op jit(solution)/shard_map/attend/pallas_call | solution.py:1086
  195.3 3.8 fusion.20
  201.4 4.3 convolution_convert_fusion.1
  205.7 37.4 %scatter_attn.1 = f32[256,2048]{1,0:T(8,128)S(1)} custom-call(bf16[4,256,2048]{2,1,0:T(8,128)(2,1)S(1)} %bitcast.108), custom_call_target="tpu_custom_call" | custom-call | flops 35999997952 | bytes 72000000 | tf_op jit(solution)/shard_map/scatter_attn/pallas_call | solution.py:459
  245.6 35.1 %gather_mid.1 = bf16[4,256,2048]{2,1,0:T(8,128)(2,1)S(1)} custom-call(bf16[256,2048]{1,0:T(8,128)(2,1)S(1)} %add_convert_fusion.1.refs_0_), custom_call_target="tpu_custom_call" | custom-call | flops 35999997952 | bytes 72000000 | tf_op jit(solution)/shard_map/gather_mid/pallas_call | solution.py:459
  282.7 16.4 %fusion.8 = (bf16[1024,2048]{1,0:T(8,128)(2,1)}, bf16[1024,2048]{1,0:T(8,128)(2,1)S(1)}) fusion(f32[2048]{0:T(1024)S(1)} %copy-done.61, bf16[1024,2048]{1,0:T(8,128)(2,1)} %bitcast.106, bf16[2048,2048]{1,0:T(8,128)(2,1)} %all-gather.6.cloned.1.call-done.refs_4_), kind=kOutput, calls=%fused_computation.11 | convolution fusion | flops 8615100416 | bytes 20979712 | tf_op jit(solution)/shard_map/dot_general | solution.py:38
  299.1 14.8 %product.1 = bf16[2048,2048]{1,0:T(8,128)(2,1)} custom-call(bf16[1024,2048]{1,0:T(8,128)(2,1)} %bitcast.22.left_ref.refs_1_, bf16[1024,2048]{1,0:T(8,128)(2,1)S(1)} %get-tuple-element.76.right_ref), custom_call_target="tpu_custom_call" | custom-call | flops 12000000000 | bytes 24000000 | tf_op jit(solution)/shard_map/product/pallas_call | solution.py:887
  316.2 13.9 %convolution_convert_fusion = bf16[1024,2048]{1,0:T(8,128)(2,1)} fusion(bf16[1024,2048]{1,0:T(8,128)(2,1)} %copy-done.27, bf16[2048,2048]{1,0:T(8,128)(2,1)} %all-gather.8.cloned.1.call-done.refs_2_), kind=kOutput, calls=%fused_computation.21 | convolution fusion | flops 8592031744 | bytes 16777216 | tf_op jit(solution)/shard_map/dot_general | solution.py:42
  330.1 36.2 %scatter_ffn.1 = (f32[256,2048]{1,0:T(8,128)}, bf16[1024,2048]{1,0:T(8,128)(2,1)}, bf16[1024,2048]{1,0:T(8,128)(2,1)}) custom-call(bf16[4,256,2048]{2,1,0:T(8,128)(2,1)} %bitcast.130, bf16[1024,2048]{1,0:T(8,128)(2,1)} %bitcast.22.left_ref.refs_1_, bf16[2048,2048]{1,0:T(8,128)(2,1)} %all-gather.8.cloned.1.call-done.refs_2_, ...), custom_call_target="tpu_custom_call" | custom-call | flops 35999997952 | bytes 72000000 | tf_op jit(solution)/shard_map/scatter_ffn/pallas_call | solution.py:459
  366.4 35.4 %scatter_mid.1 = (f32[256,2048]{1,0:T(8,128)}, bf16[2048,2048]{1,0:T(8,128)(2,1)}, f32[1,2048]{1,0:T(1,128)}) custom-call(bf16[4,256,2048]{2,1,0:T(8,128)(2,1)} %bitcast.129, bf16[1024,2048]{1,0:T(8,128)(2,1)} %bitcast.107, bf16[1024,2048]{1,0:T(8,128)(2,1)} %get-tuple-element.78.refs_2_), custom_call_target="tpu_custom_call" | custom-call | flops 35999997952 | bytes 72000000 | tf_op jit(solution)/shard_map/scatter_mid/pallas_call | solution.py:459
  401.8 2.7 multiply_reduce_fusion
  408.6 37.7 %gather_back.1 = (bf16[4,256,2048]{2,1,0:T(8,128)(2,1)S(1)}, bf16[8,32,2048]{2,1,0:T(8,128)(2,1)S(1)}) custom-call(bf16[256,2048]{1,0:T(8,128)(2,1)S(1)} %get-tuple-element.126.refs_0_, bf16[8,32,2048]{2,1,0:T(8,128)(2,1)S(1)} %bitcast.98), custom_call_target="tpu_custom_call" | custom-call | flops 35999997952 | bytes 72000000 | tf_op jit(solution)/shard_map/gather_back/pallas_call | solution.py:459
  448.3 2.5 broadcast_in_dim.24
  450.8 4.8 all-to-all-start.1
  456.0 6.7 fusion.34.x_ref
  462.7 3.4 swap_heads.6
  466.1 4.5 fusion.21.do_ref
  470.6 35.0 %attend_back.1 = (bf16[2048,768]{1,0:T(8,128)(2,1)S(1)}, f32[1,8,256]{2,1,0:T(8,128)S(1)}) custom-call(s32[5]{0:T(128)S(1)} %pad_add_fusion.info_ref, s32[1,2048]{1,0:T(1,128)S(1)} %bitcast.101, bf16[2048,768]{1,0:T(8,128)(2,1)} %copy-done.30, bf16[2048,768]{1,0:T(8,128)(2,1)} %copy-done.30, bf16[2048,768]{1,0:T(8,128)(2,1)} %copy-done.30, ...), custom_call_target="tpu_custom_call" | custom-call | flops 33999998976 | bytes 68000000 | tf_op jit(solution)/shard_map/attend_back/pallas_call | solution.py:1108
  505.6 8.7 %fusion.18 = bf16[2048,768]{1,0:T(8,128)(2,1)} fusion(bf16[2048,768]{1,0:T(8,128)(2,1)S(1)} %get-tuple-element.86, s32[2048]{0:T(1024)S(1)} %copy-done.57), kind=kOutput, calls=%fused_computation.23 | convolution fusion | flops 6448218112 | bytes 6299648 | tf_op jit(solution)/shard_map/dot_general | solution.py:38
  514.3 3.8 swap_heads.7.right_ref
  520.1 14.8 %two_products.1 = bf16[2048,2048]{1,0:T(8,128)(2,1)} custom-call(bf16[1024,2048]{1,0:T(8,128)(2,1)} %bitcast.102, bf16[1024,1536]{1,0:T(8,128)(2,1)S(1)} %copy-done.24, bf16[1024,2048]{1,0:T(8,128)(2,1)} %bitcast.105, bf16[1024,512]{1,0:T(8,128)(2,1)S(1)} %copy-done.25), custom_call_target="tpu_custom_call" | custom-call | flops 12000000000 | bytes 24000000 | tf_op jit(solution)/shard_map/two_products/pallas_call | solution.py:907
  534.9 11.1 %fusion.15 = bf16[1024,2048]{1,0:T(8,128)(2,1)} fusion(bf16[1024,1536]{1,0:T(8,128)(2,1)} %swap_heads.7.right_ref, bf16[2048,2048]{1,0:T(8,128)(2,1)} %all-gather.4.cloned.1.call-done.w_ref), kind=kOutput, calls=%fused_computation.20 | convolution fusion | flops 6444548096 | bytes 13631488 | tf_op jit(solution)/shard_map/dot_general | solution.py:42
  552.2 92.6 %finish.1 = (bf16[8,4,32,2048]{3,2,1,0:T(8,128)(2,1)}, f32[24,512]{1,0:T(8,128)S(1)}, f32[16,256]{1,0:T(8,128)S(1)}) custom-call(bf16[4,8,32,2048]{3,2,1,0:T(8,128)(2,1)} %bitcast.127, f32[8,32,2048]{2,1,0:T(8,128)S(1)} %copy-done.9, bf16[8,32,2048]{2,1,0:T(8,128)(2,1)S(1)} %copy-done.5, f32[8,32,2048]{2,1,0:T(8,128)S(1)} %bitcast.95, ...), custom_call_target="tpu_custom_call" | custom-call | flops 89999998976 | bytes 180000000 | tf_op jit(solution)/shard_map/finish/pallas_call | solution.py:658
  647.0 9.3 %settle.1 = (f32[8,4,32,2048]{3,2,1,0:T(8,128)}, bf16[8,4,32,2048]{3,2,1,0:T(8,128)(2,1)}, f32[256,2048]{1,0:T(8,128)}, f32[2048,256]{1,0:T(8,128)}, f32[1,2048]...) custom-call(bf16[8,4,32,2048]{3,2,1,0:T(8,128)(2,1)S(1)} %copy-done., ...), custom_call_target="tpu_custom_call" | custom-call | flops 10000000000 | bytes 20000000 | tf_op jit(solution)/shard_map/settle/pallas_call | solution.py:773
  656.3 8.2 %reduce-scatter.8.cloned.1.call-done.x_ref = bf16[256,2048]{1,0:T(8,128)(2,1)} async-done(((bf16[2048,2048]{1,0:T(8,128)(2,1)}), bf16[256,2048]{1,0:T(8,128)(2,1)}) %reduce-scatter.8.cloned.1.call-update) | async-done | bytes 1048592 | tf_op jit(solution)/shard_map/reduce_scatter | solution.py:1170
  (203 shorter events, 53.0 us)
Async XLA Ops:
  7.2 132.4 %copy-start = (s32[4,4]{1,0:T(4,128)S(1)}, s32[4,4]{1,0:T(4,128)}, u32[]{:S(2)}) copy-start(s32[4,4]{1,0:T(4,128)} %param.22) | copy-start | bytes 196
  7.2 133.5 %all-gather.4.cloned.1.call-start = ((), (), s32[]{:S(2)}) async-start(), calls=%async_computation.5 | async-start | bytes 9437184 | tf_op jit(solution)/shard_map/all_gather | solution.py:1173
  12.2 270.4 %all-gather.6.cloned.1.call-start = ((), (), s32[]{:S(2)}) async-start(), calls=%async_computation.6 | async-start | bytes 9437184 | tf_op jit(solution)/shard_map/all_gather | solution.py:1175
  14.8 64.6 %copy-start.10 = (f32[2048]{0:T(1024)S(1)}, f32[2048]{0:T(1024)}, u32[]{:S(2)}) copy-start(f32[2048]{0:T(1024)} %param.35) | copy-start | bytes 24580
  14.8 64.6 %copy-start.53 = (f32[2048]{0:T(1024)S(1)}, f32[2048]{0:T(1024)}, u32[]{:S(2)}) copy-start(f32[2048]{0:T(1024)} %param.36) | copy-start | bytes 24580
  74.0 169.2 %copy-start.2 = (bf16[8,32,2048]{2,1,0:T(8,128)(2,1)}, bf16[8,32,2048]{2,1,0:T(8,128)(2,1)S(1)}, u32[]{:S(2)}) copy-start(bf16[8,32,2048]{2,1,0:T(8,128)(2,1)S(1)} %get-tuple-element.70) | copy-start | bytes 3145732
  74.3 52.7 %copy-start.39 = (f32[8,32]{1,0:T(8,128)}, f32[8,32]{1,0:T(8,128)S(1)}, u32[]{:S(2)}) copy-start(f32[8,32]{1,0:T(8,128)S(1)} %broadcast_multiply_fusion) | copy-start | bytes 3076
  75.4 51.6 %copy-start.41 = (f32[8,32]{1,0:T(8,128)}, f32[8,32]{1,0:T(8,128)S(1)}, u32[]{:S(2)}) copy-start(f32[8,32]{1,0:T(8,128)S(1)} %get-tuple-element.137) | copy-start | bytes 3076
  79.4 49.6 %copy-start.51 = (f32[256]{0:T(256)}, f32[256]{0:T(256)S(1)}, u32[]{:S(2)}) copy-start(f32[256]{0:T(256)S(1)} %reshape.367) | copy-start | bytes 3076
  132.8 5.1 copy-start.35
  132.8 62.5 %all-to-all-start = ((bf16[4,256,2048]{2,1,0:T(8,128)(2,1)}), bf16[4,256,2048]{2,1,0:T(8,128)(2,1)}, u32[]{:S(2)}, u32[]{:S(2)}) async-start(bf16[4,256,2048]{2,1,0:T(8,128)(2,1)} %broadcast_in_dim.23), calls=%async_computation | async-start | bytes 8388608 | tf_op jit(solution)/shard_map/all_to_all | solution.py:481
  137.8 178.4 %all-gather.8.cloned.1.call-start = ((), (), s32[]{:S(2)}) async-start(), calls=%async_computation.7 | async-start | bytes 9437184 | tf_op jit(solution)/shard_map/all_gather | solution.py:1176
  139.3 309.0 %reduce-scatter.4.cloned.1.call-start = ((), (), s32[]{:S(2)}) async-start(), calls=%async_computation.8 | async-start | bytes 9437184 | tf_op jit(solution)/shard_map/reduce_scatter | solution.py:1170
  139.4 55.8 %copy-start.56 = (s32[2048]{0:T(1024)}, s32[2048]{0:T(1024)S(1)}, u32[]{:S(2)}) copy-start(s32[2048]{0:T(1024)S(1)} %eq.38) | copy-start | bytes 24580
  139.9 29.1 %copy-start.12 = (s32[2048]{0:T(1024)}, s32[2048]{0:T(1024)S(1)}, u32[]{:S(2)}) copy-start(s32[2048]{0:T(1024)S(1)} %select_reduce_fusion) | copy-start | bytes 24580
  195.3 3.8 copy-start.28
  205.7 37.5 %copy-start.43 = (f32[2048]{0:T(1024)S(1)}, f32[2048]{0:T(1024)}, u32[]{:S(2)}) copy-start(f32[2048]{0:T(1024)} %param.32) | copy-start | bytes 24580
  243.6 37.1 %copy-start.31 = (f32[256,2048]{1,0:T(8,128)}, f32[256,2048]{1,0:T(8,128)S(1)}, u32[]{:S(2)}) copy-start(f32[256,2048]{1,0:T(8,128)S(1)} %get-tuple-element.129) | copy-start | bytes 6291460
  245.6 37.1 %copy-start.61 = (f32[2048]{0:T(1024)S(1)}, f32[2048]{0:T(1024)}, u32[]{:S(2)}) copy-start(f32[2048]{0:T(1024)} %param.33) | copy-start | bytes 24580
  315.9 230.1 %reduce-scatter.6.cloned.1.call-start = ((), (), s32[]{:S(2)}) async-start(), calls=%async_computation.9 | async-start | bytes 9437184 | tf_op jit(solution)/shard_map/reduce_scatter | solution.py:1170
  366.3 35.5 %copy-start.32 = (f32[256,2048]{1,0:T(8,128)S(1)}, f32[256,2048]{1,0:T(8,128)}, u32[]{:S(2)}) copy-start(f32[256,2048]{1,0:T(8,128)} %copy-done.31) | copy-start | bytes 6291460
  366.3 35.5 %copy-start.38 = (f32[2048]{0:T(1024)S(1)}, f32[2048]{0:T(1024)}, u32[]{:S(2)}) copy-start(f32[2048]{0:T(1024)} %param.37) | copy-start | bytes 24580
  366.3 35.5 %copy-start.46 = (f32[256]{0:T(256)S(1)}, f32[256]{0:T(256)}, u32[]{:S(2)}) copy-start(f32[256]{0:T(256)} %copy-done.45) | copy-start | bytes 3076
  366.3 35.5 %copy-start.48 = (f32[256]{0:T(256)S(1)}, f32[256]{0:T(256)}, u32[]{:S(2)}) copy-start(f32[256]{0:T(256)} %copy-done.47) | copy-start | bytes 3076
  450.8 67.2 %all-to-all-start.1 = ((bf16[4,8,32,2048]{3,2,1,0:T(8,128)(2,1)}), bf16[4,8,32,2048]{3,2,1,0:T(8,128)(2,1)}, u32[]{:S(2)}, u32[]{:S(2)}) async-start(bf16[4,8,32,2048]{3,2,1,0:T(8,128)(2,1)} %broadcast_in_dim.24), calls=%async_computation.1 | async-start | bytes 8388608 | tf_op jit(solution)/shard_map/all_to_all | solution.py:481
  455.7 208.7 %reduce-scatter.8.cloned.1.call-start = ((), (), s32[]{:S(2)}) async-start(), calls=%async_computation.10 | async-start | bytes 9437184 | tf_op jit(solution)/shard_map/reduce_scatter | solution.py:1170
  466.1 4.5 copy-start.13
  466.1 4.5 copy-start.29
  514.3 3.8 copy-start.25
  552.2 92.6 %copy-start.14 = (bf16[256,2048]{1,0:T(8,128)(2,1)S(1)}, bf16[256,2048]{1,0:T(8,128)(2,1)}, u32[]{:S(2)}) copy-start(bf16[256,2048]{1,0:T(8,128)(2,1)} %reduce-scatter.4.cloned.1.call-done.down_ref) | copy-start | bytes 3145732
  552.2 92.6 %copy-start.15 = (bf16[256,2048]{1,0:T(8,128)(2,1)S(1)}, bf16[256,2048]{1,0:T(8,128)(2,1)}, u32[]{:S(2)}) copy-start(bf16[256,2048]{1,0:T(8,128)(2,1)} %reduce-scatter.6.cloned.1.call-done.up_ref) | copy-start | bytes 3145732
  647.0 20.1 %copy-start.1 = (s32[4,4]{1,0:T(4,128)S(1)}, s32[4,4]{1,0:T(4,128)}, u32[]{:S(2)}) copy-start(s32[4,4]{1,0:T(4,128)} %param.22) | copy-start | bytes 196
  (38 other events, 78.6 us)
Sparse Core Ops, SparseCore 0:
  12.4 119.3 all-gather.3
  133.4 83.1 all-gather.5
  218.2 80.5 all-gather.7
  316.0 87.7 reduce-scatter.3
  448.4 89.5 reduce-scatter.5
  546.2 118.2 reduce-scatter.7

commit v7 on v6

--- a/solution.py
+++ b/solution.py
@@ -514,7 +514,7 @@
     barrier = pltpu.get_barrier_semaphore()
     for device in devices:
         pl.semaphore_signal(barrier, inc=1, device_id=device, device_id_type=MESH)
-    shifts = list(range(1, size)) + [0]
+    shifts = sorted(range(1, size), key=lambda shift: abs(2 * shift - size)) + [0]
     blocks = [Block(k, shift, grid, size) for k, shift in enumerate(shifts)]
     late[...] = jnp.zeros_like(late)
     pl.semaphore_wait(barrier, len(devices))

time: 681 us -> 676 us (level)
  Pallas kernels: 505 us -> 496 us
    pallas_call x1, Pallas kernels: 35 us -> 17.9 us  [attend_back(): pl.pallas_call(functools.partial(attend_back_kernel, qb, kb), out_shape=(...]
    pallas_call x1, Pallas kernels: 24.5 us -> 13.4 us  [attend(): pl.pallas_call(functools.partial(attend_kernel, qb, kb), out_shape=(jax.S...]
    pallas_call x1, Pallas kernels: 92.6 us -> 102 us  [finish(): pl.pallas_call(functools.partial(finish_kernel, count, size), out_shape=(...]
    pallas_call x7, Pallas kernels: 288 us -> 297 us  [transfer(): pl.pallas_call(kernel, out_shape=tuple((shape for item in items for shape...]
  transfers between devices with their start and end apart: 8 -> 8, of which waited for: 1 -> 4; matrix products, arithmetic and copies ran while one was open for 15% -> 15% of each run, Pallas kernels for 75% -> 74%
where the time goes in v7:
time: 676 us; the launch traced here: 668 us
  Pallas kernels  496 us (73%)
  matrix products  78.5 us (12%)
  local copies, waits for them, and re-layouts  39.1 us (6%)
  other arithmetic  16.5 us (2%)
  between operations  15.5 us (2%)
  waiting for transfers between devices  12.3 us (2%)
  starting transfers between devices  10.8 us (2%)
    pallas_call x7, Pallas kernels, transfer(): pl.pallas_call(kernel, out_shape=tuple((shape for item in items for shape...  297 us
    pallas_call x1, Pallas kernels, finish(): pl.pallas_call(functools.partial(finish_kernel, count, size), out_shape=(...  102 us
    dot_general x6, matrix products, nn(): return jnp.dot(left, right, preferred_element_type=f32)  49 us
    unnamed x131, local copies, waits for them, and re-layouts  30.7 us
    dot_general x3, matrix products, nt(): lax.dot_general(left, right, (((1,), (1,)), ((), ())), preferred_element_...  29.5 us
    pallas_call x1, Pallas kernels, attend_back(): pl.pallas_call(functools.partial(attend_back_kernel, qb, kb), out_shape=(...  17.9 us
    pallas_call x1, Pallas kernels, product(): pl.pallas_call(product_kernel, out_shape=jax.ShapeDtypeStruct((depth, wid...  14.8 us
    pallas_call x1, Pallas kernels, two_products(): pl.pallas_call(products_kernel, out_shape=jax.ShapeDtypeStruct((depth, wi...  14.8 us
  transfers between devices with their start and end apart: 8, of which 4 were waited for; matrix products, arithmetic and copies ran while one was open for 15% of the time, Pallas kernels for 74%

profile of v7, /device:TPU:9, one launch (start us, length us, event | category | flops | bytes accessed | tf_op | source)
XLA Modules:
  0.0 668.2 jit_solution(11010097945483473542)
XLA Ops:
  14.8 59.2 %swap_in.1 = (bf16[8,32,2048]{2,1,0:T(8,128)(2,1)S(1)}, s32[8,4,256]{2,1,0:T(4,128)S(1)}) custom-call(bf16[8,32,2048]{2,1,0:T(8,128)(2,1)S(1)} %bitcast.97, s32[4,256]{1,0:T(4,128)S(1)} %copy-done.17), custom_call_target="tpu_custom_call" | custom-call | flops 35999997952 | bytes 72000000 | tf_op jit(solution)/shard_map/swap_in/pallas_call | solution.py:459
  79.9 47.1 %gather_in.1 = (bf16[4,256,2048]{2,1,0:T(8,128)(2,1)S(1)}, bf16[8,32,2048]{2,1,0:T(8,128)(2,1)S(1)}) custom-call(bf16[256,2048]{1,0:T(8,128)(2,1)S(1)} %fusion.28.refs_0_, bf16[8,32,2048]{2,1,0:T(8,128)(2,1)S(1)} %bitcast.96), custom_call_target="tpu_custom_call" | custom-call | flops 35999997952 | bytes 72000000 | tf_op jit(solution)/shard_map/gather_in/pallas_call | solution.py:459
  132.8 5.0 all-to-all-start
  142.9 11.2 %project.1.x_ref = bf16[2,1024,768]{2,1,0:T(8,128)(2,1)S(1)} custom-call(bf16[1024,2048]{1,0:T(8,128)(2,1)S(1)} %bitcast.103, bf16[2048,2048]{1,0:T(8,128)(2,1)} %all-gather.4.cloned.1.call-done.w_ref, f32[1,1536]{1,0:T(1,128)S(1)} %broadcast_in_dim_reshape.2.bias_ref, f32[1,1536]{1,0:T(1,128)S(1)} %copy-done.22), custom_call_target="tpu_custom_call" | custom-call | flops 6442450944 | bytes 12582912 | tf_op jit(solution)/shard_map/project/pallas_call | solution.py:841
  155.8 3.8 swap_heads.4
  159.6 9.4 %fusion.19.q_ref.k_ref.v_ref = bf16[2048,768]{1,0:T(8,128)(2,1)S(1)} fusion(bf16[2048,768]{1,0:T(8,128)(2,1)} %bitcast.132, s32[2048]{0:T(1024)S(1)} %eq.38), kind=kOutput, calls=%fused_computation.24 | convolution fusion | flops 6448218112 | bytes 6299648 | tf_op jit(solution)/shard_map/dot_general | solution.py:38
  169.0 13.4 %attend.1 = (bf16[2048,256]{1,0:T(8,128)(2,1)S(1)}, f32[1,8,2048]{2,1,0:T(8,128)S(1)}) custom-call(s32[5]{0:T(128)S(1)} %pad_add_fusion.info_ref, s32[1,2048]{1,0:T(1,128)S(1)} %bitcast.100, bf16[2048,768]{1,0:T(8,128)(2,1)S(1)} %fusion.19.q_ref.k_ref.v_ref, bf16[2048,768]{1,0:T(8,128)(2,1)S(1)} %fusion.19.q_ref.k_ref.v_ref, ...), custom_call_target="tpu_custom_call" | custom-call | flops 30000001024 | bytes 60000000 | tf_op jit(solution)/shard_map/attend/pallas_call | solution.py:1086
  185.4 3.8 fusion.20
  191.9 4.4 convolution_convert_fusion.1
  196.2 36.3 %scatter_attn.1 = f32[256,2048]{1,0:T(8,128)S(1)} custom-call(bf16[4,256,2048]{2,1,0:T(8,128)(2,1)S(1)} %bitcast.108), custom_call_target="tpu_custom_call" | custom-call | flops 35999997952 | bytes 72000000 | tf_op jit(solution)/shard_map/scatter_attn/pallas_call | solution.py:459
  235.0 35.0 %gather_mid.1 = bf16[4,256,2048]{2,1,0:T(8,128)(2,1)S(1)} custom-call(bf16[256,2048]{1,0:T(8,128)(2,1)S(1)} %add_convert_fusion.1.refs_0_), custom_call_target="tpu_custom_call" | custom-call | flops 35999997952 | bytes 72000000 | tf_op jit(solution)/shard_map/gather_mid/pallas_call | solution.py:459
  272.0 16.5 %fusion.8 = (bf16[1024,2048]{1,0:T(8,128)(2,1)}, bf16[1024,2048]{1,0:T(8,128)(2,1)S(1)}) fusion(f32[2048]{0:T(1024)S(1)} %copy-done.61, bf16[1024,2048]{1,0:T(8,128)(2,1)} %bitcast.106, bf16[2048,2048]{1,0:T(8,128)(2,1)} %all-gather.6.cloned.1.call-done.refs_4_), kind=kOutput, calls=%fused_computation.11 | convolution fusion | flops 8615100416 | bytes 20979712 | tf_op jit(solution)/shard_map/dot_general | solution.py:38
  288.4 14.8 %product.1 = bf16[2048,2048]{1,0:T(8,128)(2,1)} custom-call(bf16[1024,2048]{1,0:T(8,128)(2,1)} %bitcast.22.left_ref.refs_1_, bf16[1024,2048]{1,0:T(8,128)(2,1)S(1)} %get-tuple-element.76.right_ref), custom_call_target="tpu_custom_call" | custom-call | flops 12000000000 | bytes 24000000 | tf_op jit(solution)/shard_map/product/pallas_call | solution.py:887
  305.5 13.9 %convolution_convert_fusion = bf16[1024,2048]{1,0:T(8,128)(2,1)} fusion(bf16[1024,2048]{1,0:T(8,128)(2,1)} %copy-done.27, bf16[2048,2048]{1,0:T(8,128)(2,1)} %all-gather.8.cloned.1.call-done.refs_2_), kind=kOutput, calls=%fused_computation.21 | convolution fusion | flops 8592031744 | bytes 16777216 | tf_op jit(solution)/shard_map/dot_general | solution.py:42
  319.4 36.0 %scatter_ffn.1 = (f32[256,2048]{1,0:T(8,128)}, bf16[1024,2048]{1,0:T(8,128)(2,1)}, bf16[1024,2048]{1,0:T(8,128)(2,1)}) custom-call(bf16[4,256,2048]{2,1,0:T(8,128)(2,1)} %bitcast.130, bf16[1024,2048]{1,0:T(8,128)(2,1)} %bitcast.22.left_ref.refs_1_, bf16[2048,2048]{1,0:T(8,128)(2,1)} %all-gather.8.cloned.1.call-done.refs_2_, ...), custom_call_target="tpu_custom_call" | custom-call | flops 35999997952 | bytes 72000000 | tf_op jit(solution)/shard_map/scatter_ffn/pallas_call | solution.py:459
  355.5 35.2 %scatter_mid.1 = (f32[256,2048]{1,0:T(8,128)}, bf16[2048,2048]{1,0:T(8,128)(2,1)}, f32[1,2048]{1,0:T(1,128)}) custom-call(bf16[4,256,2048]{2,1,0:T(8,128)(2,1)} %bitcast.129, bf16[1024,2048]{1,0:T(8,128)(2,1)} %bitcast.107, bf16[1024,2048]{1,0:T(8,128)(2,1)} %get-tuple-element.78.refs_2_), custom_call_target="tpu_custom_call" | custom-call | flops 35999997952 | bytes 72000000 | tf_op jit(solution)/shard_map/scatter_mid/pallas_call | solution.py:459
  390.8 2.7 multiply_reduce_fusion
  397.6 48.6 %gather_back.1 = (bf16[4,256,2048]{2,1,0:T(8,128)(2,1)S(1)}, bf16[8,32,2048]{2,1,0:T(8,128)(2,1)S(1)}) custom-call(bf16[256,2048]{1,0:T(8,128)(2,1)S(1)} %get-tuple-element.126.refs_0_, bf16[8,32,2048]{2,1,0:T(8,128)(2,1)S(1)} %bitcast.98), custom_call_target="tpu_custom_call" | custom-call | flops 35999997952 | bytes 72000000 | tf_op jit(solution)/shard_map/gather_back/pallas_call | solution.py:459
  450.7 5.2 all-to-all-start.1
  456.1 6.2 fusion.34.x_ref
  462.3 2.7 swap_heads.6
  465.1 4.5 fusion.21.do_ref
  469.6 17.9 %attend_back.1 = (bf16[2048,768]{1,0:T(8,128)(2,1)S(1)}, f32[1,8,256]{2,1,0:T(8,128)S(1)}) custom-call(s32[5]{0:T(128)S(1)} %pad_add_fusion.info_ref, s32[1,2048]{1,0:T(1,128)S(1)} %bitcast.101, bf16[2048,768]{1,0:T(8,128)(2,1)} %copy-done.30, bf16[2048,768]{1,0:T(8,128)(2,1)} %copy-done.30, bf16[2048,768]{1,0:T(8,128)(2,1)} %copy-done.30, ...), custom_call_target="tpu_custom_call" | custom-call | flops 33999998976 | bytes 68000000 | tf_op jit(solution)/shard_map/attend_back/pallas_call | solution.py:1108
  487.5 8.7 %fusion.18 = bf16[2048,768]{1,0:T(8,128)(2,1)} fusion(bf16[2048,768]{1,0:T(8,128)(2,1)S(1)} %get-tuple-element.86, s32[2048]{0:T(1024)S(1)} %copy-done.57), kind=kOutput, calls=%fused_computation.23 | convolution fusion | flops 6448218112 | bytes 6299648 | tf_op jit(solution)/shard_map/dot_general | solution.py:38
  496.2 3.9 swap_heads.7.right_ref
  500.1 2.6 all-to-all-done.1.out_ref
  504.7 14.8 %two_products.1 = bf16[2048,2048]{1,0:T(8,128)(2,1)} custom-call(bf16[1024,2048]{1,0:T(8,128)(2,1)} %bitcast.102, bf16[1024,1536]{1,0:T(8,128)(2,1)S(1)} %copy-done.24, bf16[1024,2048]{1,0:T(8,128)(2,1)} %bitcast.105, bf16[1024,512]{1,0:T(8,128)(2,1)S(1)} %copy-done.25), custom_call_target="tpu_custom_call" | custom-call | flops 12000000000 | bytes 24000000 | tf_op jit(solution)/shard_map/two_products/pallas_call | solution.py:907
  519.5 11.2 %fusion.15 = bf16[1024,2048]{1,0:T(8,128)(2,1)} fusion(bf16[1024,1536]{1,0:T(8,128)(2,1)} %swap_heads.7.right_ref, bf16[2048,2048]{1,0:T(8,128)(2,1)} %all-gather.4.cloned.1.call-done.w_ref), kind=kOutput, calls=%fused_computation.20 | convolution fusion | flops 6444548096 | bytes 13631488 | tf_op jit(solution)/shard_map/dot_general | solution.py:42
  530.6 4.2 reduce-scatter.6.cloned.1.call-done.up_ref
  541.0 102.3 %finish.1 = (bf16[8,4,32,2048]{3,2,1,0:T(8,128)(2,1)}, f32[24,512]{1,0:T(8,128)S(1)}, f32[16,256]{1,0:T(8,128)S(1)}) custom-call(bf16[4,8,32,2048]{3,2,1,0:T(8,128)(2,1)} %bitcast.127, f32[8,32,2048]{2,1,0:T(8,128)S(1)} %copy-done.9, bf16[8,32,2048]{2,1,0:T(8,128)(2,1)S(1)} %copy-done.5, f32[8,32,2048]{2,1,0:T(8,128)S(1)} %bitcast.95, ...), custom_call_target="tpu_custom_call" | custom-call | flops 89999998976 | bytes 180000000 | tf_op jit(solution)/shard_map/finish/pallas_call | solution.py:658
  645.6 9.3 %settle.1 = (f32[8,4,32,2048]{3,2,1,0:T(8,128)}, bf16[8,4,32,2048]{3,2,1,0:T(8,128)(2,1)}, f32[256,2048]{1,0:T(8,128)}, f32[2048,256]{1,0:T(8,128)}, f32[1,2048]...) custom-call(bf16[8,4,32,2048]{3,2,1,0:T(8,128)(2,1)S(1)} %copy-done., ...), custom_call_target="tpu_custom_call" | custom-call | flops 10000000000 | bytes 20000000 | tf_op jit(solution)/shard_map/settle/pallas_call | solution.py:773
  654.8 3.4 reduce-scatter.8.cloned.1.call-done.x_ref
  (203 shorter events, 59.7 us)
Async XLA Ops:
  7.2 132.4 %copy-start = (s32[4,4]{1,0:T(4,128)S(1)}, s32[4,4]{1,0:T(4,128)}, u32[]{:S(2)}) copy-start(s32[4,4]{1,0:T(4,128)} %param.22) | copy-start | bytes 196
  7.2 133.5 %all-gather.4.cloned.1.call-start = ((), (), s32[]{:S(2)}) async-start(), calls=%async_computation.5 | async-start | bytes 9437184 | tf_op jit(solution)/shard_map/all_gather | solution.py:1173
  12.2 259.7 %all-gather.6.cloned.1.call-start = ((), (), s32[]{:S(2)}) async-start(), calls=%async_computation.6 | async-start | bytes 9437184 | tf_op jit(solution)/shard_map/all_gather | solution.py:1175
  14.8 64.6 %copy-start.10 = (f32[2048]{0:T(1024)S(1)}, f32[2048]{0:T(1024)}, u32[]{:S(2)}) copy-start(f32[2048]{0:T(1024)} %param.35) | copy-start | bytes 24580
  14.8 64.6 %copy-start.53 = (f32[2048]{0:T(1024)S(1)}, f32[2048]{0:T(1024)}, u32[]{:S(2)}) copy-start(f32[2048]{0:T(1024)} %param.36) | copy-start | bytes 24580
  74.0 158.6 %copy-start.2 = (bf16[8,32,2048]{2,1,0:T(8,128)(2,1)}, bf16[8,32,2048]{2,1,0:T(8,128)(2,1)S(1)}, u32[]{:S(2)}) copy-start(bf16[8,32,2048]{2,1,0:T(8,128)(2,1)S(1)} %get-tuple-element.70) | copy-start | bytes 3145732
  74.3 52.7 %copy-start.39 = (f32[8,32]{1,0:T(8,128)}, f32[8,32]{1,0:T(8,128)S(1)}, u32[]{:S(2)}) copy-start(f32[8,32]{1,0:T(8,128)S(1)} %broadcast_multiply_fusion) | copy-start | bytes 3076
  75.4 51.6 %copy-start.41 = (f32[8,32]{1,0:T(8,128)}, f32[8,32]{1,0:T(8,128)S(1)}, u32[]{:S(2)}) copy-start(f32[8,32]{1,0:T(8,128)S(1)} %get-tuple-element.137) | copy-start | bytes 3076
  79.4 49.6 %copy-start.51 = (f32[256]{0:T(256)}, f32[256]{0:T(256)S(1)}, u32[]{:S(2)}) copy-start(f32[256]{0:T(256)S(1)} %reshape.367) | copy-start | bytes 3076
  132.8 5.1 copy-start.35
  132.8 52.6 %all-to-all-start = ((bf16[4,256,2048]{2,1,0:T(8,128)(2,1)}), bf16[4,256,2048]{2,1,0:T(8,128)(2,1)}, u32[]{:S(2)}, u32[]{:S(2)}) async-start(bf16[4,256,2048]{2,1,0:T(8,128)(2,1)} %broadcast_in_dim.23), calls=%async_computation | async-start | bytes 8388608 | tf_op jit(solution)/shard_map/all_to_all | solution.py:481
  137.8 167.7 %all-gather.8.cloned.1.call-start = ((), (), s32[]{:S(2)}) async-start(), calls=%async_computation.7 | async-start | bytes 9437184 | tf_op jit(solution)/shard_map/all_gather | solution.py:1176
  139.3 308.8 %reduce-scatter.4.cloned.1.call-start = ((), (), s32[]{:S(2)}) async-start(), calls=%async_computation.8 | async-start | bytes 9437184 | tf_op jit(solution)/shard_map/reduce_scatter | solution.py:1170
  139.4 46.0 %copy-start.56 = (s32[2048]{0:T(1024)}, s32[2048]{0:T(1024)S(1)}, u32[]{:S(2)}) copy-start(s32[2048]{0:T(1024)S(1)} %eq.38) | copy-start | bytes 24580
  139.9 29.1 %copy-start.12 = (s32[2048]{0:T(1024)}, s32[2048]{0:T(1024)S(1)}, u32[]{:S(2)}) copy-start(s32[2048]{0:T(1024)S(1)} %select_reduce_fusion) | copy-start | bytes 24580
  184.1 5.1 copy-start.28
  196.2 36.3 %copy-start.43 = (f32[2048]{0:T(1024)S(1)}, f32[2048]{0:T(1024)}, u32[]{:S(2)}) copy-start(f32[2048]{0:T(1024)} %param.32) | copy-start | bytes 24580
  232.9 37.0 %copy-start.31 = (f32[256,2048]{1,0:T(8,128)}, f32[256,2048]{1,0:T(8,128)S(1)}, u32[]{:S(2)}) copy-start(f32[256,2048]{1,0:T(8,128)S(1)} %get-tuple-element.129) | copy-start | bytes 6291460
  234.9 37.0 %copy-start.61 = (f32[2048]{0:T(1024)S(1)}, f32[2048]{0:T(1024)}, u32[]{:S(2)}) copy-start(f32[2048]{0:T(1024)} %param.33) | copy-start | bytes 24580
  305.2 229.5 %reduce-scatter.6.cloned.1.call-start = ((), (), s32[]{:S(2)}) async-start(), calls=%async_computation.9 | async-start | bytes 9437184 | tf_op jit(solution)/shard_map/reduce_scatter | solution.py:1170
  355.5 35.3 %copy-start.32 = (f32[256,2048]{1,0:T(8,128)S(1)}, f32[256,2048]{1,0:T(8,128)}, u32[]{:S(2)}) copy-start(f32[256,2048]{1,0:T(8,128)} %copy-done.31) | copy-start | bytes 6291460
  355.5 35.3 %copy-start.38 = (f32[2048]{0:T(1024)S(1)}, f32[2048]{0:T(1024)}, u32[]{:S(2)}) copy-start(f32[2048]{0:T(1024)} %param.37) | copy-start | bytes 24580
  355.5 35.3 %copy-start.46 = (f32[256]{0:T(256)S(1)}, f32[256]{0:T(256)}, u32[]{:S(2)}) copy-start(f32[256]{0:T(256)} %copy-done.45) | copy-start | bytes 3076
  355.5 35.3 %copy-start.48 = (f32[256]{0:T(256)S(1)}, f32[256]{0:T(256)}, u32[]{:S(2)}) copy-start(f32[256]{0:T(256)} %copy-done.47) | copy-start | bytes 3076
  450.7 52.1 %all-to-all-start.1 = ((bf16[4,8,32,2048]{3,2,1,0:T(8,128)(2,1)}), bf16[4,8,32,2048]{3,2,1,0:T(8,128)(2,1)}, u32[]{:S(2)}, u32[]{:S(2)}) async-start(bf16[4,8,32,2048]{3,2,1,0:T(8,128)(2,1)} %broadcast_in_dim.24), calls=%async_computation.1 | async-start | bytes 8388608 | tf_op jit(solution)/shard_map/all_to_all | solution.py:481
  455.9 202.4 %reduce-scatter.8.cloned.1.call-start = ((), (), s32[]{:S(2)}) async-start(), calls=%async_computation.10 | async-start | bytes 9437184 | tf_op jit(solution)/shard_map/reduce_scatter | solution.py:1170
  465.0 4.5 copy-start.13
  465.1 4.5 copy-start.29
  496.2 6.6 copy-start.25
  541.0 102.3 %copy-start.14 = (bf16[256,2048]{1,0:T(8,128)(2,1)S(1)}, bf16[256,2048]{1,0:T(8,128)(2,1)}, u32[]{:S(2)}) copy-start(bf16[256,2048]{1,0:T(8,128)(2,1)} %reduce-scatter.4.cloned.1.call-done.down_ref) | copy-start | bytes 3145732
  541.0 102.3 %copy-start.15 = (bf16[256,2048]{1,0:T(8,128)(2,1)S(1)}, bf16[256,2048]{1,0:T(8,128)(2,1)}, u32[]{:S(2)}) copy-start(bf16[256,2048]{1,0:T(8,128)(2,1)} %reduce-scatter.6.cloned.1.call-done.up_ref) | copy-start | bytes 3145732
  645.6 15.4 %copy-start.1 = (s32[4,4]{1,0:T(4,128)S(1)}, s32[4,4]{1,0:T(4,128)}, u32[]{:S(2)}) copy-start(s32[4,4]{1,0:T(4,128)} %param.22) | copy-start | bytes 196
  (38 other events, 78.0 us)
Sparse Core Ops, SparseCore 0:
  12.4 119.3 all-gather.3
  133.4 83.1 all-gather.5
  218.2 80.6 all-gather.7
  305.4 96.2 reduce-scatter.3
  448.3 86.4 reduce-scatter.5
  536.9 121.2 reduce-scatter.7
